TPU v7x, 32 devices: a whole 2x2x4 slice. The times are simulated.
32 devices in a mesh: seq: 8 (over z, x), mlp: 4 (over y, core).
Axes of the slice: x: 2, y: 2, z: 4, core: 2. Of those that a mesh axis runs over, the one named last changes fastest.
Arguments:
- tokens: bfloat16 [12, 2048, 1024], P(None, 'seq'), may hold values from -6 to 6
- lengths: int32 [12, 8], replicated, may hold values from 1 to 2048, as said below
- counts: int32 [12], replicated, may hold values from 1 to 8
- norm_gain: float32 [1024], replicated, may hold values from 0.5 to 1.5
- norm_bias: float32 [1024], replicated, may hold values from -4 to 4
- head_weight: bfloat16 [3, 1024, 1024], P(None, None, 'mlp'), may hold values from -0.1875 to 0.1875
- merge_weight: bfloat16 [1024, 1024], P('mlp'), may hold values from -1.5 to 1.5
- up_weight: bfloat16 [1024, 4096], P(None, 'mlp'), may hold values from -0.1875 to 0.1875
- up_bias: float32 [4096], P('mlp'), may hold values from -6 to 6
- down_weight: bfloat16 [4096, 1024], P('mlp'), may hold values from -0.09375 to 0.09375
- down_bias: float32 [1024], replicated, may hold values from -6 to 6
- cotangent: bfloat16 [12, 2048, 1024], P(None, 'seq', 'mlp'), may hold values from -6 to 6
Outputs:
- result: bfloat16 [12, 2048, 1024], P(None, 'seq', 'mlp')
- tokens_grad: bfloat16 [12, 2048, 1024], P(None, 'seq')
- gain_grad: float32 [1024], P('seq')
- shift_grad: float32 [1024], P('seq')
- head_grad: float32 [3, 1024, 1024], P(None, 'seq', 'mlp')
- merge_grad: float32 [1024, 1024], P('mlp', 'seq')
- up_grad: float32 [1024, 4096], P('seq', 'mlp')
- up_bias_grad: float32 [4096], P(('mlp', 'seq'))
- down_grad: float32 [4096, 1024], P('mlp', 'seq')
- down_bias_grad: float32 [1024], P('seq')
Inputs may be any that keep to these rules, and one draw needn't show every extreme that they name: In row p the first counts[p] entries are the lengths of the proteins packed from position 0; they sum to at most 2048, and positions after them are padding. Later entries are to be ignored. In every draw one pack holds a single protein of 2048 residues.
All inputs are finite; a program needn't handle non-finite values.
Results may differ from a plain program's by a relative error of at most 0.011.
Values may be sent and summed in bfloat16 or wider, within the bound.
A program may use at most 320 MiB of HBM per device.

v0:
```python
import functools
import math

import jax
import jax.numpy as jnp
from jax import lax
from jax.experimental import pallas as pl
from jax.experimental.pallas import tpu as pltpu
from jax.sharding import PartitionSpec as P

HD = 64
ROT = 32
EPS = 1e-05
NEG = -1e30
BF16 = jnp.bfloat16
F32 = jnp.float32
VMEM_LIMIT = 56 * 1024 * 1024
COST = pl.CostEstimate(flops=1 << 20, bytes_accessed=1 << 20, transcendentals=0)


def dot(a, b, dims=((1,), (0,))):
    return lax.dot_general(a, b, (dims, ((), ())), preferred_element_type=F32)


def layout(lengths, counts, pack_len):
    slots = lengths.shape[-1]
    slot_ids = jnp.arange(slots, dtype=jnp.int32)
    used = slot_ids[None, :] < counts[:, None]
    sizes = jnp.where(used, lengths, 0)
    ends = jnp.cumsum(sizes, axis=-1)
    starts = ends - sizes
    filled = ends[:, -1:]
    place = jnp.arange(pack_len, dtype=jnp.int32)[None, :]
    begin = jnp.max(
        jnp.where(used[:, None, :] & (place[:, :, None] >= starts[:, None, :]), starts[:, None, :], 0),
        axis=-1,
    )
    inside = place < filled
    first = jnp.where(inside, begin, place)
    position = jnp.where(inside, place - begin, place - filled)
    cost = jnp.sum(sizes * sizes, axis=-1)
    return first, position, cost


def turn(values, cosine, sine, heads):
    out = []
    parity = lax.broadcasted_iota(jnp.int32, cosine.shape, 0) % 2
    for h in range(heads):
        part = values[h * HD : h * HD + ROT]
        ahead = jnp.concatenate([part[1:], part[:1]], axis=0)
        behind = jnp.concatenate([part[-1:], part[:-1]], axis=0)
        swapped = jnp.where(parity == 0, -ahead, behind)
        out.append(part * cosine + swapped * sine)
        out.append(values[h * HD + ROT : (h + 1) * HD])
    return jnp.concatenate(out, axis=0)


def head_kernel(n, heads, per, me_ref, pack_ref, x_ref, gain_ref, bias_ref, w_ref, cos_ref, sin_ref, *refs):
    normed_ref, copy_ref, outs, scr = refs[0], refs[1], refs[2:-1], refs[-1]
    s_id, g = pl.program_id(0), pl.program_id(1)
    me = me_ref[0]
    width = heads * HD
    copy_ref[0] = x_ref[0]
    x = x_ref[0].astype(F32)
    cent = x - jnp.mean(x, axis=-1, keepdims=True)
    var = jnp.mean(cent * cent, axis=-1, keepdims=True)
    normed = (cent * lax.rsqrt(var + EPS) * gain_ref[...] + bias_ref[...]).astype(BF16)
    normed_ref[0] = normed
    for j in range(3):
        part = dot(w_ref[j * width : (j + 1) * width, :], normed, ((1,), (1,)))
        if j < 2:
            part = turn(part, cos_ref[0], sin_ref[0], heads)
        if j == 0:
            part = part * (1.0 / math.sqrt(HD))
        part = part.astype(BF16)
        for h in range(heads):
            scr[h, j] = part[h * HD : (h + 1) * HD]
    for at, out in enumerate(outs):
        d = lax.bitwise_xor(jnp.int32(at % n), me)

        @pl.when((d // heads == g) & (s_id // per == at // n))
        def _():
            out[0] = scr[d % heads]


def grad_kernel(n, heads, me_ref, c_ref, w_ref, *refs):
    outs, scr = refs[:n], refs[n]
    g = pl.program_id(1)
    me = me_ref[0]
    part = dot(w_ref[...], c_ref[0], ((1,), (1,))).astype(BF16)
    for h in range(heads):
        scr[h] = part[h * HD : (h + 1) * HD]
    for k in range(n):
        d = lax.bitwise_xor(jnp.int32(k), me)

        @pl.when(d // heads == g)
        def _():
            outs[k][0] = scr[d % heads]


def load_parts(n, me, pairs):
    for k in range(n):
        d = lax.bitwise_xor(jnp.int32(k), me)
        for part, t_ref, n_ref in pairs(k):
            if t_ref is not None:
                t_ref[d] = part
            if n_ref is not None:
                n_ref[d] = part.T


def score_of(block, first, i, kn, q_t):
    rows = lax.broadcasted_iota(jnp.int32, (block, block), 0)
    cols = lax.broadcasted_iota(jnp.int32, (block, block), 1)
    ahead = rows - cols

    def scores(j, at):
        s = dot(kn[at], q_t)
        allowed = (rows >= first - j * block) & (ahead <= (i - j) * block)
        return jnp.where(allowed, s, NEG)

    return scores


def attend_kernel(n, block, skip, me_ref, pack_ref, low_ref, first_ref, *refs):
    qkv, outs, keep_ref, logsum_ref = refs[:n], refs[n : 2 * n], refs[2 * n], refs[2 * n + 1]
    qt, vt, kn = refs[2 * n + 2 :]
    s_id = pl.program_id(0) + skip
    me = me_ref[0]
    load_parts(
        n,
        me,
        lambda k: (
            (qkv[k][0, 0, 0], qt, None),
            (qkv[k][0, 0, 1], None, kn),
            (qkv[k][0, 0, 2], vt, None),
        ),
    )

    def outer(i, carry):
        scores = score_of(block, first_ref[0, pl.ds(i, 1), :], i, kn, qt[i])
        j0 = low_ref[s_id, i]

        def forward(t, state):
            top, total, acc = state
            j = j0 + 2 * t
            at = jnp.minimum(j + 1, n - 1)
            s0, s1 = scores(j, j), scores(j + 1, at)
            peak = jnp.max(jnp.maximum(s0, s1), axis=0, keepdims=True)
            new_top = jnp.maximum(top, peak)
            p0, p1 = jnp.exp(s0 - new_top), jnp.exp(s1 - new_top)
            fade = jnp.exp(top - new_top)
            total = total * fade + jnp.sum(p0 + p1, axis=0, keepdims=True)
            acc = acc * fade + dot(vt[j], p0.astype(BF16)) + dot(vt[at], p1.astype(BF16))
            return new_top, total, acc

        top, total, acc = lax.fori_loop(
            0,
            (i - j0) // 2 + 1,
            forward,
            (
                jnp.full((1, block), NEG, F32),
                jnp.zeros((1, block), F32),
                jnp.zeros((HD, block), F32),
            ),
        )
        keep_ref[0, i] = (acc / total).astype(BF16)
        logsum_ref[0, pl.ds(i, 1), :] = top + jnp.log(total)
        return carry

    lax.fori_loop(0, n, outer, 0)
    for k in range(n):
        outs[k][0] = keep_ref[0, lax.bitwise_xor(jnp.int32(k), me)]


def attend_back_kernel(n, block, skip, me_ref, pack_ref, low_ref, first_ref, *refs):
    keep_ref, logsum_ref = refs[:2]
    qkv, grads, outs = refs[2 : n + 2], refs[n + 2 : 2 * n + 2], refs[2 * n + 2 : 3 * n + 2]
    qt, kt, gt, qn, kn, vn, gn, dk, dv, res = refs[3 * n + 2 :]
    s_id = pl.program_id(0) + skip
    me = me_ref[0]
    load_parts(
        n,
        me,
        lambda k: (
            (qkv[k][0, 0, 0], qt, qn),
            (qkv[k][0, 0, 1], kt, kn),
            (qkv[k][0, 0, 2], None, vn),
            (grads[k][0, 0], gt, gn),
        ),
    )
    dk[...] = jnp.zeros_like(dk)
    dv[...] = jnp.zeros_like(dv)

    def outer(i, carry):
        q_t, g_t, q_n, g_n = qt[i], gt[i], qn[i], gn[i]
        scores = score_of(block, first_ref[0, pl.ds(i, 1), :], i, kn, q_t)
        j0 = low_ref[s_id, i]
        inner = jnp.sum(keep_ref[0, i].astype(F32) * g_t.astype(F32), axis=0, keepdims=True)
        logsum = logsum_ref[0, pl.ds(i, 1), :]

        def one(j, at):
            p = jnp.exp(scores(j, at) - logsum)
            ds = (p * (dot(vn[at], g_t) - inner)).astype(BF16)
            return ds, dot(ds, q_n), dot(p.astype(BF16), g_n), dot(kt[at], ds)

        def backward(t, dq):
            j = j0 + 2 * t
            at = jnp.minimum(j + 1, n - 1)
            _, dk0, dv0, dq0 = one(j, j)
            _, dk1, dv1, dq1 = one(j + 1, at)
            dk[j] += dk0
            dv[j] += dv0
            dk[at] += dk1
            dv[at] += dv1
            return dq + dq0 + dq1

        dq = lax.fori_loop(0, (i - j0) // 2 + 1, backward, jnp.zeros((HD, block), F32))
        res[i, 0] = (dq * (1.0 / math.sqrt(HD))).astype(BF16)
        return carry

    lax.fori_loop(0, n, outer, 0)
    for i in range(n):
        res[i, 1] = dk[i].T.astype(BF16)
        res[i, 2] = dv[i].T.astype(BF16)
    for k in range(n):
        outs[k][0] = res[lax.bitwise_xor(jnp.int32(k), me)]


def merge_kernel(n, heads, slices, me_ref, *refs):
    recv = refs[:n]
    c_ref, merge_ref, branch_ref, out_branch, out_weight, scr, acc = refs[n:]
    s_id, g = pl.program_id(0), pl.program_id(1)
    groups = pl.num_programs(1)
    me = me_ref[0]
    width = heads * HD

    @pl.when((s_id == 0) & (g == 0))
    def _():
        acc[...] = jnp.zeros_like(acc)

    for k in range(n):
        d = lax.bitwise_xor(jnp.int32(k), me)

        @pl.when(d // heads == g)
        def _():
            scr[d % heads] = recv[k][0, 0, 0]

    attended = scr[...].reshape(width, c_ref.shape[1])
    acc[...] += dot(attended, c_ref[0])
    branch = dot(attended.T, merge_ref[...]) + branch_ref[0].astype(F32)
    cols = branch.shape[1] // slices
    for m in range(slices):
        out_branch[m, 0] = branch[:, m * cols : (m + 1) * cols].astype(BF16)

    @pl.when((s_id == pl.num_programs(0) - 1) & (g == groups - 1))
    def _():
        out_weight[...] = acc[...].astype(BF16)


def close_kernel(n, heads, me_ref, *refs):
    recv = refs[:n]
    normed_ref, w_ref, cos_ref, sin_ref, low_ref, out_low, out_weight, scr, acc = refs[n:]
    s_id, g = pl.program_id(0), pl.program_id(1)
    groups = pl.num_programs(1)
    me = me_ref[0]
    width = heads * HD
    shard = normed_ref.shape[1]

    @pl.when((s_id == 0) & (g == 0))
    def _():
        acc[...] = jnp.zeros_like(acc)

    for k in range(n):
        d = lax.bitwise_xor(jnp.int32(k), me)

        @pl.when(d // heads == g)
        def _():
            for j in range(3):
                scr[j, d % heads] = recv[k][0, 0, j]

    parts = []
    for j in (0, 1):
        part = scr[j].reshape(width, shard).astype(F32)
        parts.append(turn(part, cos_ref[0], -sin_ref[0], heads).astype(BF16))
    parts.append(scr[2].reshape(width, shard))
    grads = jnp.concatenate(parts, axis=0)
    acc[...] += dot(grads, normed_ref[0])
    low = dot(grads.T, w_ref[...]) + low_ref[0].astype(F32)
    out_low[0] = low.astype(BF16)

    @pl.when((s_id == pl.num_programs(0) - 1) & (g == groups - 1))
    def _():
        out_weight[...] = acc[...]


def place_kernel(block, share, shard, slices, chunks, per_piece, pack_ref, *refs):
    pieces, out, buf, sems, out_sems = refs[:-4], refs[-4], refs[-3], refs[-2], refs[-1]
    me = pack_ref[chunks * slices * share // shard]
    loads, stores = [], []
    arrays = max(ref for ref, _ in per_piece) + 1
    for c in range(chunks):
        for k in range(slices):
            ref, where = per_piece[k]
            for t in range(share // block):
                at = len(loads)
                row = (c * slices + lax.bitwise_xor(jnp.int32(k), me)) * share + t * block
                start = pl.multiple_of(lax.rem(row, shard), block)
                loads.append(
                    pltpu.make_async_copy(
                        pieces[c * arrays + ref].at[where, pl.ds(t * block, block)],
                        buf.at[at],
                        sems.at[at],
                    )
                )
                stores.append(
                    pltpu.make_async_copy(
                        buf.at[at],
                        out.at[pack_ref[row // shard], pl.ds(start, block)],
                        out_sems.at[at],
                    )
                )
    for copy in loads:
        copy.start()
    for load, store in zip(loads, stores):
        load.wait()
        store.start()
    for copy in stores:
        copy.wait()


def small_kernel(n, slices, x_ref, out_ref, first, second, sems, sems2):
    rank, column = lax.axis_index("seq"), lax.axis_index("mlp")
    barrier = pltpu.get_barrier_semaphore()
    peers = [{"seq": lax.bitwise_xor(rank, k)} for k in range(1, n)]
    rows = [{"mlp": lax.bitwise_xor(column, k)} for k in range(1, slices)]
    for peer in peers + rows:
        pl.semaphore_signal(barrier, inc=1, device_id=peer, device_id_type=pl.DeviceIdType.MESH)
    pl.semaphore_wait(barrier, len(peers) + len(rows))

    def exchange(source, target, sems, peers):
        copies = [
            pltpu.make_async_remote_copy(
                src_ref=source(k),
                dst_ref=target.at[k],
                send_sem=sems.at[0, k],
                recv_sem=sems.at[1, k],
                device_id=peer,
                device_id_type=pl.DeviceIdType.MESH,
            )
            for k, peer in enumerate(peers)
        ]
        for copy in copies:
            copy.start()
        for copy in copies:
            copy.wait()

    exchange(lambda k: x_ref.at[lax.bitwise_xor(rank, k + 1)], first, sems, peers)
    total = x_ref[rank]
    for k in range(n - 1):
        total = total + first[k]
    second[slices - 1] = total
    second[slices] = total
    exchange(lambda k: second.at[slices], second, sems2, rows)
    parts = [
        second[jnp.where(column == c, slices - 1, lax.bitwise_xor(column, c) - 1)]
        for c in range(slices)
    ]
    out_ref[...] = functools.reduce(jnp.add, parts)


def small_sum(vectors, n, slices):
    count, width = vectors.shape
    x = jnp.transpose(vectors.reshape(count, n, width // n), (1, 0, 2))
    return pl.pallas_call(
        functools.partial(small_kernel, n, slices),
        out_shape=jax.ShapeDtypeStruct((count, width // n), F32),
        in_specs=[pl.BlockSpec(memory_space=pltpu.VMEM)],
        out_specs=pl.BlockSpec(memory_space=pltpu.VMEM),
        scratch_shapes=[
            pltpu.VMEM((n - 1, count, width // n), F32),
            pltpu.VMEM((slices + 1, count, width // n), F32),
            pltpu.SemaphoreType.DMA((2, n - 1)),
            pltpu.SemaphoreType.DMA((2, slices - 1)),
        ],
        compiler_params=pltpu.CompilerParams(collective_id=0, has_side_effects=True),
        cost_estimate=COST,
        name="small_sum",
    )(x)


def params():
    return pltpu.CompilerParams(vmem_limit_bytes=VMEM_LIMIT)


def tie(*values):
    return lax.optimization_barrier(values)


def send_x(parts):
    n = len(parts)
    sent = jnp.stack([parts[k] for k in range(1, n, 2)])
    return lax.ppermute(sent, "seq", [(i, i ^ 1) for i in range(n)])


def send_z(parts, got, steps=None):
    n = len(parts)
    return [
        lax.ppermute(
            jnp.stack([parts[k], got[k // 2]]), "seq", [(i, i ^ k) for i in range(n)]
        )
        for k in (range(2, n, 2) if steps is None else steps)
    ]


def received(parts, got, gots):
    out = [(parts[0][None], 0), (got, 0)]
    for array in gots:
        out += [(array, 0), (array, 1)]
    return out


def span(masks):
    out = [0]
    for m in masks:
        out += [v ^ m for v in out]
    return out


def cube_send(chunks, axis, n, masks):
    kept = span(masks[1:])
    sent = jnp.stack([chunks[k ^ masks[0]] for k in kept])
    return lax.ppermute(sent, axis, [(i, i ^ masks[0]) for i in range(n)])


def cube_add(chunks, got, masks, kind):
    return {
        k: (chunks[k].astype(F32) + got[at].astype(F32)).astype(kind)
        for at, k in enumerate(span(masks[1:]))
    }


def cube_sum(chunks, axis, masks, kind):
    n = len(chunks)
    chunks = {k: v.astype(kind) for k, v in enumerate(chunks)}
    for step in range(len(masks)):
        got = cube_send(chunks, axis, n, masks[step:])
        chunks = cube_add(chunks, got, masks[step:], F32 if step == len(masks) - 1 else kind)
    return chunks[0]


def gather_step(arrays, axis, n, m):
    sent = jnp.concatenate(arrays, axis=0) if len(arrays) > 1 else arrays[0]
    return arrays + [lax.ppermute(sent, axis, [(i, i ^ m) for i in range(n)])]


def masks_of(n):
    return [1 << b for b in range(n.bit_length() - 1)]


def turned(masks, by):
    by = by % len(masks)
    return masks[by:] + masks[:by]


def cut(array, axis, n, me):
    size = array.shape[axis] // n
    return [
        lax.dynamic_slice_in_dim(array, lax.bitwise_xor(jnp.int32(k), me) * size, size, axis)
        for k in range(n)
    ]


def on_device(
    tokens,
    lengths,
    counts,
    norm_gain,
    norm_bias,
    head_weight,
    merge_weight,
    up_weight,
    up_bias,
    down_weight,
    down_bias,
    cotangent,
):
    packs, shard, width = tokens.shape
    n = lax.axis_size("seq")
    slices = lax.axis_size("mlp")
    pack_len = shard * n
    rank = lax.axis_index("seq")
    column = lax.axis_index("mlp")
    heads = merge_weight.shape[0] // HD
    joined = heads * HD
    groups = n // heads
    slots = -(-packs // groups)
    dealt = groups * slots
    spare = 1 if dealt > packs else 0
    rows = dealt * shard
    chunks = 2 if slots % 2 == 0 else 1
    per = slots // chunks
    seq_masks, mlp_masks = masks_of(n), masks_of(slices)

    first, position, cost = layout(lengths, counts, pack_len)
    ids = jnp.arange(packs, dtype=jnp.int32)
    before = (cost[None, :] > cost[:, None]) | (
        (cost[None, :] == cost[:, None]) & (ids[None, :] < ids[:, None])
    )
    order = jnp.sum(before.astype(jnp.int32), axis=1)
    slot_of = order // groups
    group_of = jnp.where(slot_of % 2 == 0, order % groups, groups - 1 - order % groups)
    at = slot_of * groups + group_of
    hit = at[None, :] == jnp.arange(dealt, dtype=jnp.int32)[:, None]
    pack_at = jnp.where(
        jnp.any(hit, axis=-1), jnp.sum(jnp.where(hit, ids, 0), axis=-1), packs
    ).astype(jnp.int32)
    safe = jnp.minimum(pack_at, packs - 1)
    me = rank.astype(jnp.int32).reshape(1)

    own_cot = jnp.take(cotangent, safe, axis=0, mode="clip")
    if spare:
        own_cot = jnp.where((pack_at < packs)[:, None, None], own_cot, 0)
    cot = lax.all_gather(own_cot, "mlp", axis=2, tiled=True)

    half = ROT // 2
    freq = 10000.0 ** (-(2.0 * jnp.arange(half, dtype=F32)) / ROT)
    own_position = jnp.take(
        lax.dynamic_slice_in_dim(position, rank * shard, shard, 1), safe, axis=0, mode="clip"
    )
    angle = own_position.astype(F32)[:, None, :] * jnp.repeat(freq, 2)[None, :, None]
    cosine, sine = jnp.cos(angle), jnp.sin(angle)

    w_t = jnp.transpose(head_weight, (0, 2, 1)).reshape(3 * joined, width)

    def whole2(s, g, *_):
        return (0, 0)

    def rows_at(skip):
        return pl.BlockSpec((1, shard, width), lambda s, g, *_: ((s + skip) * groups + g, 0, 0))

    def table_at(skip):
        return pl.BlockSpec((1, ROT, shard), lambda s, g, *_: ((s + skip) * groups + g, 0, 0))

    parts = [jax.ShapeDtypeStruct((per, 3, HD, shard), BF16)] * n

    def chunk_at(c):
        return pl.BlockSpec(
            (1, 3, HD, shard), lambda s, g, *_: (jnp.clip(s - c * per, 0, per - 1), 0, 0, 0)
        )

    outs = pl.pallas_call(
        functools.partial(head_kernel, n, heads, per),
        grid_spec=pltpu.PrefetchScalarGridSpec(
            num_scalar_prefetch=2,
            grid=(slots, groups),
            in_specs=[
                pl.BlockSpec((1, shard, width), lambda s, g, a, b: (b[s * groups + g], 0, 0)),
                pl.BlockSpec((1, width), whole2),
                pl.BlockSpec((1, width), whole2),
                pl.BlockSpec((3 * joined, width), whole2),
                table_at(0),
                table_at(0),
            ],
            out_specs=[rows_at(0)] * 2 + [chunk_at(c) for c in range(chunks) for _ in range(n)],
            scratch_shapes=[pltpu.VMEM((heads, 3, HD, shard), BF16)],
        ),
        out_shape=[jax.ShapeDtypeStruct((dealt, shard, width), BF16)] * 2 + parts * chunks,
        compiler_params=params(),
        cost_estimate=COST,
        name="heads",
    )(
        me,
        safe,
        tokens,
        norm_gain.reshape(1, width),
        norm_bias.reshape(1, width),
        w_t,
        cosine,
        sine,
    )
    normed_low, tokens_dealt = outs[0], outs[1]
    qkv = [list(outs[2 + c * n : 2 + (c + 1) * n]) for c in range(chunks)]

    def out_grads(cot, merge_weight):
        return pl.pallas_call(
            functools.partial(grad_kernel, n, heads),
            grid_spec=pltpu.PrefetchScalarGridSpec(
                num_scalar_prefetch=1,
                grid=(slots, groups),
                in_specs=[rows_at(0), pl.BlockSpec((joined, width), whole2)],
                out_specs=[pl.BlockSpec((1, HD, shard), lambda s, g, *_: (s, 0, 0))] * n,
                scratch_shapes=[pltpu.VMEM((heads, HD, shard), BF16)],
            ),
            out_shape=[jax.ShapeDtypeStruct((slots, HD, shard), BF16)] * n,
            compiler_params=params(),
            cost_estimate=COST,
            name="out_grads",
        )(me, cot, merge_weight)

    mine = rank // heads + groups * jnp.arange(slots, dtype=jnp.int32)
    my_packs = jnp.take(safe, mine, mode="clip")
    first = first.reshape(packs, n, shard)
    lows = (jnp.take(first[:, :, 0], my_packs, axis=0, mode="clip") // shard).astype(jnp.int32)
    wide = [pltpu.VMEM((n, HD, shard), BF16)]
    tall = [pltpu.VMEM((n, shard, HD), BF16)]

    def first_at(skip):
        return pl.BlockSpec((1, n, shard), lambda s, a, b, c: (b[s + skip], 0, 0))

    def qkv_at(lead):
        return pl.BlockSpec((1, 1, 3, HD, shard), lambda s, *_: (lead, s, 0, 0, 0))

    def grad_at(lead, skip):
        return pl.BlockSpec((1, 1, HD, shard), lambda s, *_: (lead, s + skip, 0, 0))

    def attend(c, sources):
        return pl.pallas_call(
            functools.partial(attend_kernel, n, shard, c * per),
            grid_spec=pltpu.PrefetchScalarGridSpec(
                num_scalar_prefetch=3,
                grid=(per,),
                in_specs=[first_at(c * per)] + [qkv_at(lead) for _, lead in sources],
                out_specs=[pl.BlockSpec((1, HD, shard), lambda s, *_: (s, 0, 0))] * n
                + [
                    pl.BlockSpec((1, n, HD, shard), lambda s, *_: (s, 0, 0, 0)),
                    pl.BlockSpec((1, n, shard), lambda s, *_: (s, 0, 0)),
                ],
                scratch_shapes=wide * 2 + tall,
            ),
            out_shape=[jax.ShapeDtypeStruct((per, HD, shard), BF16)] * n
            + [
                jax.ShapeDtypeStruct((per, n, HD, shard), BF16),
                jax.ShapeDtypeStruct((per, n, shard), F32),
            ],
            compiler_params=params(),
            cost_estimate=COST,
            name="attend",
        )(me, my_packs, lows, first, *[array for array, _ in sources])

    def attend_back(c, kept, logsum, sources, grads):
        return pl.pallas_call(
            functools.partial(attend_back_kernel, n, shard, c * per),
            grid_spec=pltpu.PrefetchScalarGridSpec(
                num_scalar_prefetch=3,
                grid=(per,),
                in_specs=[
                    first_at(c * per),
                    pl.BlockSpec((1, n, HD, shard), lambda s, *_: (s, 0, 0, 0)),
                    pl.BlockSpec((1, n, shard), lambda s, *_: (s, 0, 0)),
                ]
                + [qkv_at(lead) for _, lead in sources]
                + [grad_at(lead, c * per) for _, lead in grads],
                out_specs=[pl.BlockSpec((1, 3, HD, shard), lambda s, *_: (s, 0, 0, 0))] * n,
                scratch_shapes=wide * 3
                + tall * 4
                + [pltpu.VMEM((n, shard, HD), F32)] * 2
                + [pltpu.VMEM((n, 3, HD, shard), BF16)],
            ),
            out_shape=parts,
            compiler_params=params(),
            cost_estimate=COST,
            name="attend_back",
        )(
            me,
            my_packs,
            lows,
            first,
            kept,
            logsum,
            *[array for array, _ in sources],
            *[array for array, _ in grads],
        )

    def merge(sources, branch_ff):
        return pl.pallas_call(
            functools.partial(merge_kernel, n, heads, slices),
            grid_spec=pltpu.PrefetchScalarGridSpec(
                num_scalar_prefetch=1,
                grid=(slots, groups),
                in_specs=[
                    pl.BlockSpec(
                        (1, 1, 1, HD, shard),
                        lambda s, g, *_, lead=lead: (lead, s // per, s % per, 0, 0),
                    )
                    for _, lead in sources
                ]
                + [rows_at(0), pl.BlockSpec((joined, width), whole2), rows_at(0)],
                out_specs=[
                    pl.BlockSpec(
                        (slices, 1, shard, width // slices),
                        lambda s, g, *_: (0, s * groups + g, 0, 0),
                    ),
                    pl.BlockSpec((joined, width), whole2),
                ],
                scratch_shapes=[
                    pltpu.VMEM((heads, HD, shard), BF16),
                    pltpu.VMEM((joined, width), F32),
                ],
            ),
            out_shape=[
                jax.ShapeDtypeStruct((slices, dealt, shard, width // slices), BF16),
                jax.ShapeDtypeStruct((joined, width), BF16),
            ],
            compiler_params=params(),
            cost_estimate=COST,
            name="merge",
        )(me, *[array for array, _ in sources], cot, merge_weight, branch_ff)

    def close(c, sources):
        skip = c * per
        return pl.pallas_call(
            functools.partial(close_kernel, n, heads),
            grid_spec=pltpu.PrefetchScalarGridSpec(
                num_scalar_prefetch=1,
                grid=(per, groups),
                in_specs=[
                    pl.BlockSpec(
                        (1, 1, 3, HD, shard), lambda s, g, *_, lead=lead: (lead, s, 0, 0, 0)
                    )
                    for _, lead in sources
                ]
                + [
                    rows_at(skip),
                    pl.BlockSpec((3 * joined, width), whole2),
                    table_at(skip),
                    table_at(skip),
                    rows_at(skip),
                ],
                out_specs=[rows_at(0), pl.BlockSpec((3 * joined, width), whole2)],
                scratch_shapes=[
                    pltpu.VMEM((3, heads, HD, shard), BF16),
                    pltpu.VMEM((3 * joined, width), F32),
                ],
            ),
            out_shape=[
                jax.ShapeDtypeStruct((per * groups, shard, width), BF16),
                jax.ShapeDtypeStruct((3 * joined, width), F32),
            ],
            compiler_params=params(),
            cost_estimate=COST,
            name="close",
        )(me, *[array for array, _ in sources], normed_low, w_t, cosine, sine, low_ff)

    got_x = [None] * chunks
    got_z = [None] * chunks
    got_x[0] = send_x(qkv[0])
    hidden = (
        jnp.einsum("psd,df->psf", normed_low, up_weight, preferred_element_type=F32) + up_bias
    )
    active_low = jax.nn.gelu(hidden, approximate=True).astype(BF16)
    branch_ff = jnp.einsum(
        "psf,fd->psd", active_low, down_weight, preferred_element_type=F32
    ).astype(BF16)
    got_x[0], branch_ff, qkv, out_weight, back_weight = tie(
        got_x[0], branch_ff, qkv, merge_weight, down_weight
    )

    got_z[0] = send_z(qkv[0], got_x[0])
    if chunks > 1:
        got_x[1] = send_x(qkv[1])
    sends = out_grads(cot, out_weight)
    active_grad = jnp.einsum("psd,fd->psf", cot, back_weight, preferred_element_type=F32)
    _, gelu_back = jax.vjp(lambda values: jax.nn.gelu(values, approximate=True), hidden)
    hidden_grad = gelu_back(active_grad)[0].astype(BF16)
    got_x, got_z, qkv, sends, hidden_grad = tie(got_x, got_z, qkv, sends, hidden_grad)

    got_dx = send_x(sends)
    sources = [received(qkv[0], got_x[0], got_z[0])]
    if chunks > 1:
        got_z[1] = send_z(qkv[1], got_x[1])
        sources.append(received(qkv[1], got_x[1], got_z[1]))
    ahead = [attend(0, sources[0])]
    up_grad = jnp.einsum(
        "psd,psf->df", normed_low, hidden_grad, preferred_element_type=F32
    ).astype(BF16)
    down_grad = jnp.einsum("psd,psf->df", cot, active_low, preferred_element_type=F32).astype(BF16)
    biases = jnp.sum(hidden_grad.astype(F32), axis=(0, 1)), jnp.sum(cot.astype(F32), axis=(0, 1))
    got_dx, sources_arrays, ahead, sends, hidden_grad, up_grad, down_grad, biases = tie(
        got_dx,
        [[a for a, _ in v] for v in sources],
        ahead,
        sends,
        hidden_grad,
        up_grad,
        down_grad,
        biases,
    )
    def with_row(*parts):
        weight = jnp.concatenate(parts[:2], axis=1)
        row = jnp.concatenate(parts[2:])
        row = jnp.pad(row, (0, weight.shape[1] - row.shape[0])).reshape(1, -1)
        row = jnp.broadcast_to(row, (16, weight.shape[1])).astype(BF16)
        return jnp.concatenate([weight, row], axis=0)

    terms = dict(
        enumerate(
            with_row(*parts)
            for parts in zip(*[cut(v, 0, n, rank) for v in (up_grad, down_grad, *biases)])
        )
    )
    terms_got = cube_send(terms, "seq", n, seq_masks)
    sources = [
        [(a, lead) for a, (_, lead) in zip(arrays, v)] for arrays, v in zip(sources_arrays, sources)
    ]

    got_dz = send_z(sends, got_dx)
    if chunks > 1:
        ahead.append(attend(1, sources[1]))
    low_ff = jnp.einsum(
        "psf,df->psd", hidden_grad, up_weight, preferred_element_type=F32
    ).astype(BF16)
    got_dz, ahead, low_ff = tie(got_dz, ahead, low_ff)
    grads = received(sends, got_dx, got_dz)

    attended = [jnp.stack([outs[k] for outs in ahead]) for k in range(n)]
    got_ax = send_x(attended)
    backs = [attend_back(0, ahead[0][n], ahead[0][n + 1], sources[0], grads)]
    got_ax, terms_got, backs, attended, ahead = tie(got_ax, terms_got, backs, attended, ahead)

    terms = cube_add(terms, terms_got, seq_masks, BF16)
    terms_got = cube_send(terms, "seq", n, seq_masks[1:])
    got_az = send_z(attended, got_ax)
    back_x = [send_x(backs[0])]
    if chunks > 1:
        backs.append(attend_back(1, ahead[1][n], ahead[1][n + 1], sources[1], grads))
    got_az, terms_got, back_x, backs = tie(got_az, terms_got, back_x, backs)

    back_z = [send_z(backs[0], back_x[0])]
    if chunks > 1:
        back_x.append(send_x(backs[1]))
    for step in range(1, len(seq_masks)):
        last_step = step == len(seq_masks) - 1
        terms = cube_add(terms, terms_got, seq_masks[step:], F32 if last_step else BF16)
        if not last_step:
            terms_got = cube_send(terms, "seq", n, seq_masks[step + 1 :])
    terms = terms[0]
    branch, merge_part = merge(received(attended, got_ax, got_az), branch_ff)
    summed = lax.psum_scatter(branch, "mlp", scatter_dimension=0, tiled=False)
    back_x, back_z, backs, merge_part, terms = tie(back_x, back_z, backs, merge_part, terms)

    share = per * groups * shard // slices

    def share_sum(low):
        return cube_sum(
            cut(low.reshape(share * slices, width), 0, slices, column), "mlp", mlp_masks, BF16
        )

    def finish(c, low_sum):
        start = (c * slices + column) * share
        row_in = lax.dynamic_slice_in_dim(
            tokens_dealt.reshape(rows, width), start, share, 0
        ).astype(F32)
        row_cot = lax.dynamic_slice_in_dim(cot.reshape(rows, width), start, share, 0).astype(F32)
        cent = row_in - jnp.mean(row_in, axis=-1, keepdims=True)
        inverse = lax.rsqrt(jnp.mean(cent * cent, axis=-1, keepdims=True) + EPS)
        xhat = cent * inverse
        g = low_sum * norm_gain
        row_grad = (
            row_cot
            + (
                g
                - jnp.mean(g, axis=-1, keepdims=True)
                - xhat * jnp.mean(g * xhat, axis=-1, keepdims=True)
            )
            * inverse
        ).astype(BF16)
        return row_grad, jnp.stack([jnp.sum(low_sum * xhat, axis=0), jnp.sum(low_sum, axis=0)])

    low, head_part = close(0, received(backs[0], back_x[0], back_z[0]))
    head_parts = [head_part]
    if chunks > 1:
        second = send_z(backs[1], back_x[1], [n // 2])
        second, low, head_parts, backs, back_x = tie(second, low, head_parts, backs, back_x)
        others = send_z(backs[1], back_x[1], [k for k in range(2, n, 2) if k != n // 2])
        others.insert(n // 4 - 1, second[0])
        back_z.append(others)
    row_grad, vectors = finish(0, share_sum(low))
    back_z, row_grad, vectors = tie(back_z, row_grad, vectors)

    cols = width // slices
    pieces = gather_step([row_grad[None]], "mlp", slices, mlp_masks[-1])
    result = (
        lax.dynamic_slice_in_dim(tokens, column * cols, cols, 2).astype(F32)
        + jnp.take(summed, at, axis=0, mode="clip").astype(F32)
        + lax.dynamic_slice_in_dim(down_bias, column * cols, cols, 0)
    ).astype(BF16)
    if chunks > 1:
        low, head_part = close(1, received(backs[1], back_x[1], back_z[1]))
        head_parts.append(head_part)
        pieces, low, head_parts, result = tie(pieces, low, head_parts, result)
    weights = functools.reduce(jnp.add, head_parts)
    weights = jnp.concatenate([weights.astype(BF16), merge_part], axis=0)
    weights = dict(enumerate(cut(weights, 1, n, rank)))
    weights_got = cube_send(weights, "seq", n, seq_masks)
    if chunks > 1:
        low_sum = share_sum(low)
        for m in reversed(mlp_masks[:-1]):
            pieces = gather_step(pieces, "mlp", slices, m)
        row_grad, more = finish(1, low_sum)
        vectors = vectors + more
        row_grad, pieces, weights_got, vectors = tie(row_grad, pieces, weights_got, vectors)
        last = gather_step([row_grad[None]], "mlp", slices, mlp_masks[-1])
    else:
        last, pieces = pieces, []
    vectors = small_sum(vectors, n, slices)
    weights = cube_add(weights, weights_got, seq_masks, BF16)
    weights_got = cube_send(weights, "seq", n, seq_masks[1:])
    last, vectors, weights_got = tie(last, vectors, weights_got)
    for m in reversed(mlp_masks[:-1]):
        last = gather_step(last, "mlp", slices, m)
    pieces += last
    where = [(0, 0)]
    lookup = [0]
    for i, m in enumerate(reversed(mlp_masks)):
        where += [(i + 1, j) for j in range(len(lookup))]
        lookup += [k ^ m for k in lookup]
    per_piece = [where[lookup.index(k)] for k in range(slices)]
    block = math.gcd(share, shard)
    tokens_grad = pl.pallas_call(
        functools.partial(
            place_kernel, block, share, shard, slices, chunks, per_piece
        ),
        grid_spec=pltpu.PrefetchScalarGridSpec(
            num_scalar_prefetch=1,
            grid=(1,),
            in_specs=[pl.BlockSpec(memory_space=pl.ANY)] * len(pieces),
            out_specs=pl.BlockSpec(memory_space=pl.ANY),
            scratch_shapes=[
                pltpu.VMEM((rows // block, block, width), BF16),
                pltpu.SemaphoreType.DMA((rows // block,)),
                pltpu.SemaphoreType.DMA((rows // block,)),
            ],
        ),
        out_shape=jax.ShapeDtypeStruct((packs + spare, shard, width), BF16),
        compiler_params=params(),
        name="place",
    )(jnp.concatenate([pack_at, column.astype(jnp.int32).reshape(1)]), *pieces)[:packs]

    for step in range(1, len(seq_masks)):
        weights = cube_add(
            weights, weights_got, seq_masks[step:], F32 if step == len(seq_masks) - 1 else BF16
        )
        if step < len(seq_masks) - 1:
            weights_got = cube_send(weights, "seq", n, seq_masks[step + 1 :])
    weights = weights[0]
    head_grad = jnp.transpose(
        weights[: 3 * joined].reshape(3, joined, width // n), (0, 2, 1)
    )
    merge_grad = weights[3 * joined :]
    part, hidden_here = width // n, up_weight.shape[1]
    up_grad, down_grad = terms[:part, :hidden_here], terms[:part, hidden_here:].T
    up_bias_grad = terms[part, : hidden_here // n]
    down_bias_grad = terms[part, hidden_here // n : hidden_here // n + part]
    return (
        result,
        tokens_grad,
        vectors[0],
        vectors[1],
        head_grad,
        merge_grad,
        up_grad,
        up_bias_grad,
        down_grad,
        down_bias_grad,
    )


def qkv_kernel(heads, me_ref, x_ref, w_ref, cos_ref, sin_ref, normed_ref, out_ref):
    width = heads * HD
    normed = x_ref[0]
    normed_ref[...] = normed
    for j in range(3):
        part = dot(w_ref[j * width : (j + 1) * width, :], normed, ((1,), (1,)))
        if j < 2:
            part = turn(part, cos_ref[...], sin_ref[...], heads)
        if j == 0:
            part = part * (1.0 / math.sqrt(HD))
        part = part.astype(BF16)
        for h in range(heads):
            out_ref[h, j] = part[h * HD : (h + 1) * HD]


def allowed_of(block, first, i):
    rows = lax.broadcasted_iota(jnp.int32, (block, block), 0)
    cols = lax.broadcasted_iota(jnp.int32, (block, block), 1)
    ahead = rows - cols
    return lambda j: (rows >= first - j * block) & (ahead <= (i - j) * block)


def unit_kernel(n, block, me_ref, low_ref, first_ref, qkv_ref, out_ref, keep_ref, logsum_ref, qt, vt, kn):
    me = me_ref[0]
    pair = range(qkv_ref.shape[0])
    for u in pair:
        for i in range(n):
            at = slice(i * block, (i + 1) * block)
            qt[u, i] = qkv_ref[u, 0, :, at]
            kn[u, i] = qkv_ref[u, 1, :, at].T
            vt[u, i] = qkv_ref[u, 2, :, at]

    def outer(i, carry):
        allowed = allowed_of(block, first_ref[pl.ds(i, 1), :], i)
        j0 = low_ref[i]

        def forward(t, states):
            j = j0 + 2 * t
            at = jnp.minimum(j + 1, n - 1)
            mask0, mask1 = allowed(j), allowed(j + 1)
            out = []
            for u, (top, total, acc) in zip(pair, states):
                q_t = qt[u, i]
                s0 = jnp.where(mask0, dot(kn[u, j], q_t), NEG)
                s1 = jnp.where(mask1, dot(kn[u, at], q_t), NEG)
                peak = jnp.max(jnp.maximum(s0, s1), axis=0, keepdims=True)
                new_top = jnp.maximum(top, peak)
                p0, p1 = jnp.exp(s0 - new_top), jnp.exp(s1 - new_top)
                fade = jnp.exp(top - new_top)
                total = total * fade + jnp.sum(p0 + p1, axis=0, keepdims=True)
                acc = acc * fade + dot(vt[u, j], p0.astype(BF16)) + dot(vt[u, at], p1.astype(BF16))
                out.append((new_top, total, acc))
            return tuple(out)

        states = lax.fori_loop(
            0,
            (i - j0) // 2 + 1,
            forward,
            tuple(
                (
                    jnp.full((1, block), NEG, F32),
                    jnp.zeros((1, block), F32),
                    jnp.zeros((HD, block), F32),
                )
                for _ in pair
            ),
        )
        for u, (top, total, acc) in zip(pair, states):
            keep_ref[u, i] = (acc / total).astype(BF16)
            logsum_ref[u, pl.ds(i, 1), :] = top + jnp.log(total)
        return carry

    lax.fori_loop(0, n, outer, 0)
    for k in range(n):
        for u in pair:
            out_ref[k, u] = keep_ref[u, lax.bitwise_xor(jnp.int32(k), me)]


def unit_back_kernel(
    n, block, me_ref, low_ref, first_ref, keep_ref, logsum_ref, qkv_ref, grad_ref, out_ref,
    qt, kt, gt, qn, kn, vn, gn, dk, dv, dqs
):
    me = me_ref[0]
    pair = range(qkv_ref.shape[0])
    for u in pair:
        for i in range(n):
            at = slice(i * block, (i + 1) * block)
            for j, (t_ref, n_ref) in enumerate(((qt, qn), (kt, kn), (None, vn))):
                part = qkv_ref[u, j, :, at]
                if t_ref is not None:
                    t_ref[u, i] = part
                n_ref[u, i] = part.T
        for k in range(n):
            d = lax.bitwise_xor(jnp.int32(k), me)
            part = grad_ref[k, u]
            gt[u, d] = part
            gn[u, d] = part.T
    dk[...] = jnp.zeros_like(dk)
    dv[...] = jnp.zeros_like(dv)

    def outer(i, carry):
        allowed = allowed_of(block, first_ref[pl.ds(i, 1), :], i)
        j0 = low_ref[i]
        inner = [
            jnp.sum(keep_ref[u, i].astype(F32) * gt[u, i].astype(F32), axis=0, keepdims=True)
            for u in pair
        ]
        logsum = [logsum_ref[u, pl.ds(i, 1), :] for u in pair]

        def one(u, mask, at):
            s = jnp.where(mask, dot(kn[u, at], qt[u, i]), NEG)
            p = jnp.exp(s - logsum[u])
            ds = (p * (dot(vn[u, at], gt[u, i]) - inner[u])).astype(BF16)
            return dot(ds, qn[u, i]), dot(p.astype(BF16), gn[u, i]), dot(kt[u, at], ds)

        def backward(t, dqs):
            j = j0 + 2 * t
            at = jnp.minimum(j + 1, n - 1)
            mask0, mask1 = allowed(j), allowed(j + 1)
            out = []
            for u, dq in zip(pair, dqs):
                dk0, dv0, dq0 = one(u, mask0, j)
                dk1, dv1, dq1 = one(u, mask1, at)
                dk[u, j] += dk0
                dv[u, j] += dv0
                dk[u, at] += dk1
                dv[u, at] += dv1
                out.append(dq + dq0 + dq1)
            return tuple(out)

        dq = lax.fori_loop(
            0, (i - j0) // 2 + 1, backward, tuple(jnp.zeros((HD, block), F32) for _ in pair)
        )
        for u in pair:
            dqs[u, i] = (dq[u] * (1.0 / math.sqrt(HD))).astype(BF16)
        return carry

    lax.fori_loop(0, n, outer, 0)
    for u in pair:
        for i in range(n):
            at = slice(i * block, (i + 1) * block)
            out_ref[u, 0, :, at] = dqs[u, i]
            out_ref[u, 1, :, at] = dk[u, i].T.astype(BF16)
            out_ref[u, 2, :, at] = dv[u, i].T.astype(BF16)


def rows_kernel(heads, slices, me_ref, grad_ref, normed_ref, w_ref, cos_ref, sin_ref, low_ref, weight_ref):
    width = heads * HD
    column = me_ref[1]

    @pl.when(pl.program_id(0) == 0)
    def _():
        weight_ref[...] = jnp.zeros_like(weight_ref)

    parts = []
    for j in range(3):
        part = jnp.concatenate([grad_ref[h, j] for h in range(heads)], axis=0)
        if j < 2:
            part = turn(part.astype(F32), cos_ref[...], -sin_ref[...], heads).astype(BF16)
        parts.append(part)
    grads = jnp.concatenate(parts, axis=0)
    weight_ref[...] += dot(grads, normed_ref[...])
    low = dot(grads.T, w_ref[...]).astype(BF16)
    part = low.shape[0] // slices
    for m in range(slices):
        low_ref[lax.bitwise_xor(jnp.int32(m), column), 0] = low[m * part : (m + 1) * part]


def norm_kernel(x_ref, gain_ref, bias_ref, normed_ref):
    x = x_ref[0].astype(F32)
    cent = x - jnp.mean(x, axis=-1, keepdims=True)
    var = jnp.mean(cent * cent, axis=-1, keepdims=True)
    normed_ref[0] = (cent * lax.rsqrt(var + EPS) * gain_ref[...] + bias_ref[...]).astype(BF16)


def finish_kernel(terms, which_ref, *refs):
    lows = refs[:terms]
    low_ref, x_ref, c_ref, gain_ref, out_ref, sums_ref = refs[terms:]

    @pl.when(pl.program_id(0) == 0)
    def _():
        sums_ref[...] = jnp.zeros_like(sums_ref)

    low = low_ref[0].astype(F32)
    for ref in lows:
        low = low + ref[0].astype(F32)
    x = x_ref[0].astype(F32)
    cent = x - jnp.mean(x, axis=-1, keepdims=True)
    inverse = lax.rsqrt(jnp.mean(cent * cent, axis=-1, keepdims=True) + EPS)
    xhat = cent * inverse
    g = low * gain_ref[...]
    inner = jnp.mean(g * xhat, axis=-1, keepdims=True)
    back = (g - jnp.mean(g, axis=-1, keepdims=True) - xhat * inner) * inverse
    out_ref[0] = (c_ref[0].astype(F32) + back).astype(BF16)
    sums_ref[0:1] += jnp.sum(low * xhat, axis=0, keepdims=True)
    sums_ref[1:2] += jnp.sum(low, axis=0, keepdims=True)


def join_kernel(slices, attended_ref, c_ref, merge_ref, branch_ref, out_branch, out_weight):
    @pl.when(pl.program_id(0) == 0)
    def _():
        out_weight[...] = jnp.zeros_like(out_weight)

    attended = attended_ref[0]
    out_weight[...] += dot(attended, c_ref[0])
    branch = dot(attended.T, merge_ref[...]) + branch_ref[0].astype(F32)
    cols = branch.shape[1] // slices
    for m in range(slices):
        out_branch[m, 0] = branch[:, m * cols : (m + 1) * cols].astype(BF16)


def settle_kernel(counts, slices, sub, per_piece, table_ref, *refs):
    pieces, out, buf, sems, out_sems = refs[:-4], refs[-4], refs[-3], refs[-2], refs[-1]
    column = table_ref[sum(counts)]
    loads, stores = [], []
    arrays = max(ref for ref, _ in per_piece) + 1
    first = 0
    for c, count in enumerate(counts):
        for k in range(slices):
            ref, where = per_piece[k]
            start = pl.multiple_of(lax.bitwise_xor(jnp.int32(k), column) * sub, sub)
            for t in range(count):
                at = len(loads)
                loads.append(
                    pltpu.make_async_copy(
                        pieces[c * arrays + ref].at[where, t], buf.at[at], sems.at[at]
                    )
                )
                stores.append(
                    pltpu.make_async_copy(
                        buf.at[at],
                        out.at[table_ref[first + t], pl.ds(start, sub)],
                        out_sems.at[at],
                    )
                )
        first += count
    for copy in loads:
        copy.start()
    for load, store in zip(loads, stores):
        load.wait()
        store.start()
    for copy in stores:
        copy.wait()


def exchange_x(array):
    n = array.shape[0]
    return lax.ppermute(array[1::2], "seq", [(i, i ^ 1) for i in range(n)])


def exchange_z(array, got, steps=None):
    n = array.shape[0]
    return [
        lax.ppermute(jnp.stack([array[k], got[k // 2]]), "seq", [(i, i ^ k) for i in range(n)])
        for k in (range(2, n, 2) if steps is None else steps)
    ]


def exchanged(array, got, gots):
    return jnp.concatenate([array[:1], got[:1], *gots], axis=0)


def take(array, index):
    return jnp.take(array, index, axis=0, mode="clip")


def on_device_pairs(
    tokens,
    lengths,
    counts,
    norm_gain,
    norm_bias,
    head_weight,
    merge_weight,
    up_weight,
    up_bias,
    down_weight,
    down_bias,
    cotangent,
):
    packs, shard, width = tokens.shape
    n = lax.axis_size("seq")
    slices = lax.axis_size("mlp")
    pack_len = shard * n
    rank = lax.axis_index("seq").astype(jnp.int32)
    column = lax.axis_index("mlp").astype(jnp.int32)
    heads = merge_weight.shape[0] // HD
    joined = heads * HD
    half = heads // 2
    cols = width // slices
    sub = shard // slices
    seq_masks, mlp_masks = masks_of(n), masks_of(slices)
    pairs = n // 2

    cot = lax.all_gather(cotangent, "mlp", axis=2, tiled=True)

    first, position, cost = layout(lengths, counts, pack_len)
    ids = jnp.arange(packs, dtype=jnp.int32)
    before = (cost[None, :] > cost[:, None]) | (
        (cost[None, :] == cost[:, None]) & (ids[None, :] < ids[:, None])
    )
    order = jnp.sum(before.astype(jnp.int32), axis=1)
    by_order = jnp.sum(
        jnp.where(order[None, :] == ids[:, None], ids[None, :], 0), axis=-1
    ).astype(jnp.int32)
    devices = jnp.arange(n, dtype=jnp.int32)
    shared_of = by_order[:pairs]
    own_of = by_order[pairs + 2 * (pairs - 1 - devices // 2) + devices % 2]
    late = order - pairs
    pair_of = jnp.where(late < 0, order, pairs - 1 - late // 2)
    device_of = 2 * pair_of + jnp.where(late < 0, 0, late % 2)
    dest = jnp.bitwise_xor(rank, devices)
    own_dest, shared_dest = own_of[dest], shared_of[dest // 2]
    me = jnp.stack([rank, column])

    token_cols = lax.dynamic_slice_in_dim(tokens, column * cols, cols, 2)
    head_ids = jnp.arange(heads, dtype=jnp.int32)
    half_ids = jnp.arange(half, dtype=jnp.int32)
    units_out = jnp.concatenate(
        [
            own_dest[:, None] * heads + head_ids[None, :],
            shared_dest[:, None] * heads + (dest % 2)[:, None] * half + half_ids[None, :],
        ],
        axis=1,
    ).reshape(-1)
    is_shared = (order < pairs)[:, None]
    holder = device_of[:, None] + jnp.where(is_shared, head_ids[None, :] // half, 0)
    units_in = (
        jnp.bitwise_xor(holder, rank) * (heads + half)
        + jnp.where(is_shared, heads + head_ids[None, :] % half, head_ids[None, :])
    ).reshape(-1)

    def tables(pack):
        freq = 10000.0 ** (-(2.0 * jnp.arange(ROT // 2, dtype=F32)) / ROT)
        angle = take(position, pack).astype(F32)[None, :] * jnp.repeat(freq, 2)[:, None]
        return jnp.cos(angle), jnp.sin(angle)

    w_heads = jnp.transpose(head_weight, (0, 2, 1)).reshape(3, heads, HD, width)
    w_own = w_heads.reshape(3 * joined, width)
    part_at = (rank % 2) * half
    w_shared = lax.dynamic_slice_in_dim(w_heads, part_at, half, 1).reshape(3 * half * HD, width)
    packs_here = (own_of[rank], shared_of[rank // 2])
    turns = [tables(p) for p in packs_here]
    firsts = [take(first, p).reshape(n, shard) for p in packs_here]
    lows = [(f[:, 0] // shard).astype(jnp.int32) for f in firsts]
    gain, bias = norm_gain.reshape(1, width), norm_bias.reshape(1, width)

    def whole2(s, *_):
        return (0, 0)

    def lane_at(s, *_):
        return (0, s)

    def project(rows, weight, cosine, sine):
        h = weight.shape[0] // (3 * HD)
        return pl.pallas_call(
            functools.partial(qkv_kernel, h),
            grid_spec=pltpu.PrefetchScalarGridSpec(
                num_scalar_prefetch=1,
                grid=(n,),
                in_specs=[
                    pl.BlockSpec(
                        (1, shard, width), lambda s, me: (lax.bitwise_xor(s, me[0]), 0, 0)
                    ),
                    pl.BlockSpec(weight.shape, whole2),
                    pl.BlockSpec((ROT, shard), lane_at),
                    pl.BlockSpec((ROT, shard), lane_at),
                ],
                out_specs=[
                    pl.BlockSpec((shard, width), lambda s, *_: (s, 0)),
                    pl.BlockSpec((h, 3, HD, shard), lambda s, *_: (0, 0, 0, s)),
                ],
            ),
            out_shape=[
                jax.ShapeDtypeStruct((pack_len, width), BF16),
                jax.ShapeDtypeStruct((h, 3, HD, pack_len), BF16),
            ],
            compiler_params=params(),
            cost_estimate=COST,
            name="project",
        )(me, rows, weight, cosine, sine)

    wide = [pltpu.VMEM((2, n, HD, shard), BF16)]
    tall = [pltpu.VMEM((2, n, shard, HD), BF16)]
    keep_spec = pl.BlockSpec((2, n, HD, shard), lambda u, *_: (u, 0, 0, 0))
    log_spec = pl.BlockSpec((2, n, shard), lambda u, *_: (u, 0, 0))
    unit_spec = pl.BlockSpec((2, 3, HD, pack_len), lambda u, *_: (u, 0, 0, 0))

    def attend(c, qkv):
        h = qkv.shape[0]
        return pl.pallas_call(
            functools.partial(unit_kernel, n, shard),
            grid_spec=pltpu.PrefetchScalarGridSpec(
                num_scalar_prefetch=2,
                grid=(h // 2,),
                in_specs=[pl.BlockSpec((n, shard), whole2), unit_spec],
                out_specs=[
                    pl.BlockSpec((n, 2, HD, shard), lambda u, *_: (0, u, 0, 0)),
                    keep_spec,
                    log_spec,
                ],
                scratch_shapes=wide * 2 + tall,
            ),
            out_shape=[
                jax.ShapeDtypeStruct((n, h, HD, shard), BF16),
                jax.ShapeDtypeStruct((h, n, HD, shard), BF16),
                jax.ShapeDtypeStruct((h, n, shard), F32),
            ],
            compiler_params=params(),
            cost_estimate=COST,
            name="attend",
        )(me, lows[c], firsts[c], qkv)

    def attend_back(c, kept, logsum, qkv, grads):
        h = qkv.shape[0]
        skip = c * heads // 2
        return pl.pallas_call(
            functools.partial(unit_back_kernel, n, shard),
            grid_spec=pltpu.PrefetchScalarGridSpec(
                num_scalar_prefetch=2,
                grid=(h // 2,),
                in_specs=[
                    pl.BlockSpec((n, shard), whole2),
                    keep_spec,
                    log_spec,
                    unit_spec,
                    pl.BlockSpec((n, 2, HD, shard), lambda u, *_: (0, u + skip, 0, 0)),
                ],
                out_specs=unit_spec,
                scratch_shapes=wide * 3
                + tall * 4
                + [pltpu.VMEM((2, n, shard, HD), F32)] * 2
                + [pltpu.VMEM((2, n, HD, shard), BF16)],
            ),
            out_shape=jax.ShapeDtypeStruct((h, 3, HD, pack_len), BF16),
            compiler_params=params(),
            cost_estimate=COST,
            name="attend_back",
        )(me, lows[c], firsts[c], kept, logsum, qkv, grads)

    def rows_back(grads, normed, weight, cosine, sine):
        h = grads.shape[0]
        return pl.pallas_call(
            functools.partial(rows_kernel, h, slices),
            grid_spec=pltpu.PrefetchScalarGridSpec(
                num_scalar_prefetch=1,
                grid=(n,),
                in_specs=[
                    pl.BlockSpec((h, 3, HD, shard), lambda s, *_: (0, 0, 0, s)),
                    pl.BlockSpec((shard, width), lambda s, *_: (s, 0)),
                    pl.BlockSpec(weight.shape, whole2),
                    pl.BlockSpec((ROT, shard), lane_at),
                    pl.BlockSpec((ROT, shard), lane_at),
                ],
                out_specs=[
                    pl.BlockSpec(
                        (slices, 1, sub, width),
                        lambda s, me: (0, lax.bitwise_xor(s, me[0]), 0, 0),
                    ),
                    pl.BlockSpec(weight.shape, whole2),
                ],
            ),
            out_shape=[
                jax.ShapeDtypeStruct((slices, n, sub, width), BF16),
                jax.ShapeDtypeStruct(weight.shape, F32),
            ],
            compiler_params=params(),
            cost_estimate=COST,
            name="rows_back",
        )(me, grads, normed, weight, cosine, sine)

    pack_spec = pl.BlockSpec((1, shard, width), lambda p: (p, 0, 0))
    normed_low = pl.pallas_call(
        norm_kernel,
        grid=(packs,),
        in_specs=[pack_spec, pl.BlockSpec((1, width), whole2), pl.BlockSpec((1, width), whole2)],
        out_specs=pack_spec,
        out_shape=jax.ShapeDtypeStruct((packs, shard, width), BF16),
        compiler_params=params(),
        cost_estimate=COST,
        name="norm",
    )(tokens, gain, bias)
    normed_cols = lax.dynamic_slice_in_dim(normed_low, column * cols, cols, 2)
    send_own = take(normed_cols, own_dest)
    send_shared = take(normed_cols, shared_dest)
    own_x = exchange_x(send_own)

    hidden = (
        jnp.einsum("psd,df->psf", normed_low, up_weight, preferred_element_type=F32) + up_bias
    )
    own_x, hidden, send_own, send_shared = tie(own_x, hidden, send_own, send_shared)

    own_z = exchange_z(send_own, own_x, [2])
    shared_x = exchange_x(send_shared)
    active_low = jax.nn.gelu(hidden, approximate=True).astype(BF16)
    branch_ff = jnp.einsum(
        "psf,fd->psd", active_low, down_weight, preferred_element_type=F32
    ).astype(BF16)
    own_z, shared_x, branch_ff, send_own, own_x, merge_here, down_here, turns, w_own, w_shared = tie(
        own_z,
        shared_x,
        branch_ff,
        send_own,
        own_x,
        merge_weight,
        down_weight,
        turns,
        w_own,
        w_shared,
    )

    own_z += exchange_z(send_own, own_x, range(4, n, 2))
    active_grad = jnp.einsum("psd,fd->psf", cot, down_here, preferred_element_type=F32)
    _, gelu_back = jax.vjp(lambda values: jax.nn.gelu(values, approximate=True), hidden)
    hidden_grad = gelu_back(active_grad)[0].astype(BF16)
    own_z, hidden_grad, send_shared, shared_x = tie(own_z, hidden_grad, send_shared, shared_x)
    rows_own = lax.all_gather(exchanged(send_own, own_x, own_z), "mlp", axis=2, tiled=True)

    shared_z = exchange_z(send_shared, shared_x)
    out_grad = jnp.einsum("hd,psd->phs", merge_here, cot, preferred_element_type=F32).astype(BF16)
    send_grad = take(out_grad.reshape(packs * heads, HD, shard), units_out).reshape(
        n, heads + half, HD, shard
    )
    up_grad = jnp.einsum(
        "psd,psf->df", normed_low, hidden_grad, preferred_element_type=F32
    ).astype(BF16)
    down_grad = jnp.einsum("psd,psf->df", cot, active_low, preferred_element_type=F32).astype(BF16)
    shared_z, send_grad, up_grad, down_grad, send_shared, shared_x, hidden_grad = tie(
        shared_z, send_grad, up_grad, down_grad, send_shared, shared_x, hidden_grad
    )
    rows_shared = lax.all_gather(
        exchanged(send_shared, shared_x, shared_z), "mlp", axis=2, tiled=True
    )

    grad_x = exchange_x(send_grad)
    low_ff = jnp.einsum(
        "psf,df->psd", hidden_grad, up_weight, preferred_element_type=F32
    ).astype(BF16)
    low_ff = jnp.transpose(low_ff.reshape(packs, slices, sub, width), (1, 0, 2, 3)).reshape(
        slices * packs * sub, width
    )
    biases = jnp.sum(hidden_grad.astype(F32), axis=(0, 1)), jnp.sum(cot.astype(F32), axis=(0, 1))
    grad_x, send_grad, low_ff, rows_own, biases = tie(grad_x, send_grad, low_ff, rows_own, biases)
    low_ff = lax.psum_scatter(low_ff, "mlp", scatter_dimension=0, tiled=True).reshape(
        packs, sub, width
    )

    grad_z = exchange_z(send_grad, grad_x)
    normed_own, qkv_own = project(rows_own, w_own, *turns[0])
    out_own, kept_own, log_own = attend(0, qkv_own)
    grad_z, out_own, kept_own, log_own, rows_shared = tie(
        grad_z, out_own, kept_own, log_own, rows_shared
    )
    grads = exchanged(send_grad, grad_x, grad_z)

    def with_row(*parts):
        weight = jnp.concatenate(parts[:2], axis=1)
        row = jnp.concatenate(parts[2:])
        row = jnp.pad(row, (0, weight.shape[1] - row.shape[0])).reshape(1, -1)
        row = jnp.broadcast_to(row, (16, weight.shape[1])).astype(BF16)
        return jnp.concatenate([weight, row], axis=0)

    terms = dict(
        enumerate(
            with_row(*parts)
            for parts in zip(*[cut(v, 0, n, rank) for v in (up_grad, down_grad, *biases)])
        )
    )
    terms_got = cube_send(terms, "seq", n, seq_masks)
    normed_shared, qkv_shared = project(rows_shared, w_shared, *turns[1])
    out_shared, kept_shared, log_shared = attend(1, qkv_shared)
    out_shared, kept_shared, log_shared, grads = tie(out_shared, kept_shared, log_shared, grads)

    send_out = jnp.concatenate([out_own, out_shared], axis=1)
    out_x = exchange_x(send_out)
    back_own = attend_back(0, kept_own, log_own, qkv_own, grads)
    out_x, back_own, terms_got, send_out = tie(out_x, back_own, terms_got, send_out)

    terms = cube_add(terms, terms_got, seq_masks, BF16)
    terms_got = cube_send(terms, "seq", n, seq_masks[1:])
    out_z = exchange_z(send_out, out_x)
    low_own, head_own = rows_back(back_own, normed_own, w_own, *turns[0])
    back_shared = attend_back(1, kept_shared, log_shared, qkv_shared, grads)
    out_z, terms_got, low_own, back_shared, send_out, out_x = tie(
        out_z, terms_got, low_own, back_shared, send_out, out_x
    )

    low_own = cube_sum([low_own[k] for k in range(slices)], "mlp", mlp_masks, BF16).astype(BF16)
    for step in range(1, len(seq_masks)):
        last_step = step == len(seq_masks) - 1
        terms = cube_add(terms, terms_got, seq_masks[step:], F32 if last_step else BF16)
        if not last_step:
            terms_got = cube_send(terms, "seq", n, seq_masks[step + 1 :])
    terms = terms[0]
    low_shared, head_shared = rows_back(back_shared, normed_shared, w_shared, *turns[1])
    attended = take(
        exchanged(send_out, out_x, out_z).reshape(n * (heads + half), HD, shard), units_in
    ).reshape(packs, joined, shard)
    branch, merge_part = pl.pallas_call(
        functools.partial(join_kernel, slices),
        grid=(packs,),
        in_specs=[
            pl.BlockSpec((1, joined, shard), lambda p: (p, 0, 0)),
            pl.BlockSpec((1, shard, width), lambda p: (p, 0, 0)),
            pl.BlockSpec((joined, width), whole2),
            pl.BlockSpec((1, shard, width), lambda p: (p, 0, 0)),
        ],
        out_specs=[
            pl.BlockSpec((slices, 1, shard, cols), lambda p: (0, p, 0, 0)),
            pl.BlockSpec((joined, width), whole2),
        ],
        out_shape=[
            jax.ShapeDtypeStruct((slices, packs, shard, cols), BF16),
            jax.ShapeDtypeStruct((joined, width), F32),
        ],
        compiler_params=params(),
        cost_estimate=COST,
        name="join",
    )(attended, cot, merge_weight, branch_ff)
    low_terms = {k: low_shared[k] for k in range(slices)}
    low_got = cube_send(low_terms, "mlp", slices, mlp_masks)
    low_terms, low_got, low_own, branch, terms, low_ff, head_shared = tie(
        low_terms, low_got, low_own, branch, terms, low_ff, head_shared
    )

    summed = lax.psum_scatter(branch, "mlp", scatter_dimension=0, tiled=False)

    low_own_x = exchange_x(low_own)
    for step in range(len(mlp_masks)):
        low_terms = cube_add(low_terms, low_got, mlp_masks[step:], BF16)
        if step < len(mlp_masks) - 1:
            low_got = cube_send(low_terms, "mlp", slices, mlp_masks[step + 1 :])
    low_shared = low_terms[0]
    head_all = head_own.reshape(3, heads, HD, width)
    there = lax.dynamic_slice_in_dim(head_all, part_at, half, 1)
    head_all = lax.dynamic_update_slice_in_dim(
        head_all, there + head_shared.reshape(3, half, HD, width), part_at, 1
    ).reshape(3 * joined, width)
    weights = jnp.concatenate([head_all, merge_part], axis=0).astype(BF16)
    weights = dict(enumerate(cut(weights, 1, n, rank)))
    low_own_z = exchange_z(low_own, low_own_x)
    weights_got = cube_send(weights, "seq", n, seq_masks)
    low_own_z, low_shared, low_own, low_own_x, weights, weights_got = tie(
        low_own_z, low_shared, low_own, low_own_x, weights, weights_got
    )

    low_shared_x = exchange_x(low_shared)
    weights = cube_add(weights, weights_got, seq_masks, BF16)
    weights_got = cube_send(weights, "seq", n, seq_masks[1:])

    def finish(lows, index, which):
        count = which.shape[0]
        row_spec = pl.BlockSpec((1, sub, width), lambda t, at: (at[count + t], at[0], 0))

        def part(i):
            return pl.BlockSpec(
                (1, sub, width), lambda t, at: (at[(2 + i) * count + t], 0, 0)
            )

        table = [jnp.full((count,), column), which, *index]
        return pl.pallas_call(
            functools.partial(finish_kernel, len(lows)),
            grid_spec=pltpu.PrefetchScalarGridSpec(
                num_scalar_prefetch=1,
                grid=(count,),
                in_specs=[part(i) for i in range(len(lows))]
                + [
                    pl.BlockSpec((1, sub, width), lambda t, at: (at[count + t], 0, 0)),
                    row_spec,
                    row_spec,
                    pl.BlockSpec((1, width), whole2),
                ],
                out_specs=[
                    pl.BlockSpec((1, sub, width), lambda t, *_: (t, 0, 0)),
                    pl.BlockSpec((2, width), whole2),
                ],
            ),
            out_shape=[
                jax.ShapeDtypeStruct((count, sub, width), BF16),
                jax.ShapeDtypeStruct((2, width), F32),
            ],
            compiler_params=params(),
            cost_estimate=COST,
            name="finish",
        )(jnp.concatenate(table), *lows, low_ff, tokens, cot, gain)

    row_own, sums_own = finish(
        [exchanged(low_own, low_own_x, low_own_z)], [devices], own_dest
    )
    low_shared_x, row_own, sums_own, low_shared, weights_got = tie(
        low_shared_x, row_own, sums_own, low_shared, weights_got
    )
    for step in range(1, len(seq_masks)):
        last_step = step == len(seq_masks) - 1
        weights = cube_add(weights, weights_got, seq_masks[step:], F32 if last_step else BF16)
        if not last_step:
            weights_got = cube_send(weights, "seq", n, seq_masks[step + 1 :])
    weights = weights[0]
    low_shared_z = exchange_z(low_shared, low_shared_x)
    pieces = gather_step([row_own[None]], "mlp", slices, mlp_masks[-1])
    low_shared_z, pieces, weights = tie(low_shared_z, pieces, weights)

    for m in reversed(mlp_masks[:-1]):
        pieces = gather_step(pieces, "mlp", slices, m)
    both = exchanged(low_shared, low_shared_x, low_shared_z)
    even = jnp.bitwise_xor(2 * jnp.arange(pairs, dtype=jnp.int32), rank)
    row_shared, sums = finish([both, both], [even, jnp.bitwise_xor(even, 1)], shared_of)
    last = gather_step([row_shared[None]], "mlp", slices, mlp_masks[-1])
    vectors = small_sum(sums_own + sums, n, slices)
    result = (
        token_cols.astype(F32)
        + summed.astype(F32)
        + lax.dynamic_slice_in_dim(down_bias, column * cols, cols, 0)
    ).astype(BF16)
    last, pieces, vectors, result = tie(last, pieces, vectors, result)

    for m in reversed(mlp_masks[:-1]):
        last = gather_step(last, "mlp", slices, m)
    pieces += last
    where = [(0, 0)]
    lookup = [0]
    for i, m in enumerate(reversed(mlp_masks)):
        where += [(i + 1, j) for j in range(len(lookup))]
        lookup += [k ^ m for k in lookup]
    per_piece = [where[lookup.index(k)] for k in range(slices)]
    tokens_grad = pl.pallas_call(
        functools.partial(settle_kernel, (n, pairs), slices, sub, per_piece),
        grid_spec=pltpu.PrefetchScalarGridSpec(
            num_scalar_prefetch=1,
            grid=(1,),
            in_specs=[pl.BlockSpec(memory_space=pl.ANY)] * len(pieces),
            out_specs=pl.BlockSpec(memory_space=pl.ANY),
            scratch_shapes=[
                pltpu.VMEM((packs * slices, sub, width), BF16),
                pltpu.SemaphoreType.DMA((packs * slices,)),
                pltpu.SemaphoreType.DMA((packs * slices,)),
            ],
        ),
        out_shape=jax.ShapeDtypeStruct((packs, shard, width), BF16),
        compiler_params=params(),
        name="settle",
    )(jnp.concatenate([own_dest, shared_of, column.reshape(1)]), *pieces)

    part, hidden_here = width // n, up_weight.shape[1]
    return (
        result,
        tokens_grad,
        vectors[0],
        vectors[1],
        jnp.transpose(weights[: 3 * joined].reshape(3, joined, part), (0, 2, 1)),
        weights[3 * joined :],
        terms[:part, :hidden_here],
        terms[part, : hidden_here // n],
        terms[:part, hidden_here:].T,
        terms[part, hidden_here // n : hidden_here // n + part],
    )


def solution(mesh):
    in_specs = (
        P(None, "seq", None),
        P(),
        P(),
        P(),
        P(),
        P(None, None, "mlp"),
        P("mlp", None),
        P(None, "mlp"),
        P("mlp"),
        P("mlp", None),
        P(),
        P(None, "seq", "mlp"),
    )
    out_specs = (
        P(None, "seq", "mlp"),
        P(None, "seq", None),
        P("seq"),
        P("seq"),
        P(None, "seq", "mlp"),
        P("mlp", "seq"),
        P("seq", "mlp"),
        P(("mlp", "seq")),
        P("mlp", "seq"),
        P("seq"),
    )
    n, slices = mesh.shape["seq"], mesh.shape["mlp"]

    def plan(*args):
        packs, pack_len, _ = args[0].shape
        heads = args[6].shape[0] // HD // slices
        pairs = (
            2 * packs == 3 * n
            and n >= 4
            and heads % 4 == 0
            and (pack_len // n) % 128 == 0
            and (pack_len // n) % (16 * slices) == 0
        )
        return jax.shard_map(
            on_device_pairs if pairs else on_device,
            mesh=mesh,
            in_specs=in_specs,
            out_specs=out_specs,
            check_vma=False,
        )(*args)

    return plan
```

profile of v0, /device:TPU:17, one launch (start us, length us, event | category | flops | bytes accessed | tf_op | source)
XLA Modules:
  0.0 549.4 jit_solution(13066489264100781491)
XLA Ops:
  10.9 11.4 %norm.1 = bf16[12,256,1024]{2,1,0:T(8,128)(2,1)} custom-call(bf16[12,256,1024]{2,1,0:T(8,128)(2,1)} %refs_3_.1, f32[1,1024]{1,0:T(1,128)} %bitcast.208, f32[1,1024]{1,0:T(1,128)} %bitcast.213), custom_call_target="tpu_custom_call" | custom-call | flops 1048576 | bytes 1048576 | tf_op jit(solution)/shard_map/norm/pallas_call | solution.py:1440
  22.4 2.7 constant_dynamic-slice_fusion.21
  31.3 2.6 copy.45
  38.2 12.7 %broadcast_add_fusion = f32[12,256,1024]{2,1,0:T(8,128)} fusion(f32[1024]{0:T(1024)S(1)} %copy-done.50, bf16[12,256,1024]{2,1,0:T(8,128)(2,1)} %norm.1, bf16[1024,1024]{1,0:T(8,128)(2,1)S(1)} %copy-done.48), kind=kOutput, calls=%fused_computation.24 | convolution fusion | flops 6445596672 | bytes 20975616 | tf_op jit(solution)/shard_map/psd,df->psf/dot_general | solution.py:1456
  53.1 2.8 multiply_sine_fusion
  58.3 12.8 %convolution_convert_fusion.1.branch_ref = bf16[12,256,1024]{2,1,0:T(8,128)(2,1)} fusion(bf16[1024,1024]{1,0:T(8,128)(2,1)S(1)} %copy-done, f32[12,256,1024]{2,1,0:T(8,128)} %broadcast_add_fusion), kind=kOutput, calls=%fused_computation.36 | convolution fusion | flops 6473908224 | bytes 20971520 | tf_op jit(solution)/shard_map/psf,fd->psd/dot_general | solution.py:1463
  76.5 28.1 %fusion.6 = bf16[12,256,1024]{2,1,0:T(8,128)(2,1)} fusion(f32[12,256,1024]{2,1,0:T(8,128)} %broadcast_add_fusion, bf16[12,256,1024]{2,1,0:T(8,128)(2,1)} %all-gather.4.cloned.1.call-done.c_ref.refs_3_.refs_4_, bf16[1024,1024]{1,0:T(8,128)(2,1)S(1)} %copy-done), kind=kOutput, calls=%fused_computation.15 | convolution fusion | flops 6505365504 | bytes 27262976 | tf_op jit(solution)/shard_map/psd,fd->psf/dot_general | solution.py:1480
  114.7 11.7 %bitcast_convert_fusion.1 = bf16[1024,1024]{1,0:T(8,128)(2,1)} fusion(bf16[12,256,1024]{2,1,0:T(8,128)(2,1)} %norm.1, bf16[12,256,1024]{2,1,0:T(8,128)(2,1)} %fusion.6), kind=kOutput, calls=%fused_computation.34 | convolution fusion | flops 6443499520 | bytes 14680064 | tf_op jit(solution)/shard_map/psd,psf->df/dot_general | solution.py:1491
  126.4 11.0 %fusion.19 = bf16[1024,1024]{1,0:T(8,128)(2,1)} fusion(bf16[12,256,1024]{2,1,0:T(8,128)(2,1)S(1)} %bitcast.176, f32[12,256,1024]{2,1,0:T(8,128)} %broadcast_add_fusion), kind=kOutput, calls=%fused_computation.66 | convolution fusion | flops 6471811072 | bytes 20971520 | tf_op jit(solution)/shard_map/psd,psf->df/dot_general | solution.py:1494
  137.4 3.0 convolution_convert_fusion.2
  148.1 3.9 convert_reduce_fusion
  153.5 10.0 %convolution_convert_fusion = bf16[12,256,1024]{2,1,0:T(8,128)(2,1)S(1)} fusion(bf16[12,256,1024]{2,1,0:T(8,128)(2,1)} %fusion.6, bf16[1024,1024]{1,0:T(8,128)(2,1)S(1)} %copy-done.49), kind=kOutput, calls=%fused_computation.35 | convolution fusion | flops 6445596672 | bytes 14680064 | tf_op jit(solution)/shard_map/psf,df->psd/dot_general | solution.py:1503
  163.5 3.3 copy.50
  170.5 2.6 constant_dynamic-slice_fusion.5
  185.5 11.1 %project.2 = (bf16[2048,1024]{1,0:T(8,128)(2,1)}, bf16[4,3,64,2048]{3,2,1,0:T(8,128)(2,1)}) custom-call(s32[2]{0:T(128)} %pad_add_fusion.2.me_ref, bf16[8,256,1024]{2,1,0:T(8,128)(2,1)} %all-gather.6.cloned.1.call-done.x_ref, bf16[768,1024]{1,0:T(8,128)(2,1)} %bitcast.179, f32[32,2048]{1,0:T(8,128)} %get-tuple-element.150.cos_ref, ...), custom_call_target="tpu_custom_call" | custom-call | flops 1048576 | bytes 1048576 | tf_op jit(solution)/shard_map/project/pallas_call | solution.py:1323
  196.6 22.6 %attend.2 = (bf16[8,4,64,256]{3,2,1,0:T(8,128)(2,1)}, bf16[4,8,64,256]{3,2,1,0:T(8,128)(2,1)}, f32[4,8,256]{2,1,0:T(8,128)}) custom-call(s32[2]{0:T(128)} %pad_add_fusion.2.me_ref, s32[8]{0:T(128)} %get-tuple-element.433.low_ref, s32[8,256]{1,0:T(8,128)} %copy-done.44, bf16[4,3,64,2048]{3,2,1,0:T(8,128)(2,1)} %get-tuple-element.152.qkv_ref), custom_call_target="tpu_custom_call" | custom-call | flops 1048576 | bytes 1048576 | tf_op jit(solution)/shard_map/attend/pallas_call | solution.py:1358
  219.3 10.1 %project.3 = (bf16[2048,1024]{1,0:T(8,128)(2,1)}, bf16[2,3,64,2048]{3,2,1,0:T(8,128)(2,1)}) custom-call(s32[2]{0:T(128)} %pad_add_fusion.2.me_ref, bf16[8,256,1024]{2,1,0:T(8,128)(2,1)} %all-gather.8.cloned.1.call-done.x_ref, bf16[384,1024]{1,0:T(8,128)(2,1)} %bitcast.184, f32[32,2048]{1,0:T(8,128)} %get-tuple-element.164.cos_ref, ...), custom_call_target="tpu_custom_call" | custom-call | flops 1048576 | bytes 1048576 | tf_op jit(solution)/shard_map/project/pallas_call | solution.py:1323
  229.4 14.6 %attend.3 = (bf16[8,2,64,256]{3,2,1,0:T(8,128)(2,1)}, bf16[2,8,64,256]{3,2,1,0:T(8,128)(2,1)}, f32[2,8,256]{2,1,0:T(8,128)}) custom-call(s32[2]{0:T(128)} %pad_add_fusion.2.me_ref, s32[8]{0:T(128)} %get-tuple-element.432.low_ref, s32[8,256]{1,0:T(8,128)} %copy-done.43, bf16[2,3,64,2048]{3,2,1,0:T(8,128)(2,1)} %get-tuple-element.166.qkv_ref), custom_call_target="tpu_custom_call" | custom-call | flops 1048576 | bytes 1048576 | tf_op jit(solution)/shard_map/attend/pallas_call | solution.py:1358
  247.4 30.2 %attend_back.2.grad_ref = bf16[4,3,64,2048]{3,2,1,0:T(8,128)(2,1)} custom-call(s32[2]{0:T(128)} %pad_add_fusion.2.me_ref, s32[8]{0:T(128)} %get-tuple-element.433.low_ref, s32[8,256]{1,0:T(8,128)} %copy-done.44, bf16[4,8,64,256]{3,2,1,0:T(8,128)(2,1)} %get-tuple-element.174.keep_ref, f32[4,8,256]{2,1,0:T(8,128)} %get-tuple-element.175.logsum_ref, ...), custom_call_target="tpu_custom_call" | custom-call | flops 1048576 | bytes 1048576 | tf_op jit(solution)/shard_map/attend_back/pallas_call | solution.py:1384
  279.8 10.1 %collective-permute-start.17 = (bf16[2,144,2048]{2,1,0:T(8,128)(2,1)S(1)}, bf16[2,144,2048]{2,1,0:T(8,128)(2,1)S(1)}, u32[]{:S(2)}, u32[]{:S(2)}) collective-permute-start(bf16[2,144,2048]{2,1,0:T(8,128)(2,1)S(1)} %pad_maximum_fusion.4), channel_id=1, source_target_pairs={{0,8},{4,12},{8,0},{12,4},{16,24},{20,28},{24,16},{28,20},{1,9},{5... | collective-permute-start | bytes 3538952 | tf_op jit(solution)/shard_map/ppermute | solution.py:432
  290.2 2.7 collective-permute-start.16
  292.9 18.9 %attend_back.3.grad_ref = bf16[2,3,64,2048]{3,2,1,0:T(8,128)(2,1)} custom-call(s32[2]{0:T(128)} %pad_add_fusion.2.me_ref, s32[8]{0:T(128)} %get-tuple-element.432.low_ref, s32[8,256]{1,0:T(8,128)} %copy-done.43, bf16[2,8,64,256]{3,2,1,0:T(8,128)(2,1)} %get-tuple-element.187.keep_ref, f32[2,8,256]{2,1,0:T(8,128)} %get-tuple-element.188.logsum_ref, ...), custom_call_target="tpu_custom_call" | custom-call | flops 1048576 | bytes 1048576 | tf_op jit(solution)/shard_map/attend_back/pallas_call | solution.py:1384
  311.9 14.1 %rows_back.2 = (bf16[4,8,64,1024]{3,2,1,0:T(8,128)(2,1)}, f32[768,1024]{1,0:T(8,128)}) custom-call(s32[2]{0:T(128)} %pad_add_fusion.2.me_ref, bf16[4,3,64,2048]{3,2,1,0:T(8,128)(2,1)} %attend_back.2.grad_ref, bf16[2048,1024]{1,0:T(8,128)(2,1)} %get-tuple-element.185.normed_ref, bf16[768,1024]{1,0:T(8,128)(2,1)} %bitcast.180, ...), custom_call_target="tpu_custom_call" | custom-call | flops 1048576 | bytes 1048576 | tf_op jit(solution)/shard_map/rows_back/pallas_call | solution.py:1410
  325.9 12.1 %collective-permute-done.14 = bf16[2,6,64,256]{3,2,1,0:T(8,128)(2,1)S(1)} collective-permute-done((bf16[2,6,64,256]{3,2,1,0:T(8,128)(2,1)S(1)}, bf16[2,6,64,256]{3,2,1,0:T(8,128)(2,1)S(1)}, u32[]{:S(2)}, u32[]{:S(2)}) %collective-permute-start.14) | collective-permute-done | bytes 393248 | tf_op jit(solution)/shard_map/ppermute | solution.py:1221
  338.1 2.6 fusion.86
  342.2 3.3 collective-permute-start.19
  348.1 11.1 %rows_back.3 = (bf16[4,8,64,1024]{3,2,1,0:T(8,128)(2,1)}, f32[384,1024]{1,0:T(8,128)}) custom-call(s32[2]{0:T(128)} %pad_add_fusion.2.me_ref, bf16[2,3,64,2048]{3,2,1,0:T(8,128)(2,1)} %attend_back.3.grad_ref, bf16[2048,1024]{1,0:T(8,128)(2,1)} %get-tuple-element.190.normed_ref, bf16[384,1024]{1,0:T(8,128)(2,1)} %bitcast.185, ...), custom_call_target="tpu_custom_call" | custom-call | flops 1048576 | bytes 1048576 | tf_op jit(solution)/shard_map/rows_back/pallas_call | solution.py:1410
  359.1 4.2 fusion.87
  367.1 2.5 collective-permute-start.21
  371.2 3.0 add_convert_fusion.1
  379.1 3.4 gather_fusion.6
  382.4 13.9 %join.1 = (bf16[4,12,256,256]{3,2,1,0:T(8,128)(2,1)}, f32[256,1024]{1,0:T(8,128)}) custom-call(bf16[12,256,256]{2,1,0:T(8,128)(2,1)} %bitcast.189, bf16[12,256,1024]{2,1,0:T(8,128)(2,1)} %all-gather.4.cloned.1.call-done.c_ref.refs_3_.refs_4_, bf16[256,1024]{1,0:T(8,128)(2,1)} %merge_ref.1, bf16[12,256,1024]{2,1,0:T(8,128)(2,1)} %convolution_convert_fusion.1.branch_ref), custom_call_target="tpu_custom_call" | custom-call | flops 1048576 | bytes 1048576 | tf_op jit(solution)/shard_map/join/pallas_call | solution.py:1566
  398.8 3.5 fusion.22
  405.6 2.9 add_dynamic-update-slice_fusion
  408.5 2.4 convert.103
  414.6 7.7 %collective-permute-done.22 = bf16[4,64,1024]{2,1,0:T(8,128)(2,1)S(1)} collective-permute-done((bf16[4,64,1024]{2,1,0:T(8,128)(2,1)S(1)}, bf16[4,64,1024]{2,1,0:T(8,128)(2,1)S(1)}, u32[]{:S(2)}, u32[]{:S(2)}) %collective-permute-start.22) | collective-permute-done | bytes 524320 | tf_op jit(solution)/shard_map/ppermute | solution.py:1215
  422.3 3.2 collective-permute-start.23
  427.8 18.7 %collective-permute-done.26 = bf16[1,8,64,1024]{3,2,1,0:T(8,128)(2,1)S(1)} collective-permute-done((bf16[1,8,64,1024]{3,2,1,0:T(8,128)(2,1)S(1)}, bf16[1,8,64,1024]{3,2,1,0:T(8,128)(2,1)S(1)}, u32[]{:S(2)}, u32[]{:S(2)}) %collective-permute-start.26) | collective-permute-done | bytes 1048608 | tf_op jit(solution)/shard_map/ppermute | solution.py:432
  449.1 2.8 collective-permute-start.29
  453.1 7.7 %finish.2 = (bf16[8,64,1024]{2,1,0:T(8,128)(2,1)}, f32[2,1024]{1,0:T(2,128)}) custom-call(s32[24]{0:T(128)} %pad_add_fusion.3.which_ref, bf16[8,64,1024]{2,1,0:T(8,128)(2,1)} %copy-done.22, bf16[12,64,1024]{2,1,0:T(8,128)(2,1)} %bitcast.192, bf16[12,256,1024]{2,1,0:T(8,128)(2,1)} %refs_3_.1, ...), custom_call_target="tpu_custom_call" | custom-call | flops 1048576 | bytes 1048576 | tf_op jit(solution)/shard_map/finish/pallas_call | solution.py:1628
  462.0 4.1 collective-permute-start.34
  470.6 3.7 collective-permute-done.34
  475.3 17.9 %collective-permute-done.31 = bf16[2,64,1024]{2,1,0:T(8,128)(2,1)S(1)} collective-permute-done((bf16[2,64,1024]{2,1,0:T(8,128)(2,1)S(1)}, bf16[2,64,1024]{2,1,0:T(8,128)(2,1)S(1)}, u32[]{:S(2)}, u32[]{:S(2)}) %collective-permute-start.31) | collective-permute-done | bytes 262176 | tf_op jit(solution)/shard_map/ppermute | solution.py:1221
  493.1 6.5 %collective-permute-done.32 = bf16[2,64,1024]{2,1,0:T(8,128)(2,1)S(1)} collective-permute-done((bf16[2,64,1024]{2,1,0:T(8,128)(2,1)S(1)}, bf16[2,64,1024]{2,1,0:T(8,128)(2,1)S(1)}, u32[]{:S(2)}, u32[]{:S(2)}) %collective-permute-start.32) | collective-permute-done | bytes 262176 | tf_op jit(solution)/shard_map/ppermute | solution.py:1221
  505.6 5.1 finish.3
  513.5 12.1 %small_sum.1 = f32[2,128]{1,0:T(2,128)} custom-call(f32[8,2,128]{2,1,0:T(2,128)} %add_bitcast_fusion.x_ref), custom_call_target="tpu_custom_call" | custom-call | flops 1048576 | bytes 1048576 | tf_op jit(solution)/shard_map/small_sum/pallas_call | solution.py:374
  525.6 3.5 fusion.11
  536.0 6.7 %settle.1 = bf16[12,256,1024]{2,1,0:T(8,128)(2,1)} custom-call(s32[13]{0:T(128)} %pad_add_fusion.4.table_ref, bf16[1,8,64,1024]{3,2,1,0:T(8,128)(2,1)} %bitcast.195, bf16[1,8,64,1024]{3,2,1,0:T(8,128)(2,1)} %copy-done.12, bf16[2,8,64,1024]{3,2,1,0:T(8,128)(2,1)} %collective-permute-done.36.refs_2_, bf16[1,4,64,1024]{3,2,1,0:T(8,128)(2,1)} %bitcast.198, ...), custom_call_target="tpu_custom_call" | custom-call | tf_op jit(solution)/shard_map/settle/pallas_call | solution.py:1693
  (372 shorter events, 116.8 us)
Async XLA Ops:
  7.2 51.2 %copy-start = (bf16[1024,1024]{1,0:T(8,128)(2,1)S(1)}, bf16[1024,1024]{1,0:T(8,128)(2,1)}, u32[]{:S(2)}) copy-start(bf16[1024,1024]{1,0:T(8,128)(2,1)} %param.21) | copy-start | bytes 6291460
  7.2 69.3 %all-gather.4.cloned.1.call-start = ((), (), s32[]{:S(2)}) async-start(), calls=%async_computation.2 | async-start | bytes 7864320 | tf_op jit(solution)/shard_map/all_gather | solution.py:1262
  7.9 160.1 %all-gather.6.cloned.1.call-start = ((), (), s32[]{:S(2)}) async-start(), calls=%async_computation.3 | async-start | bytes 5242880 | tf_op jit(solution)/shard_map/all_gather | solution.py:1484
  28.1 27.8 %collective-permute-start = (bf16[4,256,256]{2,1,0:T(8,128)(2,1)}, bf16[4,256,256]{2,1,0:T(8,128)(2,1)}, u32[]{:S(2)}, u32[]{:S(2)}) collective-permute-start(bf16[4,256,256]{2,1,0:T(8,128)(2,1)} %slice.271), channel_id=1, source_target_pairs={{0,4},{4,0},{8,12},{12,8},{16,20},{20,16},{24,28},{28,24},{1,5},{5... | collective-permute-start | bytes 1572872 | tf_op jit(solution)/shard_map/ppermute | solution.py:1215
  56.8 14.3 %collective-permute-start.1 = (bf16[2,256,256]{2,1,0:T(8,128)(2,1)S(1)}, bf16[2,256,256]{2,1,0:T(8,128)(2,1)S(1)}, u32[]{:S(2)}, u32[]{:S(2)}) collective-permute-start(bf16[2,256,256]{2,1,0:T(8,128)(2,1)S(1)} %pad_maximum_fusion.14), channel_id=1, source_target_pairs={{0,8},{4,12},{8,0},{12,4},{16,24},{20,28},{24,16},{28,20},{1,9},{5... | collective-permute-start | bytes 786440 | tf_op jit(solution)/shard_map/ppermute | solution.py:1221
  58.2 12.9 %collective-permute-start.2 = (bf16[4,256,256]{2,1,0:T(8,128)(2,1)S(1)}, bf16[4,256,256]{2,1,0:T(8,128)(2,1)S(1)}, u32[]{:S(2)}, u32[]{:S(2)}) collective-permute-start(bf16[4,256,256]{2,1,0:T(8,128)(2,1)S(1)} %slice.274), channel_id=1, source_target_pairs={{0,4},{4,0},{8,12},{12,8},{16,20},{20,16},{24,28},{28,24},{1,5},{5... | collective-permute-start | bytes 1572872 | tf_op jit(solution)/shard_map/ppermute | solution.py:1215
  74.4 30.2 %collective-permute-start.3 = (bf16[2,256,256]{2,1,0:T(8,128)(2,1)}, bf16[2,256,256]{2,1,0:T(8,128)(2,1)}, u32[]{:S(2)}, u32[]{:S(2)}) collective-permute-start(bf16[2,256,256]{2,1,0:T(8,128)(2,1)} %pad_maximum_fusion.15), channel_id=1, source_target_pairs={{0,16},{4,20},{8,24},{12,28},{16,0},{20,4},{24,8},{28,12},{1,17},{... | collective-permute-start | bytes 786440 | tf_op jit(solution)/shard_map/ppermute | solution.py:1221
  75.2 29.4 %collective-permute-start.4 = (bf16[2,256,256]{2,1,0:T(8,128)(2,1)}, bf16[2,256,256]{2,1,0:T(8,128)(2,1)}, u32[]{:S(2)}, u32[]{:S(2)}) collective-permute-start(bf16[2,256,256]{2,1,0:T(8,128)(2,1)} %pad_maximum_fusion.16), channel_id=1, source_target_pairs={{0,24},{4,28},{8,16},{12,20},{16,8},{20,12},{24,0},{28,4},{1,25},{... | collective-permute-start | bytes 786440 | tf_op jit(solution)/shard_map/ppermute | solution.py:1221
  108.7 110.5 %all-gather.8.cloned.1.call-start = ((), (), s32[]{:S(2)}) async-start(), calls=%async_computation.4 | async-start | bytes 5242880 | tf_op jit(solution)/shard_map/all_gather | solution.py:1498
  109.9 32.6 %collective-permute-start.5 = (bf16[2,256,256]{2,1,0:T(8,128)(2,1)}, bf16[2,256,256]{2,1,0:T(8,128)(2,1)S(1)}, u32[]{:S(2)}, u32[]{:S(2)}) collective-permute-start(bf16[2,256,256]{2,1,0:T(8,128)(2,1)} %pad_maximum_fusion.17), channel_id=1, source_target_pairs={{0,8},{4,12},{8,0},{12,4},{16,24},{20,28},{24,16},{28,20},{1,9},{5... | collective-permute-start | bytes 786440 | tf_op jit(solution)/shard_map/ppermute | solution.py:1221
  112.8 29.8 %collective-permute-start.6 = (bf16[2,256,256]{2,1,0:T(8,128)(2,1)}, bf16[2,256,256]{2,1,0:T(8,128)(2,1)}, u32[]{:S(2)}, u32[]{:S(2)}) collective-permute-start(bf16[2,256,256]{2,1,0:T(8,128)(2,1)} %pad_maximum_fusion.18), channel_id=1, source_target_pairs={{0,16},{4,20},{8,24},{12,28},{16,0},{20,4},{24,8},{28,12},{1,17},{... | collective-permute-start | bytes 786440 | tf_op jit(solution)/shard_map/ppermute | solution.py:1221
  113.5 29.0 %collective-permute-start.7 = (bf16[2,256,256]{2,1,0:T(8,128)(2,1)}, bf16[2,256,256]{2,1,0:T(8,128)(2,1)}, u32[]{:S(2)}, u32[]{:S(2)}) collective-permute-start(bf16[2,256,256]{2,1,0:T(8,128)(2,1)} %pad_maximum_fusion.19), channel_id=1, source_target_pairs={{0,24},{4,28},{8,16},{12,20},{16,8},{20,12},{24,0},{28,4},{1,25},{... | collective-permute-start | bytes 786440 | tf_op jit(solution)/shard_map/ppermute | solution.py:1221
  148.0 254.3 %reduce-scatter.3.cloned.1.call-start = ((), (), s32[]{:S(2)}) async-start(), calls=%async_computation.5 | async-start | bytes 7864320 | tf_op jit(solution)/shard_map/reduce_scatter | solution.py:1511
  152.1 15.9 %collective-permute-start.8 = (bf16[4,6,64,256]{3,2,1,0:T(8,128)(2,1)S(1)}, bf16[4,6,64,256]{3,2,1,0:T(8,128)(2,1)S(1)}, u32[]{:S(2)}, u32[]{:S(2)}) collective-permute-start(bf16[4,6,64,256]{3,2,1,0:T(8,128)(2,1)S(1)} %slice.286), channel_id=1, source_target_pairs={{0,4},{4,0},{8,12},{12,8},{16,20},{20,16},{24,28},{28,24},{1,5},{5... | collective-permute-start | bytes 2359304 | tf_op jit(solution)/shard_map/ppermute | solution.py:1215
  168.9 356.7 %reduce-scatter.5.cloned.1.call-start = ((), (), s32[]{:S(2)}) async-start(), calls=%async_computation.6 | async-start | bytes 7864320 | tf_op jit(solution)/shard_map/reduce_scatter | solution.py:1593
  176.9 100.7 %collective-permute-start.13 = (bf16[4,144,2048]{2,1,0:T(8,128)(2,1)}, bf16[4,144,2048]{2,1,0:T(8,128)(2,1)}, u32[]{:S(2)}, u32[]{:S(2)}) collective-permute-start(bf16[4,144,2048]{2,1,0:T(8,128)(2,1)} %pad_maximum_fusion), channel_id=1, source_target_pairs={{0,4},{4,0},{8,12},{12,8},{16,20},{20,16},{24,28},{28,24},{1,5},{5... | collective-permute-start | bytes 7077896 | tf_op jit(solution)/shard_map/ppermute | solution.py:432
  179.2 40.0 %collective-permute-start.9 = (bf16[2,6,64,256]{3,2,1,0:T(8,128)(2,1)}, bf16[2,6,64,256]{3,2,1,0:T(8,128)(2,1)}, u32[]{:S(2)}, u32[]{:S(2)}) collective-permute-start(bf16[2,6,64,256]{3,2,1,0:T(8,128)(2,1)} %pad_maximum_fusion.8), channel_id=1, source_target_pairs={{0,8},{4,12},{8,0},{12,4},{16,24},{20,28},{24,16},{28,20},{1,9},{5... | collective-permute-start | bytes 1179656 | tf_op jit(solution)/shard_map/ppermute | solution.py:1221
  182.3 36.9 %collective-permute-start.10 = (bf16[2,6,64,256]{3,2,1,0:T(8,128)(2,1)}, bf16[2,6,64,256]{3,2,1,0:T(8,128)(2,1)}, u32[]{:S(2)}, u32[]{:S(2)}) collective-permute-start(bf16[2,6,64,256]{3,2,1,0:T(8,128)(2,1)} %pad_maximum_fusion.9), channel_id=1, source_target_pairs={{0,16},{4,20},{8,24},{12,28},{16,0},{20,4},{24,8},{28,12},{1,17},{... | collective-permute-start | bytes 1179656 | tf_op jit(solution)/shard_map/ppermute | solution.py:1221
  183.1 36.1 %collective-permute-start.11 = (bf16[2,6,64,256]{3,2,1,0:T(8,128)(2,1)}, bf16[2,6,64,256]{3,2,1,0:T(8,128)(2,1)S(1)}, u32[]{:S(2)}, u32[]{:S(2)}) collective-permute-start(bf16[2,6,64,256]{3,2,1,0:T(8,128)(2,1)} %pad_maximum_fusion.10), channel_id=1, source_target_pairs={{0,24},{4,28},{8,16},{12,20},{16,8},{20,12},{24,0},{28,4},{1,25},{... | collective-permute-start | bytes 1179656 | tf_op jit(solution)/shard_map/ppermute | solution.py:1221
  246.3 43.5 %copy-start.8 = (bf16[8,6,64,256]{3,2,1,0:T(8,128)(2,1)}, bf16[8,6,64,256]{3,2,1,0:T(8,128)(2,1)S(1)}, u32[]{:S(2)}) copy-start(bf16[8,6,64,256]{3,2,1,0:T(8,128)(2,1)S(1)} %constant_dynamic-update-slice_fusion.9) | copy-start | bytes 4718596
  247.3 30.3 %collective-permute-start.12 = (bf16[4,6,64,256]{3,2,1,0:T(8,128)(2,1)S(1)}, bf16[4,6,64,256]{3,2,1,0:T(8,128)(2,1)S(1)}, u32[]{:S(2)}, u32[]{:S(2)}) collective-permute-start(bf16[4,6,64,256]{3,2,1,0:T(8,128)(2,1)S(1)} %slice.301), channel_id=1, source_target_pairs={{0,4},{4,0},{8,12},{12,8},{16,20},{20,16},{24,28},{28,24},{1,5},{5... | collective-permute-start | bytes 2359304 | tf_op jit(solution)/shard_map/ppermute | solution.py:1215
  279.8 58.3 %collective-permute-start.17 = (bf16[2,144,2048]{2,1,0:T(8,128)(2,1)S(1)}, bf16[2,144,2048]{2,1,0:T(8,128)(2,1)S(1)}, u32[]{:S(2)}, u32[]{:S(2)}) collective-permute-start(bf16[2,144,2048]{2,1,0:T(8,128)(2,1)S(1)} %pad_maximum_fusion.4), channel_id=1, source_target_pairs={{0,8},{4,12},{8,0},{12,4},{16,24},{20,28},{24,16},{28,20},{1,9},{5... | collective-permute-start | bytes 3538952 | tf_op jit(solution)/shard_map/ppermute | solution.py:432
  290.0 48.0 %collective-permute-start.14 = (bf16[2,6,64,256]{3,2,1,0:T(8,128)(2,1)S(1)}, bf16[2,6,64,256]{3,2,1,0:T(8,128)(2,1)S(1)}, u32[]{:S(2)}, u32[]{:S(2)}) collective-permute-start(bf16[2,6,64,256]{3,2,1,0:T(8,128)(2,1)S(1)} %pad_maximum_fusion.11), channel_id=1, source_target_pairs={{0,8},{4,12},{8,0},{12,4},{16,24},{20,28},{24,16},{28,20},{1,9},{5... | collective-permute-start | bytes 1179656 | tf_op jit(solution)/shard_map/ppermute | solution.py:1221
  290.1 47.9 %collective-permute-start.15 = (bf16[2,6,64,256]{3,2,1,0:T(8,128)(2,1)S(1)}, bf16[2,6,64,256]{3,2,1,0:T(8,128)(2,1)S(1)}, u32[]{:S(2)}, u32[]{:S(2)}) collective-permute-start(bf16[2,6,64,256]{3,2,1,0:T(8,128)(2,1)S(1)} %pad_maximum_fusion.12), channel_id=1, source_target_pairs={{0,16},{4,20},{8,24},{12,28},{16,0},{20,4},{24,8},{28,12},{1,17},{... | collective-permute-start | bytes 1179656 | tf_op jit(solution)/shard_map/ppermute | solution.py:1221
  290.2 47.8 %collective-permute-start.16 = (bf16[2,6,64,256]{3,2,1,0:T(8,128)(2,1)S(1)}, bf16[2,6,64,256]{3,2,1,0:T(8,128)(2,1)S(1)}, u32[]{:S(2)}, u32[]{:S(2)}) collective-permute-start(bf16[2,6,64,256]{3,2,1,0:T(8,128)(2,1)S(1)} %pad_maximum_fusion.13), channel_id=1, source_target_pairs={{0,24},{4,28},{8,16},{12,20},{16,8},{20,12},{24,0},{28,4},{1,25},{... | collective-permute-start | bytes 1179656 | tf_op jit(solution)/shard_map/ppermute | solution.py:1221
  342.2 29.0 %collective-permute-start.19 = (bf16[2,8,64,1024]{3,2,1,0:T(8,128)(2,1)}, bf16[2,8,64,1024]{3,2,1,0:T(8,128)(2,1)}, u32[]{:S(2)}, u32[]{:S(2)}) collective-permute-start(bf16[2,8,64,1024]{3,2,1,0:T(8,128)(2,1)} %pad_maximum_fusion.2), channel_id=1, source_target_pairs={{0,1},{1,0},{2,3},{3,2},{4,5},{5,4},{6,7},{7,6},{8,9},{9,8},{10,11... | collective-permute-start | bytes 6291464 | tf_op jit(solution)/shard_map/ppermute | solution.py:432
  364.9 37.5 %collective-permute-start.18 = (bf16[2,8,64,1024]{3,2,1,0:T(8,128)(2,1)}, bf16[2,8,64,1024]{3,2,1,0:T(8,128)(2,1)S(1)}, u32[]{:S(2)}, u32[]{:S(2)}) collective-permute-start(bf16[2,8,64,1024]{3,2,1,0:T(8,128)(2,1)} %pad_maximum_fusion.1), channel_id=1, source_target_pairs={{0,1},{1,0},{2,3},{3,2},{4,5},{5,4},{6,7},{7,6},{8,9},{9,8},{10,11... | collective-permute-start | bytes 6291464 | tf_op jit(solution)/shard_map/ppermute | solution.py:432
  367.1 29.2 %collective-permute-start.21 = (bf16[1,144,2048]{2,1,0:T(8,128)(2,1)}, bf16[1,144,2048]{2,1,0:T(8,128)(2,1)S(1)}, u32[]{:S(2)}, u32[]{:S(2)}) collective-permute-start(bf16[1,144,2048]{2,1,0:T(8,128)(2,1)} %add_convert_fusion.3), channel_id=1, source_target_pairs={{0,16},{4,20},{8,24},{12,28},{16,0},{20,4},{24,8},{28,12},{1,17},{... | collective-permute-start | bytes 1769480 | tf_op jit(solution)/shard_map/ppermute | solution.py:432
  374.3 24.5 %collective-permute-start.20 = (bf16[1,8,64,1024]{3,2,1,0:T(8,128)(2,1)}, bf16[1,8,64,1024]{3,2,1,0:T(8,128)(2,1)}, u32[]{:S(2)}, u32[]{:S(2)}) collective-permute-start(bf16[1,8,64,1024]{3,2,1,0:T(8,128)(2,1)} %add_convert_fusion.1), channel_id=1, source_target_pairs={{0,2},{1,3},{2,0},{3,1},{4,6},{5,7},{6,4},{7,5},{8,10},{9,11},{10,... | collective-permute-start | bytes 3145736 | tf_op jit(solution)/shard_map/ppermute | solution.py:432
  411.0 11.3 %collective-permute-start.22 = (bf16[4,64,1024]{2,1,0:T(8,128)(2,1)S(1)}, bf16[4,64,1024]{2,1,0:T(8,128)(2,1)S(1)}, u32[]{:S(2)}, u32[]{:S(2)}) collective-permute-start(bf16[4,64,1024]{2,1,0:T(8,128)(2,1)S(1)} %slice.327), channel_id=1, source_target_pairs={{0,4},{4,0},{8,12},{12,8},{16,20},{20,16},{24,28},{28,24},{1,5},{5... | collective-permute-start | bytes 1572872 | tf_op jit(solution)/shard_map/ppermute | solution.py:1215
  413.2 33.3 %collective-permute-start.26 = (bf16[1,8,64,1024]{3,2,1,0:T(8,128)(2,1)S(1)}, bf16[1,8,64,1024]{3,2,1,0:T(8,128)(2,1)S(1)}, u32[]{:S(2)}, u32[]{:S(2)}) collective-permute-start(bf16[1,8,64,1024]{3,2,1,0:T(8,128)(2,1)S(1)} %fusion.23), channel_id=1, source_target_pairs={{0,2},{1,3},{2,0},{3,1},{4,6},{5,7},{6,4},{7,5},{8,10},{9,11},{10,... | collective-permute-start | bytes 3145736 | tf_op jit(solution)/shard_map/ppermute | solution.py:432
  414.3 32.2 %copy-start.15 = (bf16[8,64,1024]{2,1,0:T(8,128)(2,1)S(1)}, bf16[8,64,1024]{2,1,0:T(8,128)(2,1)}, u32[]{:S(2)}) copy-start(bf16[8,64,1024]{2,1,0:T(8,128)(2,1)} %get-tuple-element.204) | copy-start | bytes 3145732
  414.3 34.5 %collective-permute-start.27 = (bf16[4,1024,128]{2,1,0:T(8,128)(2,1)S(1)}, bf16[4,1024,128]{2,1,0:T(8,128)(2,1)S(1)}, u32[]{:S(2)}, u32[]{:S(2)}) collective-permute-start(bf16[4,1024,128]{2,1,0:T(8,128)(2,1)S(1)} %pad_maximum_fusion.5), channel_id=1, source_target_pairs={{0,4},{4,0},{8,12},{12,8},{16,20},{20,16},{24,28},{28,24},{1,5},{5... | collective-permute-start | bytes 3145736 | tf_op jit(solution)/shard_map/ppermute | solution.py:432
  422.3 24.9 %collective-permute-start.23 = (bf16[2,64,1024]{2,1,0:T(8,128)(2,1)S(1)}, bf16[2,64,1024]{2,1,0:T(8,128)(2,1)S(1)}, u32[]{:S(2)}, u32[]{:S(2)}) collective-permute-start(bf16[2,64,1024]{2,1,0:T(8,128)(2,1)S(1)} %pad_maximum_fusion.20), channel_id=1, source_target_pairs={{0,8},{4,12},{8,0},{12,4},{16,24},{20,28},{24,16},{28,20},{1,9},{5... | collective-permute-start | bytes 786440 | tf_op jit(solution)/shard_map/ppermute | solution.py:1221
  425.5 21.6 %collective-permute-start.24 = (bf16[2,64,1024]{2,1,0:T(8,128)(2,1)S(1)}, bf16[2,64,1024]{2,1,0:T(8,128)(2,1)S(1)}, u32[]{:S(2)}, u32[]{:S(2)}) collective-permute-start(bf16[2,64,1024]{2,1,0:T(8,128)(2,1)S(1)} %pad_maximum_fusion.21), channel_id=1, source_target_pairs={{0,16},{4,20},{8,24},{12,28},{16,0},{20,4},{24,8},{28,12},{1,17},{... | collective-permute-start | bytes 786440 | tf_op jit(solution)/shard_map/ppermute | solution.py:1221
  427.5 21.4 %collective-permute-start.25 = (bf16[2,64,1024]{2,1,0:T(8,128)(2,1)S(1)}, bf16[2,64,1024]{2,1,0:T(8,128)(2,1)S(1)}, u32[]{:S(2)}, u32[]{:S(2)}) collective-permute-start(bf16[2,64,1024]{2,1,0:T(8,128)(2,1)S(1)} %pad_maximum_fusion.22), channel_id=1, source_target_pairs={{0,24},{4,28},{8,16},{12,20},{16,8},{20,12},{24,0},{28,4},{1,25},{... | collective-permute-start | bytes 786440 | tf_op jit(solution)/shard_map/ppermute | solution.py:1221
  449.1 11.7 %collective-permute-start.29 = (bf16[2,1024,128]{2,1,0:T(8,128)(2,1)S(1)}, bf16[2,1024,128]{2,1,0:T(8,128)(2,1)S(1)}, u32[]{:S(2)}, u32[]{:S(2)}) collective-permute-start(bf16[2,1024,128]{2,1,0:T(8,128)(2,1)S(1)} %pad_maximum_fusion.7), channel_id=1, source_target_pairs={{0,8},{4,12},{8,0},{12,4},{16,24},{20,28},{24,16},{28,20},{1,9},{5... | collective-permute-start | bytes 1572872 | tf_op jit(solution)/shard_map/ppermute | solution.py:432
  452.0 10.0 %collective-permute-start.28 = (bf16[4,64,1024]{2,1,0:T(8,128)(2,1)S(1)}, bf16[4,64,1024]{2,1,0:T(8,128)(2,1)S(1)}, u32[]{:S(2)}, u32[]{:S(2)}) collective-permute-start(bf16[4,64,1024]{2,1,0:T(8,128)(2,1)S(1)} %slice.335), channel_id=1, source_target_pairs={{0,4},{4,0},{8,12},{12,8},{16,20},{20,16},{24,28},{28,24},{1,5},{5... | collective-permute-start | bytes 1572872 | tf_op jit(solution)/shard_map/ppermute | solution.py:1215
  462.0 12.3 %collective-permute-start.34 = (bf16[1,1024,128]{2,1,0:T(8,128)(2,1)S(1)}, bf16[1,1024,128]{2,1,0:T(8,128)(2,1)S(1)}, u32[]{:S(2)}, u32[]{:S(2)}) collective-permute-start(bf16[1,1024,128]{2,1,0:T(8,128)(2,1)S(1)} %fusion.42), channel_id=1, source_target_pairs={{0,16},{4,20},{8,24},{12,28},{16,0},{20,4},{24,8},{28,12},{1,17},{... | collective-permute-start | bytes 786440 | tf_op jit(solution)/shard_map/ppermute | solution.py:432
  466.1 33.5 %collective-permute-start.33 = (bf16[1,8,64,1024]{3,2,1,0:T(8,128)(2,1)}, bf16[1,8,64,1024]{3,2,1,0:T(8,128)(2,1)S(1)}, u32[]{:S(2)}, u32[]{:S(2)}) collective-permute-start(bf16[1,8,64,1024]{3,2,1,0:T(8,128)(2,1)} %bitcast.194), channel_id=1, source_target_pairs={{0,2},{1,3},{2,0},{3,1},{4,6},{5,7},{6,4},{7,5},{8,10},{9,11},{10,... | collective-permute-start | bytes 3145736 | tf_op jit(solution)/shard_map/ppermute | solution.py:453
  467.6 32.0 %copy-start.11 = (bf16[8,64,1024]{2,1,0:T(8,128)(2,1)S(1)}, bf16[8,64,1024]{2,1,0:T(8,128)(2,1)}, u32[]{:S(2)}) copy-start(bf16[8,64,1024]{2,1,0:T(8,128)(2,1)} %get-tuple-element.224) | copy-start | bytes 3145732
  467.7 7.6 %collective-permute-start.30 = (bf16[2,64,1024]{2,1,0:T(8,128)(2,1)S(1)}, bf16[2,64,1024]{2,1,0:T(8,128)(2,1)S(1)}, u32[]{:S(2)}, u32[]{:S(2)}) collective-permute-start(bf16[2,64,1024]{2,1,0:T(8,128)(2,1)S(1)} %pad_maximum_fusion.23), channel_id=1, source_target_pairs={{0,8},{4,12},{8,0},{12,4},{16,24},{20,28},{24,16},{28,20},{1,9},{5... | collective-permute-start | bytes 786440 | tf_op jit(solution)/shard_map/ppermute | solution.py:1221
  468.9 24.2 %collective-permute-start.31 = (bf16[2,64,1024]{2,1,0:T(8,128)(2,1)S(1)}, bf16[2,64,1024]{2,1,0:T(8,128)(2,1)S(1)}, u32[]{:S(2)}, u32[]{:S(2)}) collective-permute-start(bf16[2,64,1024]{2,1,0:T(8,128)(2,1)S(1)} %pad_maximum_fusion.24), channel_id=1, source_target_pairs={{0,16},{4,20},{8,24},{12,28},{16,0},{20,4},{24,8},{28,12},{1,17},{... | collective-permute-start | bytes 786440 | tf_op jit(solution)/shard_map/ppermute | solution.py:1221
  469.1 30.5 %collective-permute-start.32 = (bf16[2,64,1024]{2,1,0:T(8,128)(2,1)S(1)}, bf16[2,64,1024]{2,1,0:T(8,128)(2,1)S(1)}, u32[]{:S(2)}, u32[]{:S(2)}) collective-permute-start(bf16[2,64,1024]{2,1,0:T(8,128)(2,1)S(1)} %pad_maximum_fusion.25), channel_id=1, source_target_pairs={{0,24},{4,28},{8,16},{12,20},{16,8},{20,12},{24,0},{28,4},{1,25},{... | collective-permute-start | bytes 786440 | tf_op jit(solution)/shard_map/ppermute | solution.py:1221
  474.4 29.6 %copy-start.3 = (s32[12]{0:T(128)S(1)}, s32[12]{0:T(128)}, u32[]{:S(2)}) copy-start(s32[12]{0:T(128)} %copy-done.2) | copy-start | bytes 148
  501.4 27.8 %collective-permute-start.36 = (bf16[2,8,64,1024]{3,2,1,0:T(8,128)(2,1)}, bf16[2,8,64,1024]{3,2,1,0:T(8,128)(2,1)}, u32[]{:S(2)}, u32[]{:S(2)}) collective-permute-start(bf16[2,8,64,1024]{3,2,1,0:T(8,128)(2,1)} %pad_maximum_fusion.3), channel_id=1, source_target_pairs={{0,1},{1,0},{2,3},{3,2},{4,5},{5,4},{6,7},{7,6},{8,9},{9,8},{10,11... | collective-permute-start | bytes 6291464 | tf_op jit(solution)/shard_map/ppermute | solution.py:453
  510.7 18.5 %collective-permute-start.35 = (bf16[1,4,64,1024]{3,2,1,0:T(8,128)(2,1)}, bf16[1,4,64,1024]{3,2,1,0:T(8,128)(2,1)S(1)}, u32[]{:S(2)}, u32[]{:S(2)}) collective-permute-start(bf16[1,4,64,1024]{3,2,1,0:T(8,128)(2,1)} %bitcast.197), channel_id=1, source_target_pairs={{0,2},{1,3},{2,0},{3,1},{4,6},{5,7},{6,4},{7,5},{8,10},{9,11},{10,... | collective-permute-start | bytes 1572872 | tf_op jit(solution)/shard_map/ppermute | solution.py:453
  530.3 5.6 %collective-permute-start.37 = (bf16[2,4,64,1024]{3,2,1,0:T(8,128)(2,1)}, bf16[2,4,64,1024]{3,2,1,0:T(8,128)(2,1)}, u32[]{:S(2)}, u32[]{:S(2)}) collective-permute-start(bf16[2,4,64,1024]{3,2,1,0:T(8,128)(2,1)} %pad_maximum_fusion.6), channel_id=1, source_target_pairs={{0,1},{1,0},{2,3},{3,2},{4,5},{5,4},{6,7},{7,6},{8,9},{9,8},{10,11... | collective-permute-start | bytes 3145736 | tf_op jit(solution)/shard_map/ppermute | solution.py:453
  (53 other events, 382.2 us)
Sparse Core Ops, SparseCore 0:
  9.6 48.6 all-gather.3
  108.8 38.9 all-gather.5
  149.3 39.8 all-gather.7
  191.6 57.9 reduce-scatter.2
  402.5 72.7 reduce-scatter.4
where the time goes:
time: 558 us; the launch traced here: 549 us
  Pallas kernels  190 us (34%)
  matrix products  89.2 us (16%)
  local copies, waits for them, and re-layouts  73 us (13%)
  waiting for transfers between devices  71.2 us (13%)
  other arithmetic  56.6 us (10%)
  starting transfers between devices  54.6 us (10%)
  between operations  15.3 us (3%)
    pallas_call x2, Pallas kernels, attend_back(): pl.pallas_call(functools.partial(unit_back_kernel, n, shard), grid_spec=p...  49.1 us
    ppermute x18, waiting for transfers between devices, exchange_z(): lax.ppermute(jnp.stack([array[k], got[k // 2]]), 'seq', [(i, i ^ k) for i...  39 us
    pallas_call x2, Pallas kernels, attend(): pl.pallas_call(functools.partial(unit_kernel, n, shard), grid_spec=pltpu....  37.2 us
    dot_general x1, matrix products, on_device_pairs(): jnp.einsum('psd,fd->psf', cot, down_here, preferred_element_type=F32)  28.1 us
    unnamed x139, local copies, waits for them, and re-layouts  28 us
    ppermute x10, starting transfers between devices, cube_send(): return lax.ppermute(sent, axis, [(i, i ^ masks[0]) for i in range(n)])  25.6 us
    pallas_call x2, Pallas kernels, rows_back(): pl.pallas_call(functools.partial(rows_kernel, h, slices), grid_spec=pltpu...  25.1 us
    ppermute x10, waiting for transfers between devices, cube_send(): return lax.ppermute(sent, axis, [(i, i ^ masks[0]) for i in range(n)])  22.4 us
  transfers between devices with their start and end apart: 43, of which 10 were waited for; matrix products, arithmetic and copies ran while one was open for 37% of the time, Pallas kernels for 33%

commit v1 on v0

--- a/solution.py
+++ b/solution.py
@@ -1044,7 +1044,7 @@
 
 
 def unit_back_kernel(
-    n, block, me_ref, low_ref, first_ref, keep_ref, logsum_ref, qkv_ref, grad_ref, out_ref,
+    n, block, by, me_ref, low_ref, first_ref, keep_ref, logsum_ref, qkv_ref, grad_ref, out_ref,
     qt, kt, gt, qn, kn, vn, gn, dk, dv, dqs
 ):
     me = me_ref[0]
@@ -1081,22 +1081,21 @@
             return dot(ds, qn[u, i]), dot(p.astype(BF16), gn[u, i]), dot(kt[u, at], ds)
 
         def backward(t, dqs):
-            j = j0 + 2 * t
-            at = jnp.minimum(j + 1, n - 1)
-            mask0, mask1 = allowed(j), allowed(j + 1)
+            j = j0 + by * t
+            spots = [jnp.minimum(j + b, n - 1) if b else j for b in range(by)]
+            masks = [allowed(j + b) for b in range(by)]
             out = []
             for u, dq in zip(pair, dqs):
-                dk0, dv0, dq0 = one(u, mask0, j)
-                dk1, dv1, dq1 = one(u, mask1, at)
-                dk[u, j] += dk0
-                dv[u, j] += dv0
-                dk[u, at] += dk1
-                dv[u, at] += dv1
-                out.append(dq + dq0 + dq1)
+                terms = [one(u, mask, at) for mask, at in zip(masks, spots)]
+                for (dk0, dv0, dq0), at in zip(terms, spots):
+                    dk[u, at] += dk0
+                    dv[u, at] += dv0
+                    dq = dq + dq0
+                out.append(dq)
             return tuple(out)
 
         dq = lax.fori_loop(
-            0, (i - j0) // 2 + 1, backward, tuple(jnp.zeros((HD, block), F32) for _ in pair)
+            0, (i - j0) // by + 1, backward, tuple(jnp.zeros((HD, block), F32) for _ in pair)
         )
         for u in pair:
             dqs[u, i] = (dq[u] * (1.0 / math.sqrt(HD))).astype(BF16)
@@ -1111,13 +1110,17 @@
             out_ref[u, 2, :, at] = dv[u, i].T.astype(BF16)
 
 
-def rows_kernel(heads, slices, me_ref, grad_ref, normed_ref, w_ref, cos_ref, sin_ref, low_ref, weight_ref):
+def rows_kernel(heads, slices, me_ref, grad_ref, normed_ref, w_ref, cos_ref, sin_ref, *refs):
+    low_ref, weight_ref = refs[-2:]
     width = heads * HD
     column = me_ref[1]
 
     @pl.when(pl.program_id(0) == 0)
     def _():
-        weight_ref[...] = jnp.zeros_like(weight_ref)
+        if len(refs) > 2:
+            weight_ref[...] = refs[0][...]
+        else:
+            weight_ref[...] = jnp.zeros_like(weight_ref)
 
     parts = []
     for j in range(3):
@@ -1126,7 +1129,14 @@
             part = turn(part.astype(F32), cos_ref[...], -sin_ref[...], heads).astype(BF16)
         parts.append(part)
     grads = jnp.concatenate(parts, axis=0)
-    weight_ref[...] += dot(grads, normed_ref[...])
+    if len(refs) > 2:
+        whole = weight_ref.shape[0] // 3
+        start = lax.rem(me_ref[0], 2) * width
+        for j in range(3):
+            rows = pl.ds(pl.multiple_of(j * whole + start, width), width)
+            weight_ref[rows, :] += dot(parts[j], normed_ref[...])
+    else:
+        weight_ref[...] += dot(grads, normed_ref[...])
     low = dot(grads.T, w_ref[...]).astype(BF16)
     part = low.shape[0] // slices
     for m in range(slices):
@@ -1134,10 +1144,13 @@
 
 
 def norm_kernel(x_ref, gain_ref, bias_ref, normed_ref):
-    x = x_ref[0].astype(F32)
-    cent = x - jnp.mean(x, axis=-1, keepdims=True)
-    var = jnp.mean(cent * cent, axis=-1, keepdims=True)
-    normed_ref[0] = (cent * lax.rsqrt(var + EPS) * gain_ref[...] + bias_ref[...]).astype(BF16)
+    step = math.gcd(x_ref.shape[1], 32)
+    for r in range(0, x_ref.shape[1], step):
+        x = x_ref[0, r : r + step].astype(F32)
+        cent = x - jnp.mean(x, axis=-1, keepdims=True)
+        var = jnp.mean(cent * cent, axis=-1, keepdims=True)
+        normed = cent * lax.rsqrt(var + EPS) * gain_ref[...] + bias_ref[...]
+        normed_ref[0, r : r + step] = normed.astype(BF16)
 
 
 def finish_kernel(terms, which_ref, *refs):
@@ -1280,7 +1293,6 @@
     own_dest, shared_dest = own_of[dest], shared_of[dest // 2]
     me = jnp.stack([rank, column])
 
-    token_cols = lax.dynamic_slice_in_dim(tokens, column * cols, cols, 2)
     head_ids = jnp.arange(heads, dtype=jnp.int32)
     half_ids = jnp.arange(half, dtype=jnp.int32)
     units_out = jnp.concatenate(
@@ -1347,11 +1359,20 @@
             name="project",
         )(me, rows, weight, cosine, sine)
 
-    wide = [pltpu.VMEM((2, n, HD, shard), BF16)]
-    tall = [pltpu.VMEM((2, n, shard, HD), BF16)]
-    keep_spec = pl.BlockSpec((2, n, HD, shard), lambda u, *_: (u, 0, 0, 0))
-    log_spec = pl.BlockSpec((2, n, shard), lambda u, *_: (u, 0, 0))
-    unit_spec = pl.BlockSpec((2, 3, HD, pack_len), lambda u, *_: (u, 0, 0, 0))
+    def wide(h):
+        return [pltpu.VMEM((h, n, HD, shard), BF16)]
+
+    def tall(h, kind=BF16):
+        return [pltpu.VMEM((h, n, shard, HD), kind)]
+
+    def keep_spec(h):
+        return pl.BlockSpec((h, n, HD, shard), lambda u, *_: (u, 0, 0, 0))
+
+    def log_spec(h):
+        return pl.BlockSpec((h, n, shard), lambda u, *_: (u, 0, 0))
+
+    def unit_spec(h):
+        return pl.BlockSpec((h, 3, HD, pack_len), lambda u, *_: (u, 0, 0, 0))
 
     def attend(c, qkv):
         h = qkv.shape[0]
@@ -1359,14 +1380,14 @@
             functools.partial(unit_kernel, n, shard),
             grid_spec=pltpu.PrefetchScalarGridSpec(
                 num_scalar_prefetch=2,
-                grid=(h // 2,),
-                in_specs=[pl.BlockSpec((n, shard), whole2), unit_spec],
+                grid=(1,),
+                in_specs=[pl.BlockSpec((n, shard), whole2), unit_spec(h)],
                 out_specs=[
-                    pl.BlockSpec((n, 2, HD, shard), lambda u, *_: (0, u, 0, 0)),
-                    keep_spec,
-                    log_spec,
+                    pl.BlockSpec((n, h, HD, shard), lambda u, *_: (0, u, 0, 0)),
+                    keep_spec(h),
+                    log_spec(h),
                 ],
-                scratch_shapes=wide * 2 + tall,
+                scratch_shapes=wide(h) * 2 + tall(h),
             ),
             out_shape=[
                 jax.ShapeDtypeStruct((n, h, HD, shard), BF16),
@@ -1380,24 +1401,22 @@
 
     def attend_back(c, kept, logsum, qkv, grads):
         h = qkv.shape[0]
-        skip = c * heads // 2
+        step = h if c == 0 else 2
+        skip = c * heads // step
         return pl.pallas_call(
-            functools.partial(unit_back_kernel, n, shard),
+            functools.partial(unit_back_kernel, n, shard, c + 1),
             grid_spec=pltpu.PrefetchScalarGridSpec(
                 num_scalar_prefetch=2,
-                grid=(h // 2,),
+                grid=(h // step,),
                 in_specs=[
                     pl.BlockSpec((n, shard), whole2),
-                    keep_spec,
-                    log_spec,
-                    unit_spec,
-                    pl.BlockSpec((n, 2, HD, shard), lambda u, *_: (0, u + skip, 0, 0)),
+                    keep_spec(step),
+                    log_spec(step),
+                    unit_spec(step),
+                    pl.BlockSpec((n, step, HD, shard), lambda u, *_: (0, u + skip, 0, 0)),
                 ],
-                out_specs=unit_spec,
-                scratch_shapes=wide * 3
-                + tall * 4
-                + [pltpu.VMEM((2, n, shard, HD), F32)] * 2
-                + [pltpu.VMEM((2, n, HD, shard), BF16)],
+                out_specs=unit_spec(step),
+                scratch_shapes=wide(step) * 3 + tall(step) * 4 + tall(step, F32) * 2 + wide(step),
             ),
             out_shape=jax.ShapeDtypeStruct((h, 3, HD, pack_len), BF16),
             compiler_params=params(),
@@ -1405,7 +1424,7 @@
             name="attend_back",
         )(me, lows[c], firsts[c], kept, logsum, qkv, grads)
 
-    def rows_back(grads, normed, weight, cosine, sine):
+    def rows_back(grads, normed, weight, cosine, sine, *base):
         h = grads.shape[0]
         return pl.pallas_call(
             functools.partial(rows_kernel, h, slices),
@@ -1418,23 +1437,24 @@
                     pl.BlockSpec(weight.shape, whole2),
                     pl.BlockSpec((ROT, shard), lane_at),
                     pl.BlockSpec((ROT, shard), lane_at),
-                ],
+                ]
+                + [pl.BlockSpec(v.shape, whole2) for v in base],
                 out_specs=[
                     pl.BlockSpec(
                         (slices, 1, sub, width),
                         lambda s, me: (0, lax.bitwise_xor(s, me[0]), 0, 0),
                     ),
-                    pl.BlockSpec(weight.shape, whole2),
+                    pl.BlockSpec((3 * joined, width), whole2),
                 ],
             ),
             out_shape=[
                 jax.ShapeDtypeStruct((slices, n, sub, width), BF16),
-                jax.ShapeDtypeStruct(weight.shape, F32),
+                jax.ShapeDtypeStruct((3 * joined, width), F32),
             ],
             compiler_params=params(),
             cost_estimate=COST,
             name="rows_back",
-        )(me, grads, normed, weight, cosine, sine)
+        )(me, grads, normed, weight, cosine, sine, *base)
 
     pack_spec = pl.BlockSpec((1, shard, width), lambda p: (p, 0, 0))
     normed_low = pl.pallas_call(
@@ -1559,7 +1579,7 @@
         if not last_step:
             terms_got = cube_send(terms, "seq", n, seq_masks[step + 1 :])
     terms = terms[0]
-    low_shared, head_shared = rows_back(back_shared, normed_shared, w_shared, *turns[1])
+    low_shared, head_all = rows_back(back_shared, normed_shared, w_shared, *turns[1], head_own)
     attended = take(
         exchanged(send_out, out_x, out_z).reshape(n * (heads + half), HD, shard), units_in
     ).reshape(packs, joined, shard)
@@ -1586,8 +1606,8 @@
     )(attended, cot, merge_weight, branch_ff)
     low_terms = {k: low_shared[k] for k in range(slices)}
     low_got = cube_send(low_terms, "mlp", slices, mlp_masks)
-    low_terms, low_got, low_own, branch, terms, low_ff, head_shared = tie(
-        low_terms, low_got, low_own, branch, terms, low_ff, head_shared
+    low_terms, low_got, low_own, branch, terms, low_ff, head_all = tie(
+        low_terms, low_got, low_own, branch, terms, low_ff, head_all
     )
 
     summed = lax.psum_scatter(branch, "mlp", scatter_dimension=0, tiled=False)
@@ -1598,13 +1618,10 @@
         if step < len(mlp_masks) - 1:
             low_got = cube_send(low_terms, "mlp", slices, mlp_masks[step + 1 :])
     low_shared = low_terms[0]
-    head_all = head_own.reshape(3, heads, HD, width)
-    there = lax.dynamic_slice_in_dim(head_all, part_at, half, 1)
-    head_all = lax.dynamic_update_slice_in_dim(
-        head_all, there + head_shared.reshape(3, half, HD, width), part_at, 1
-    ).reshape(3 * joined, width)
-    weights = jnp.concatenate([head_all, merge_part], axis=0).astype(BF16)
-    weights = dict(enumerate(cut(weights, 1, n, rank)))
+    weights = {
+        k: jnp.concatenate(pair, axis=0).astype(BF16)
+        for k, pair in enumerate(zip(cut(head_all, 1, n, rank), cut(merge_part, 1, n, rank)))
+    }
     low_own_z = exchange_z(low_own, low_own_x)
     weights_got = cube_send(weights, "seq", n, seq_masks)
     low_own_z, low_shared, low_own, low_own_x, weights, weights_got = tie(
@@ -1665,7 +1682,12 @@
     weights = weights[0]
     low_shared_z = exchange_z(low_shared, low_shared_x)
     pieces = gather_step([row_own[None]], "mlp", slices, mlp_masks[-1])
-    low_shared_z, pieces, weights = tie(low_shared_z, pieces, weights)
+    result = (
+        lax.dynamic_slice_in_dim(tokens, column * cols, cols, 2).astype(F32)
+        + summed.astype(F32)
+        + lax.dynamic_slice_in_dim(down_bias, column * cols, cols, 0)
+    ).astype(BF16)
+    low_shared_z, pieces, weights, result = tie(low_shared_z, pieces, weights, result)
 
     for m in reversed(mlp_masks[:-1]):
         pieces = gather_step(pieces, "mlp", slices, m)
@@ -1674,12 +1696,7 @@
     row_shared, sums = finish([both, both], [even, jnp.bitwise_xor(even, 1)], shared_of)
     last = gather_step([row_shared[None]], "mlp", slices, mlp_masks[-1])
     vectors = small_sum(sums_own + sums, n, slices)
-    result = (
-        token_cols.astype(F32)
-        + summed.astype(F32)
-        + lax.dynamic_slice_in_dim(down_bias, column * cols, cols, 0)
-    ).astype(BF16)
-    last, pieces, vectors, result = tie(last, pieces, vectors, result)
+    last, pieces, vectors = tie(last, pieces, vectors)
 
     for m in reversed(mlp_masks[:-1]):
         last = gather_step(last, "mlp", slices, m)

time: 558 us -> 541 us (0.970)
  waiting for transfers between devices: 71.2 us -> 59.7 us
  matrix products: 89.2 us -> 81.3 us
  Pallas kernels: 190 us -> 197 us
    ppermute x18, waiting for transfers between devices: 39 us -> 21 us  [exchange_z(): lax.ppermute(jnp.stack([array[k], got[k // 2]]), 'seq', [(i, i ^ k) for i...]
    dot_general x1, matrix products: 28.1 us -> 18.8 us  [on_device_pairs(): jnp.einsum('psd,fd->psf', cot, down_here, preferred_element_type=F32)]
    reduce_scatter x1, waiting for transfers between devices: 0.02 us -> 9.25 us  [on_device_pairs(): summed = lax.psum_scatter(branch, 'mlp', scatter_dimension=0, tiled=False)]
    unnamed x139 -> x129, local copies, waits for them, and re-layouts: 28 us -> 25 us
  transfers between devices with their start and end apart: 43 -> 43, of which waited for: 10 -> 12; matrix products, arithmetic and copies ran while one was open for 37% -> 36% of each run, Pallas kernels for 33% -> 36%
where the time goes in v1:
time: 541 us; the launch traced here: 531 us
  Pallas kernels  197 us (36%)
  matrix products  81.3 us (15%)
  local copies, waits for them, and re-layouts  72 us (13%)
  waiting for transfers between devices  59.7 us (11%)
  other arithmetic  54 us (10%)
  starting transfers between devices  51.5 us (10%)
  between operations  15.5 us (3%)
    pallas_call x2, Pallas kernels, attend_back(): pl.pallas_call(functools.partial(unit_back_kernel, n, shard, c + 1), grid...  51.5 us
    pallas_call x2, Pallas kernels, attend(): pl.pallas_call(functools.partial(unit_kernel, n, shard), grid_spec=pltpu....  40.9 us
    pallas_call x2, Pallas kernels, rows_back(): pl.pallas_call(functools.partial(rows_kernel, h, slices), grid_spec=pltpu...  26.7 us
    unnamed x129, local copies, waits for them, and re-layouts  25 us
    ppermute x10, starting transfers between devices, cube_send(): return lax.ppermute(sent, axis, [(i, i ^ masks[0]) for i in range(n)])  23.3 us
    ppermute x18, waiting for transfers between devices, exchange_z(): lax.ppermute(jnp.stack([array[k], got[k // 2]]), 'seq', [(i, i ^ k) for i...  21 us
    pallas_call x2, Pallas kernels, project(): pl.pallas_call(functools.partial(qkv_kernel, h), grid_spec=pltpu.Prefetch...  21 us
    ppermute x10, waiting for transfers between devices, cube_send(): return lax.ppermute(sent, axis, [(i, i ^ masks[0]) for i in range(n)])  19.9 us
  transfers between devices with their start and end apart: 43, of which 12 were waited for; matrix products, arithmetic and copies ran while one was open for 36% of the time, Pallas kernels for 36%

profile of v1, /device:TPU:17, one launch (start us, length us, event | category | flops | bytes accessed | tf_op | source)
XLA Modules:
  0.0 531.2 jit_solution(4161614149692350535)
XLA Ops:
  10.9 11.5 %norm.1 = bf16[12,256,1024]{2,1,0:T(8,128)(2,1)} custom-call(bf16[12,256,1024]{2,1,0:T(8,128)(2,1)} %refs_3_.1, f32[1,1024]{1,0:T(1,128)} %bitcast.209, f32[1,1024]{1,0:T(1,128)} %bitcast.214), custom_call_target="tpu_custom_call" | custom-call | flops 1048576 | bytes 1048576 | tf_op jit(solution)/shard_map/norm/pallas_call | solution.py:1460
  22.3 2.7 constant_dynamic-slice_fusion.21
  31.3 2.6 copy.45
  38.1 12.7 %broadcast_add_fusion = f32[12,256,1024]{2,1,0:T(8,128)} fusion(f32[1024]{0:T(1024)S(1)} %copy-done.44, bf16[12,256,1024]{2,1,0:T(8,128)(2,1)} %norm.1, bf16[1024,1024]{1,0:T(8,128)(2,1)S(1)} %copy-done.42), kind=kOutput, calls=%fused_computation.24 | convolution fusion | flops 6445596672 | bytes 20975616 | tf_op jit(solution)/shard_map/psd,df->psf/dot_general | solution.py:1476
  53.0 2.8 multiply_sine_fusion
  58.3 12.8 %convolution_convert_fusion.1.branch_ref = bf16[12,256,1024]{2,1,0:T(8,128)(2,1)} fusion(bf16[1024,1024]{1,0:T(8,128)(2,1)S(1)} %copy-done, f32[12,256,1024]{2,1,0:T(8,128)} %broadcast_add_fusion), kind=kOutput, calls=%fused_computation.28 | convolution fusion | flops 6473908224 | bytes 20971520 | tf_op jit(solution)/shard_map/psf,fd->psd/dot_general | solution.py:1483
  76.4 18.8 %fusion.6 = bf16[12,256,1024]{2,1,0:T(8,128)(2,1)} fusion(f32[12,256,1024]{2,1,0:T(8,128)} %broadcast_add_fusion, bf16[12,256,1024]{2,1,0:T(8,128)(2,1)} %all-gather.4.cloned.1.call-done.c_ref.refs_3_.refs_4_, bf16[1024,1024]{1,0:T(8,128)(2,1)S(1)} %copy-done), kind=kOutput, calls=%fused_computation.15 | convolution fusion | flops 6505365504 | bytes 27262976 | tf_op jit(solution)/shard_map/psd,fd->psf/dot_general | solution.py:1500
  95.2 3.3 collective-permute-done.4
  104.5 2.3 collective-permute-start.6
  107.9 12.9 %bitcast_convert_fusion.1 = bf16[1024,1024]{1,0:T(8,128)(2,1)} fusion(bf16[12,256,1024]{2,1,0:T(8,128)(2,1)} %norm.1, bf16[12,256,1024]{2,1,0:T(8,128)(2,1)} %fusion.6), kind=kOutput, calls=%fused_computation.26 | convolution fusion | flops 6443499520 | bytes 14680064 | tf_op jit(solution)/shard_map/psd,psf->df/dot_general | solution.py:1511
  120.8 11.0 %fusion.19 = bf16[1024,1024]{1,0:T(8,128)(2,1)} fusion(bf16[12,256,1024]{2,1,0:T(8,128)(2,1)S(1)} %bitcast.185, f32[12,256,1024]{2,1,0:T(8,128)} %broadcast_add_fusion), kind=kOutput, calls=%fused_computation.50 | convolution fusion | flops 6471811072 | bytes 20971520 | tf_op jit(solution)/shard_map/psd,psf->df/dot_general | solution.py:1514
  131.8 3.0 convolution_convert_fusion.2
  142.6 3.9 convert_reduce_fusion
  148.1 10.2 %convolution_convert_fusion = bf16[12,256,1024]{2,1,0:T(8,128)(2,1)S(1)} fusion(bf16[12,256,1024]{2,1,0:T(8,128)(2,1)} %fusion.6, bf16[1024,1024]{1,0:T(8,128)(2,1)S(1)} %copy-done.43), kind=kOutput, calls=%fused_computation.27 | convolution fusion | flops 6445596672 | bytes 14680064 | tf_op jit(solution)/shard_map/psf,df->psd/dot_general | solution.py:1523
  158.3 3.3 copy.50
  166.0 2.6 constant_dynamic-slice_fusion.5
  180.5 10.8 %project.2 = (bf16[2048,1024]{1,0:T(8,128)(2,1)}, bf16[4,3,64,2048]{3,2,1,0:T(8,128)(2,1)}) custom-call(s32[2]{0:T(128)} %pad_add_fusion.1.me_ref, bf16[8,256,1024]{2,1,0:T(8,128)(2,1)} %all-gather.6.cloned.1.call-done.x_ref, bf16[768,1024]{1,0:T(8,128)(2,1)} %bitcast.188, f32[32,2048]{1,0:T(8,128)} %get-tuple-element.150.cos_ref, ...), custom_call_target="tpu_custom_call" | custom-call | flops 1048576 | bytes 1048576 | tf_op jit(solution)/shard_map/project/pallas_call | solution.py:1335
  191.3 23.6 %attend.2 = (bf16[8,4,64,256]{3,2,1,0:T(8,128)(2,1)}, bf16[4,8,64,256]{3,2,1,0:T(8,128)(2,1)}, f32[4,8,256]{2,1,0:T(8,128)}) custom-call(s32[2]{0:T(128)} %pad_add_fusion.1.me_ref, s32[8]{0:T(128)} %get-tuple-element.441.low_ref, s32[8,256]{1,0:T(8,128)} %copy-done.38, bf16[4,3,64,2048]{3,2,1,0:T(8,128)(2,1)} %get-tuple-element.152.qkv_ref), custom_call_target="tpu_custom_call" | custom-call | flops 1048576 | bytes 1048576 | tf_op jit(solution)/shard_map/attend/pallas_call | solution.py:1379
  215.0 10.1 %project.3 = (bf16[2048,1024]{1,0:T(8,128)(2,1)}, bf16[2,3,64,2048]{3,2,1,0:T(8,128)(2,1)}) custom-call(s32[2]{0:T(128)} %pad_add_fusion.1.me_ref, bf16[8,256,1024]{2,1,0:T(8,128)(2,1)} %all-gather.8.cloned.1.call-done.x_ref, bf16[384,1024]{1,0:T(8,128)(2,1)} %bitcast.190, f32[32,2048]{1,0:T(8,128)} %get-tuple-element.164.cos_ref, ...), custom_call_target="tpu_custom_call" | custom-call | flops 1048576 | bytes 1048576 | tf_op jit(solution)/shard_map/project/pallas_call | solution.py:1335
  225.1 17.2 %attend.3 = (bf16[8,2,64,256]{3,2,1,0:T(8,128)(2,1)}, bf16[2,8,64,256]{3,2,1,0:T(8,128)(2,1)}, f32[2,8,256]{2,1,0:T(8,128)}) custom-call(s32[2]{0:T(128)} %pad_add_fusion.1.me_ref, s32[8]{0:T(128)} %get-tuple-element.440.low_ref, s32[8,256]{1,0:T(8,128)} %copy-done.37, bf16[2,3,64,2048]{3,2,1,0:T(8,128)(2,1)} %get-tuple-element.166.qkv_ref), custom_call_target="tpu_custom_call" | custom-call | flops 1048576 | bytes 1048576 | tf_op jit(solution)/shard_map/attend/pallas_call | solution.py:1379
  245.8 29.2 %attend_back.2.grad_ref = bf16[4,3,64,2048]{3,2,1,0:T(8,128)(2,1)} custom-call(s32[2]{0:T(128)} %pad_add_fusion.1.me_ref, s32[8]{0:T(128)} %get-tuple-element.441.low_ref, s32[8,256]{1,0:T(8,128)} %copy-done.38, bf16[4,8,64,256]{3,2,1,0:T(8,128)(2,1)} %get-tuple-element.174.keep_ref, f32[4,8,256]{2,1,0:T(8,128)} %get-tuple-element.175.logsum_ref, ...), custom_call_target="tpu_custom_call" | custom-call | flops 1048576 | bytes 1048576 | tf_op jit(solution)/shard_map/attend_back/pallas_call | solution.py:1406
  277.2 3.7 collective-permute-start.17
  281.2 3.6 collective-permute-start.15
  284.9 22.3 %attend_back.3.grad_ref = bf16[2,3,64,2048]{3,2,1,0:T(8,128)(2,1)} custom-call(s32[2]{0:T(128)} %pad_add_fusion.1.me_ref, s32[8]{0:T(128)} %get-tuple-element.440.low_ref, s32[8,256]{1,0:T(8,128)} %copy-done.37, bf16[2,8,64,256]{3,2,1,0:T(8,128)(2,1)} %get-tuple-element.187.keep_ref, f32[2,8,256]{2,1,0:T(8,128)} %get-tuple-element.188.logsum_ref, ...), custom_call_target="tpu_custom_call" | custom-call | flops 1048576 | bytes 1048576 | tf_op jit(solution)/shard_map/attend_back/pallas_call | solution.py:1406
  307.2 14.0 %rows_back.2 = (bf16[4,8,64,1024]{3,2,1,0:T(8,128)(2,1)}, f32[768,1024]{1,0:T(8,128)}) custom-call(s32[2]{0:T(128)} %pad_add_fusion.1.me_ref, bf16[4,3,64,2048]{3,2,1,0:T(8,128)(2,1)} %attend_back.2.grad_ref, bf16[2048,1024]{1,0:T(8,128)(2,1)} %get-tuple-element.185.normed_ref, bf16[768,1024]{1,0:T(8,128)(2,1)} %bitcast.189, ...), custom_call_target="tpu_custom_call" | custom-call | flops 1048576 | bytes 1048576 | tf_op jit(solution)/shard_map/rows_back/pallas_call | solution.py:1429
  323.1 2.5 fusion.86
  327.1 6.9 %collective-permute-start.19 = (bf16[2,8,64,1024]{3,2,1,0:T(8,128)(2,1)}, bf16[2,8,64,1024]{3,2,1,0:T(8,128)(2,1)}, u32[]{:S(2)}, u32[]{:S(2)}) collective-permute-start(bf16[2,8,64,1024]{3,2,1,0:T(8,128)(2,1)} %pad_maximum_fusion.2), channel_id=1, source_target_pairs={{0,1},{1,0},{2,3},{3,2},{4,5},{5,4},{6,7},{7,6},{8,9},{9,8},{10,11... | collective-permute-start | bytes 6291464 | tf_op jit(solution)/shard_map/ppermute | solution.py:432
  336.5 12.7 %rows_back.3 = (bf16[4,8,64,1024]{3,2,1,0:T(8,128)(2,1)}, f32[768,1024]{1,0:T(8,128)}) custom-call(s32[2]{0:T(128)} %pad_add_fusion.1.me_ref, bf16[2,3,64,2048]{3,2,1,0:T(8,128)(2,1)} %attend_back.3.grad_ref, bf16[2048,1024]{1,0:T(8,128)(2,1)} %get-tuple-element.190.normed_ref, bf16[384,1024]{1,0:T(8,128)(2,1)} %bitcast.191, ...), custom_call_target="tpu_custom_call" | custom-call | flops 1048576 | bytes 1048576 | tf_op jit(solution)/shard_map/rows_back/pallas_call | solution.py:1429
  349.2 3.9 fusion.87
  356.7 6.8 %collective-permute-start.21 = (bf16[1,144,2048]{2,1,0:T(8,128)(2,1)}, bf16[1,144,2048]{2,1,0:T(8,128)(2,1)S(1)}, u32[]{:S(2)}, u32[]{:S(2)}) collective-permute-start(bf16[1,144,2048]{2,1,0:T(8,128)(2,1)} %add_convert_fusion.3), channel_id=1, source_target_pairs={{0,16},{4,20},{8,24},{12,28},{16,0},{20,4},{24,8},{28,12},{1,17},{... | collective-permute-start | bytes 1769480 | tf_op jit(solution)/shard_map/ppermute | solution.py:432
  372.7 3.2 gather_fusion.6
  375.9 13.9 %join.1 = (bf16[4,12,256,256]{3,2,1,0:T(8,128)(2,1)}, f32[256,1024]{1,0:T(8,128)}) custom-call(bf16[12,256,256]{2,1,0:T(8,128)(2,1)} %bitcast.195, bf16[12,256,1024]{2,1,0:T(8,128)(2,1)} %all-gather.4.cloned.1.call-done.c_ref.refs_3_.refs_4_, bf16[256,1024]{1,0:T(8,128)(2,1)} %merge_ref.1, bf16[12,256,1024]{2,1,0:T(8,128)(2,1)} %convolution_convert_fusion.1.branch_ref), custom_call_target="tpu_custom_call" | custom-call | flops 1048576 | bytes 1048576 | tf_op jit(solution)/shard_map/join/pallas_call | solution.py:1586
  392.3 2.5 fusion.22
  402.3 7.7 %collective-permute-done.22 = bf16[4,64,1024]{2,1,0:T(8,128)(2,1)S(1)} collective-permute-done((bf16[4,64,1024]{2,1,0:T(8,128)(2,1)S(1)}, bf16[4,64,1024]{2,1,0:T(8,128)(2,1)S(1)}, u32[]{:S(2)}, u32[]{:S(2)}) %collective-permute-start.22) | collective-permute-done | bytes 524320 | tf_op jit(solution)/shard_map/ppermute | solution.py:1228
  413.8 14.2 %collective-permute-done.26 = bf16[1,8,64,1024]{3,2,1,0:T(8,128)(2,1)S(1)} collective-permute-done((bf16[1,8,64,1024]{3,2,1,0:T(8,128)(2,1)S(1)}, bf16[1,8,64,1024]{3,2,1,0:T(8,128)(2,1)S(1)}, u32[]{:S(2)}, u32[]{:S(2)}) %collective-permute-start.26) | collective-permute-done | bytes 1048608 | tf_op jit(solution)/shard_map/ppermute | solution.py:432
  429.9 5.2 collective-permute-done.25
  437.6 8.0 %finish.2 = (bf16[8,64,1024]{2,1,0:T(8,128)(2,1)}, f32[2,1024]{1,0:T(2,128)}) custom-call(s32[24]{0:T(128)} %pad_add_fusion.2.which_ref, bf16[8,64,1024]{2,1,0:T(8,128)(2,1)} %copy-done.15, bf16[12,64,1024]{2,1,0:T(8,128)(2,1)} %bitcast.198, bf16[12,256,1024]{2,1,0:T(8,128)(2,1)} %refs_3_.1, ...), custom_call_target="tpu_custom_call" | custom-call | flops 1048576 | bytes 1048576 | tf_op jit(solution)/shard_map/finish/pallas_call | solution.py:1645
  450.7 2.3 collective-permute-start.31
  453.8 5.0 collective-permute-done.34
  458.9 9.2 %reduce-scatter.5.cloned.1.call-done = bf16[1,12,256,256]{3,2,1,0:T(8,128)(2,1)} async-done(((bf16[4,12,256,256]{3,2,1,0:T(8,128)(2,1)}), bf16[1,12,256,256]{3,2,1,0:T(8,128)(2,1)}) %reduce-scatter.5.cloned.1.call-update) | async-done | bytes 1572880 | tf_op jit(solution)/shard_map/reduce_scatter | solution.py:1613
  468.2 3.6 fusion.11
  471.8 3.1 collective-permute-done.31
  474.8 7.5 %collective-permute-done.32 = bf16[2,64,1024]{2,1,0:T(8,128)(2,1)} collective-permute-done((bf16[2,64,1024]{2,1,0:T(8,128)(2,1)}, bf16[2,64,1024]{2,1,0:T(8,128)(2,1)}, u32[]{:S(2)}, u32[]{:S(2)}) %collective-permute-start.32) | collective-permute-done | bytes 262176 | tf_op jit(solution)/shard_map/ppermute | solution.py:1234
  482.4 2.7 pad_maximum_fusion.3
  489.6 5.1 finish.3
  497.4 12.2 %small_sum.1 = f32[2,128]{1,0:T(2,128)} custom-call(f32[8,2,128]{2,1,0:T(2,128)} %add_bitcast_fusion.x_ref), custom_call_target="tpu_custom_call" | custom-call | flops 1048576 | bytes 1048576 | tf_op jit(solution)/shard_map/small_sum/pallas_call | solution.py:374
  509.6 2.3 pad_maximum_fusion.5
  517.5 6.7 %settle.1 = bf16[12,256,1024]{2,1,0:T(8,128)(2,1)} custom-call(s32[13]{0:T(128)} %pad_add_fusion.3.table_ref, bf16[1,8,64,1024]{3,2,1,0:T(8,128)(2,1)} %bitcast.201, bf16[1,8,64,1024]{3,2,1,0:T(8,128)(2,1)} %collective-permute-done.33.refs_1_, bf16[2,8,64,1024]{3,2,1,0:T(8,128)(2,1)} %collective-permute-done.36.refs_2_, bf16[1,4,64,1024]{3,2,1,0:T(8,128)(2,1)} %bitcast.205, ...), custom_call_target="tpu_custom_call" | custom-call | tf_op jit(solution)/shard_map/settle/pallas_call | solution.py:1710
  (361 shorter events, 117.8 us)
Async XLA Ops:
  7.2 51.1 %copy-start = (bf16[1024,1024]{1,0:T(8,128)(2,1)S(1)}, bf16[1024,1024]{1,0:T(8,128)(2,1)}, u32[]{:S(2)}) copy-start(bf16[1024,1024]{1,0:T(8,128)(2,1)} %param.21) | copy-start | bytes 6291460
  7.2 69.2 %all-gather.4.cloned.1.call-start = ((), (), s32[]{:S(2)}) async-start(), calls=%async_computation.2 | async-start | bytes 7864320 | tf_op jit(solution)/shard_map/all_gather | solution.py:1275
  7.9 155.7 %all-gather.6.cloned.1.call-start = ((), (), s32[]{:S(2)}) async-start(), calls=%async_computation.3 | async-start | bytes 5242880 | tf_op jit(solution)/shard_map/all_gather | solution.py:1504
  9.5 20.9 %copy-start.2 = (s32[12]{0:T(128)}, s32[12]{0:T(128)S(1)}, u32[]{:S(2)}) copy-start(s32[12]{0:T(128)S(1)} %select_reduce_fusion.1) | copy-start | bytes 148
  28.0 27.8 %collective-permute-start = (bf16[4,256,256]{2,1,0:T(8,128)(2,1)}, bf16[4,256,256]{2,1,0:T(8,128)(2,1)}, u32[]{:S(2)}, u32[]{:S(2)}) collective-permute-start(bf16[4,256,256]{2,1,0:T(8,128)(2,1)} %slice.270), channel_id=1, source_target_pairs={{0,4},{4,0},{8,12},{12,8},{16,20},{20,16},{24,28},{28,24},{1,5},{5... | collective-permute-start | bytes 1572872 | tf_op jit(solution)/shard_map/ppermute | solution.py:1228
  56.8 14.3 %collective-permute-start.1 = (bf16[2,256,256]{2,1,0:T(8,128)(2,1)S(1)}, bf16[2,256,256]{2,1,0:T(8,128)(2,1)S(1)}, u32[]{:S(2)}, u32[]{:S(2)}) collective-permute-start(bf16[2,256,256]{2,1,0:T(8,128)(2,1)S(1)} %pad_maximum_fusion.13), channel_id=1, source_target_pairs={{0,8},{4,12},{8,0},{12,4},{16,24},{20,28},{24,16},{28,20},{1,9},{5... | collective-permute-start | bytes 786440 | tf_op jit(solution)/shard_map/ppermute | solution.py:1234
  58.2 12.9 %collective-permute-start.2 = (bf16[4,256,256]{2,1,0:T(8,128)(2,1)S(1)}, bf16[4,256,256]{2,1,0:T(8,128)(2,1)S(1)}, u32[]{:S(2)}, u32[]{:S(2)}) collective-permute-start(bf16[4,256,256]{2,1,0:T(8,128)(2,1)S(1)} %slice.274), channel_id=1, source_target_pairs={{0,4},{4,0},{8,12},{12,8},{16,20},{20,16},{24,28},{28,24},{1,5},{5... | collective-permute-start | bytes 1572872 | tf_op jit(solution)/shard_map/ppermute | solution.py:1228
  74.4 20.9 %collective-permute-start.3 = (bf16[2,256,256]{2,1,0:T(8,128)(2,1)}, bf16[2,256,256]{2,1,0:T(8,128)(2,1)}, u32[]{:S(2)}, u32[]{:S(2)}) collective-permute-start(bf16[2,256,256]{2,1,0:T(8,128)(2,1)} %pad_maximum_fusion.14), channel_id=1, source_target_pairs={{0,16},{4,20},{8,24},{12,28},{16,0},{20,4},{24,8},{28,12},{1,17},{... | collective-permute-start | bytes 786440 | tf_op jit(solution)/shard_map/ppermute | solution.py:1234
  75.1 23.4 %collective-permute-start.4 = (bf16[2,256,256]{2,1,0:T(8,128)(2,1)}, bf16[2,256,256]{2,1,0:T(8,128)(2,1)}, u32[]{:S(2)}, u32[]{:S(2)}) collective-permute-start(bf16[2,256,256]{2,1,0:T(8,128)(2,1)} %pad_maximum_fusion.15), channel_id=1, source_target_pairs={{0,24},{4,28},{8,16},{12,20},{16,8},{20,12},{24,0},{28,4},{1,25},{... | collective-permute-start | bytes 786440 | tf_op jit(solution)/shard_map/ppermute | solution.py:1234
  102.6 112.3 %all-gather.8.cloned.1.call-start = ((), (), s32[]{:S(2)}) async-start(), calls=%async_computation.4 | async-start | bytes 5242880 | tf_op jit(solution)/shard_map/all_gather | solution.py:1518
  103.8 33.1 %collective-permute-start.5 = (bf16[2,256,256]{2,1,0:T(8,128)(2,1)}, bf16[2,256,256]{2,1,0:T(8,128)(2,1)S(1)}, u32[]{:S(2)}, u32[]{:S(2)}) collective-permute-start(bf16[2,256,256]{2,1,0:T(8,128)(2,1)} %pad_maximum_fusion.16), channel_id=1, source_target_pairs={{0,8},{4,12},{8,0},{12,4},{16,24},{20,28},{24,16},{28,20},{1,9},{5... | collective-permute-start | bytes 786440 | tf_op jit(solution)/shard_map/ppermute | solution.py:1234
  104.5 32.4 %collective-permute-start.6 = (bf16[2,256,256]{2,1,0:T(8,128)(2,1)}, bf16[2,256,256]{2,1,0:T(8,128)(2,1)}, u32[]{:S(2)}, u32[]{:S(2)}) collective-permute-start(bf16[2,256,256]{2,1,0:T(8,128)(2,1)} %pad_maximum_fusion.17), channel_id=1, source_target_pairs={{0,16},{4,20},{8,24},{12,28},{16,0},{20,4},{24,8},{28,12},{1,17},{... | collective-permute-start | bytes 786440 | tf_op jit(solution)/shard_map/ppermute | solution.py:1234
  107.6 29.3 %collective-permute-start.7 = (bf16[2,256,256]{2,1,0:T(8,128)(2,1)}, bf16[2,256,256]{2,1,0:T(8,128)(2,1)}, u32[]{:S(2)}, u32[]{:S(2)}) collective-permute-start(bf16[2,256,256]{2,1,0:T(8,128)(2,1)} %pad_maximum_fusion.18), channel_id=1, source_target_pairs={{0,24},{4,28},{8,16},{12,20},{16,8},{20,12},{24,0},{28,4},{1,25},{... | collective-permute-start | bytes 786440 | tf_op jit(solution)/shard_map/ppermute | solution.py:1234
  142.5 252.3 %reduce-scatter.3.cloned.1.call-start = ((), (), s32[]{:S(2)}) async-start(), calls=%async_computation.5 | async-start | bytes 7864320 | tf_op jit(solution)/shard_map/reduce_scatter | solution.py:1531
  146.5 17.0 %collective-permute-start.8 = (bf16[4,6,64,256]{3,2,1,0:T(8,128)(2,1)S(1)}, bf16[4,6,64,256]{3,2,1,0:T(8,128)(2,1)S(1)}, u32[]{:S(2)}, u32[]{:S(2)}) collective-permute-start(bf16[4,6,64,256]{3,2,1,0:T(8,128)(2,1)S(1)} %slice.286), channel_id=1, source_target_pairs={{0,4},{4,0},{8,12},{12,8},{16,20},{20,16},{24,28},{28,24},{1,5},{5... | collective-permute-start | bytes 2359304 | tf_op jit(solution)/shard_map/ppermute | solution.py:1228
  164.5 303.7 %reduce-scatter.5.cloned.1.call-start = ((), (), s32[]{:S(2)}) async-start(), calls=%async_computation.6 | async-start | bytes 7864320 | tf_op jit(solution)/shard_map/reduce_scatter | solution.py:1613
  172.4 102.6 %collective-permute-start.13 = (bf16[4,144,2048]{2,1,0:T(8,128)(2,1)}, bf16[4,144,2048]{2,1,0:T(8,128)(2,1)}, u32[]{:S(2)}, u32[]{:S(2)}) collective-permute-start(bf16[4,144,2048]{2,1,0:T(8,128)(2,1)} %pad_maximum_fusion), channel_id=1, source_target_pairs={{0,4},{4,0},{8,12},{12,8},{16,20},{20,16},{24,28},{28,24},{1,5},{5... | collective-permute-start | bytes 7077896 | tf_op jit(solution)/shard_map/ppermute | solution.py:432
  175.0 39.9 %collective-permute-start.9 = (bf16[2,6,64,256]{3,2,1,0:T(8,128)(2,1)}, bf16[2,6,64,256]{3,2,1,0:T(8,128)(2,1)}, u32[]{:S(2)}, u32[]{:S(2)}) collective-permute-start(bf16[2,6,64,256]{3,2,1,0:T(8,128)(2,1)} %pad_maximum_fusion.7), channel_id=1, source_target_pairs={{0,8},{4,12},{8,0},{12,4},{16,24},{20,28},{24,16},{28,20},{1,9},{5... | collective-permute-start | bytes 1179656 | tf_op jit(solution)/shard_map/ppermute | solution.py:1234
  175.8 39.1 %collective-permute-start.10 = (bf16[2,6,64,256]{3,2,1,0:T(8,128)(2,1)}, bf16[2,6,64,256]{3,2,1,0:T(8,128)(2,1)}, u32[]{:S(2)}, u32[]{:S(2)}) collective-permute-start(bf16[2,6,64,256]{3,2,1,0:T(8,128)(2,1)} %pad_maximum_fusion.8), channel_id=1, source_target_pairs={{0,16},{4,20},{8,24},{12,28},{16,0},{20,4},{24,8},{28,12},{1,17},{... | collective-permute-start | bytes 1179656 | tf_op jit(solution)/shard_map/ppermute | solution.py:1234
  178.9 36.1 %collective-permute-start.11 = (bf16[2,6,64,256]{3,2,1,0:T(8,128)(2,1)}, bf16[2,6,64,256]{3,2,1,0:T(8,128)(2,1)S(1)}, u32[]{:S(2)}, u32[]{:S(2)}) collective-permute-start(bf16[2,6,64,256]{3,2,1,0:T(8,128)(2,1)} %pad_maximum_fusion.9), channel_id=1, source_target_pairs={{0,24},{4,28},{8,16},{12,20},{16,8},{20,12},{24,0},{28,4},{1,25},{... | collective-permute-start | bytes 1179656 | tf_op jit(solution)/shard_map/ppermute | solution.py:1234
  244.7 36.2 %copy-start.8 = (bf16[8,6,64,256]{3,2,1,0:T(8,128)(2,1)}, bf16[8,6,64,256]{3,2,1,0:T(8,128)(2,1)S(1)}, u32[]{:S(2)}) copy-start(bf16[8,6,64,256]{3,2,1,0:T(8,128)(2,1)S(1)} %constant_dynamic-update-slice_fusion.9) | copy-start | bytes 4718596
  245.7 29.3 %collective-permute-start.12 = (bf16[4,6,64,256]{3,2,1,0:T(8,128)(2,1)S(1)}, bf16[4,6,64,256]{3,2,1,0:T(8,128)(2,1)S(1)}, u32[]{:S(2)}, u32[]{:S(2)}) collective-permute-start(bf16[4,6,64,256]{3,2,1,0:T(8,128)(2,1)S(1)} %slice.301), channel_id=1, source_target_pairs={{0,4},{4,0},{8,12},{12,8},{16,20},{20,16},{24,28},{28,24},{1,5},{5... | collective-permute-start | bytes 2359304 | tf_op jit(solution)/shard_map/ppermute | solution.py:1228
  277.2 46.0 %collective-permute-start.17 = (bf16[2,144,2048]{2,1,0:T(8,128)(2,1)S(1)}, bf16[2,144,2048]{2,1,0:T(8,128)(2,1)S(1)}, u32[]{:S(2)}, u32[]{:S(2)}) collective-permute-start(bf16[2,144,2048]{2,1,0:T(8,128)(2,1)S(1)} %pad_maximum_fusion.4), channel_id=1, source_target_pairs={{0,8},{4,12},{8,0},{12,4},{16,24},{20,28},{24,16},{28,20},{1,9},{5... | collective-permute-start | bytes 3538952 | tf_op jit(solution)/shard_map/ppermute | solution.py:432
  281.1 40.2 %collective-permute-start.14 = (bf16[2,6,64,256]{3,2,1,0:T(8,128)(2,1)S(1)}, bf16[2,6,64,256]{3,2,1,0:T(8,128)(2,1)S(1)}, u32[]{:S(2)}, u32[]{:S(2)}) collective-permute-start(bf16[2,6,64,256]{3,2,1,0:T(8,128)(2,1)S(1)} %pad_maximum_fusion.10), channel_id=1, source_target_pairs={{0,8},{4,12},{8,0},{12,4},{16,24},{20,28},{24,16},{28,20},{1,9},{5... | collective-permute-start | bytes 1179656 | tf_op jit(solution)/shard_map/ppermute | solution.py:1234
  281.2 41.9 %collective-permute-start.15 = (bf16[2,6,64,256]{3,2,1,0:T(8,128)(2,1)S(1)}, bf16[2,6,64,256]{3,2,1,0:T(8,128)(2,1)S(1)}, u32[]{:S(2)}, u32[]{:S(2)}) collective-permute-start(bf16[2,6,64,256]{3,2,1,0:T(8,128)(2,1)S(1)} %pad_maximum_fusion.11), channel_id=1, source_target_pairs={{0,16},{4,20},{8,24},{12,28},{16,0},{20,4},{24,8},{28,12},{1,17},{... | collective-permute-start | bytes 1179656 | tf_op jit(solution)/shard_map/ppermute | solution.py:1234
  284.8 38.3 %collective-permute-start.16 = (bf16[2,6,64,256]{3,2,1,0:T(8,128)(2,1)S(1)}, bf16[2,6,64,256]{3,2,1,0:T(8,128)(2,1)S(1)}, u32[]{:S(2)}, u32[]{:S(2)}) collective-permute-start(bf16[2,6,64,256]{3,2,1,0:T(8,128)(2,1)S(1)} %pad_maximum_fusion.12), channel_id=1, source_target_pairs={{0,24},{4,28},{8,16},{12,20},{16,8},{20,12},{24,0},{28,4},{1,25},{... | collective-permute-start | bytes 1179656 | tf_op jit(solution)/shard_map/ppermute | solution.py:1234
  323.1 31.4 %copy-start.16 = (bf16[2,144,2048]{2,1,0:T(8,128)(2,1)}, bf16[2,144,2048]{2,1,0:T(8,128)(2,1)S(1)}, u32[]{:S(2)}) copy-start(bf16[2,144,2048]{2,1,0:T(8,128)(2,1)S(1)} %collective-permute-done.17) | copy-start | bytes 3538948
  327.1 38.0 %collective-permute-start.19 = (bf16[2,8,64,1024]{3,2,1,0:T(8,128)(2,1)}, bf16[2,8,64,1024]{3,2,1,0:T(8,128)(2,1)}, u32[]{:S(2)}, u32[]{:S(2)}) collective-permute-start(bf16[2,8,64,1024]{3,2,1,0:T(8,128)(2,1)} %pad_maximum_fusion.2), channel_id=1, source_target_pairs={{0,1},{1,0},{2,3},{3,2},{4,5},{5,4},{6,7},{7,6},{8,9},{9,8},{10,11... | collective-permute-start | bytes 6291464 | tf_op jit(solution)/shard_map/ppermute | solution.py:432
  354.6 40.2 %collective-permute-start.18 = (bf16[2,8,64,1024]{3,2,1,0:T(8,128)(2,1)}, bf16[2,8,64,1024]{3,2,1,0:T(8,128)(2,1)}, u32[]{:S(2)}, u32[]{:S(2)}) collective-permute-start(bf16[2,8,64,1024]{3,2,1,0:T(8,128)(2,1)} %pad_maximum_fusion.1), channel_id=1, source_target_pairs={{0,1},{1,0},{2,3},{3,2},{4,5},{5,4},{6,7},{7,6},{8,9},{9,8},{10,11... | collective-permute-start | bytes 6291464 | tf_op jit(solution)/shard_map/ppermute | solution.py:432
  356.7 33.1 %collective-permute-start.21 = (bf16[1,144,2048]{2,1,0:T(8,128)(2,1)}, bf16[1,144,2048]{2,1,0:T(8,128)(2,1)S(1)}, u32[]{:S(2)}, u32[]{:S(2)}) collective-permute-start(bf16[1,144,2048]{2,1,0:T(8,128)(2,1)} %add_convert_fusion.3), channel_id=1, source_target_pairs={{0,16},{4,20},{8,24},{12,28},{16,0},{20,4},{24,8},{28,12},{1,17},{... | collective-permute-start | bytes 1769480 | tf_op jit(solution)/shard_map/ppermute | solution.py:432
  367.2 25.1 %collective-permute-start.20 = (bf16[1,8,64,1024]{3,2,1,0:T(8,128)(2,1)S(1)}, bf16[1,8,64,1024]{3,2,1,0:T(8,128)(2,1)}, u32[]{:S(2)}, u32[]{:S(2)}) collective-permute-start(bf16[1,8,64,1024]{3,2,1,0:T(8,128)(2,1)S(1)} %add_convert_fusion.1), channel_id=1, source_target_pairs={{0,2},{1,3},{2,0},{3,1},{4,6},{5,7},{6,4},{7,5},{8,10},{9,11},{10,... | collective-permute-start | bytes 3145736 | tf_op jit(solution)/shard_map/ppermute | solution.py:432
  397.6 12.4 %collective-permute-start.22 = (bf16[4,64,1024]{2,1,0:T(8,128)(2,1)S(1)}, bf16[4,64,1024]{2,1,0:T(8,128)(2,1)S(1)}, u32[]{:S(2)}, u32[]{:S(2)}) collective-permute-start(bf16[4,64,1024]{2,1,0:T(8,128)(2,1)S(1)} %slice.327), channel_id=1, source_target_pairs={{0,4},{4,0},{8,12},{12,8},{16,20},{20,16},{24,28},{28,24},{1,5},{5... | collective-permute-start | bytes 1572872 | tf_op jit(solution)/shard_map/ppermute | solution.py:1228
  400.4 27.6 %collective-permute-start.26 = (bf16[1,8,64,1024]{3,2,1,0:T(8,128)(2,1)S(1)}, bf16[1,8,64,1024]{3,2,1,0:T(8,128)(2,1)S(1)}, u32[]{:S(2)}, u32[]{:S(2)}) collective-permute-start(bf16[1,8,64,1024]{3,2,1,0:T(8,128)(2,1)S(1)} %fusion.23), channel_id=1, source_target_pairs={{0,2},{1,3},{2,0},{3,1},{4,6},{5,7},{6,4},{7,5},{8,10},{9,11},{10,... | collective-permute-start | bytes 3145736 | tf_op jit(solution)/shard_map/ppermute | solution.py:432
  401.4 33.7 %collective-permute-start.27 = (bf16[4,1024,128]{2,1,0:T(8,128)(2,1)S(1)}, bf16[4,1024,128]{2,1,0:T(8,128)(2,1)S(1)}, u32[]{:S(2)}, u32[]{:S(2)}) collective-permute-start(bf16[4,1024,128]{2,1,0:T(8,128)(2,1)S(1)} %maximum_maximum_fusion), channel_id=1, source_target_pairs={{0,4},{4,0},{8,12},{12,8},{16,20},{20,16},{24,28},{28,24},{1,5},{5... | collective-permute-start | bytes 3145736 | tf_op jit(solution)/shard_map/ppermute | solution.py:432
  402.2 25.8 %copy-start.12 = (bf16[8,64,1024]{2,1,0:T(8,128)(2,1)S(1)}, bf16[8,64,1024]{2,1,0:T(8,128)(2,1)}, u32[]{:S(2)}) copy-start(bf16[8,64,1024]{2,1,0:T(8,128)(2,1)} %get-tuple-element.205) | copy-start | bytes 3145732
  410.1 19.8 %collective-permute-start.23 = (bf16[2,64,1024]{2,1,0:T(8,128)(2,1)S(1)}, bf16[2,64,1024]{2,1,0:T(8,128)(2,1)S(1)}, u32[]{:S(2)}, u32[]{:S(2)}) collective-permute-start(bf16[2,64,1024]{2,1,0:T(8,128)(2,1)S(1)} %pad_maximum_fusion.19), channel_id=1, source_target_pairs={{0,8},{4,12},{8,0},{12,4},{16,24},{20,28},{24,16},{28,20},{1,9},{5... | collective-permute-start | bytes 786440 | tf_op jit(solution)/shard_map/ppermute | solution.py:1234
  412.4 17.5 %collective-permute-start.24 = (bf16[2,64,1024]{2,1,0:T(8,128)(2,1)S(1)}, bf16[2,64,1024]{2,1,0:T(8,128)(2,1)S(1)}, u32[]{:S(2)}, u32[]{:S(2)}) collective-permute-start(bf16[2,64,1024]{2,1,0:T(8,128)(2,1)S(1)} %pad_maximum_fusion.20), channel_id=1, source_target_pairs={{0,16},{4,20},{8,24},{12,28},{16,0},{20,4},{24,8},{28,12},{1,17},{... | collective-permute-start | bytes 786440 | tf_op jit(solution)/shard_map/ppermute | solution.py:1234
  412.8 22.2 %collective-permute-start.25 = (bf16[2,64,1024]{2,1,0:T(8,128)(2,1)S(1)}, bf16[2,64,1024]{2,1,0:T(8,128)(2,1)S(1)}, u32[]{:S(2)}, u32[]{:S(2)}) collective-permute-start(bf16[2,64,1024]{2,1,0:T(8,128)(2,1)S(1)} %pad_maximum_fusion.21), channel_id=1, source_target_pairs={{0,24},{4,28},{8,16},{12,20},{16,8},{20,12},{24,0},{28,4},{1,25},{... | collective-permute-start | bytes 786440 | tf_op jit(solution)/shard_map/ppermute | solution.py:1234
  435.3 10.8 %collective-permute-start.29 = (bf16[2,1024,128]{2,1,0:T(8,128)(2,1)S(1)}, bf16[2,1024,128]{2,1,0:T(8,128)(2,1)S(1)}, u32[]{:S(2)}, u32[]{:S(2)}) collective-permute-start(bf16[2,1024,128]{2,1,0:T(8,128)(2,1)S(1)} %pad_maximum_fusion.6), channel_id=1, source_target_pairs={{0,8},{4,12},{8,0},{12,4},{16,24},{20,28},{24,16},{28,20},{1,9},{5... | collective-permute-start | bytes 1572872 | tf_op jit(solution)/shard_map/ppermute | solution.py:432
  435.4 10.8 %collective-permute-start.28 = (bf16[4,64,1024]{2,1,0:T(8,128)(2,1)S(1)}, bf16[4,64,1024]{2,1,0:T(8,128)(2,1)S(1)}, u32[]{:S(2)}, u32[]{:S(2)}) collective-permute-start(bf16[4,64,1024]{2,1,0:T(8,128)(2,1)S(1)} %slice.335), channel_id=1, source_target_pairs={{0,4},{4,0},{8,12},{12,8},{16,20},{20,16},{24,28},{28,24},{1,5},{5... | collective-permute-start | bytes 1572872 | tf_op jit(solution)/shard_map/ppermute | solution.py:1228
  446.4 12.4 %collective-permute-start.34 = (bf16[1,1024,128]{2,1,0:T(8,128)(2,1)S(1)}, bf16[1,1024,128]{2,1,0:T(8,128)(2,1)S(1)}, u32[]{:S(2)}, u32[]{:S(2)}) collective-permute-start(bf16[1,1024,128]{2,1,0:T(8,128)(2,1)S(1)} %fusion.34), channel_id=1, source_target_pairs={{0,16},{4,20},{8,24},{12,28},{16,0},{20,4},{24,8},{28,12},{1,17},{... | collective-permute-start | bytes 786440 | tf_op jit(solution)/shard_map/ppermute | solution.py:432
  447.6 34.7 %collective-permute-start.33 = (bf16[1,8,64,1024]{3,2,1,0:T(8,128)(2,1)}, bf16[1,8,64,1024]{3,2,1,0:T(8,128)(2,1)}, u32[]{:S(2)}, u32[]{:S(2)}) collective-permute-start(bf16[1,8,64,1024]{3,2,1,0:T(8,128)(2,1)} %bitcast.200), channel_id=1, source_target_pairs={{0,2},{1,3},{2,0},{3,1},{4,6},{5,7},{6,4},{7,5},{8,10},{9,11},{10,... | collective-permute-start | bytes 3145736 | tf_op jit(solution)/shard_map/ppermute | solution.py:453
  449.7 22.1 %collective-permute-start.30 = (bf16[2,64,1024]{2,1,0:T(8,128)(2,1)}, bf16[2,64,1024]{2,1,0:T(8,128)(2,1)S(1)}, u32[]{:S(2)}, u32[]{:S(2)}) collective-permute-start(bf16[2,64,1024]{2,1,0:T(8,128)(2,1)} %pad_maximum_fusion.26), channel_id=1, source_target_pairs={{0,8},{4,12},{8,0},{12,4},{16,24},{20,28},{24,16},{28,20},{1,9},{5... | collective-permute-start | bytes 786440 | tf_op jit(solution)/shard_map/ppermute | solution.py:1234
  450.7 24.2 %collective-permute-start.31 = (bf16[2,64,1024]{2,1,0:T(8,128)(2,1)}, bf16[2,64,1024]{2,1,0:T(8,128)(2,1)S(1)}, u32[]{:S(2)}, u32[]{:S(2)}) collective-permute-start(bf16[2,64,1024]{2,1,0:T(8,128)(2,1)} %pad_maximum_fusion.27), channel_id=1, source_target_pairs={{0,16},{4,20},{8,24},{12,28},{16,0},{20,4},{24,8},{28,12},{1,17},{... | collective-permute-start | bytes 786440 | tf_op jit(solution)/shard_map/ppermute | solution.py:1234
  453.7 28.7 %collective-permute-start.32 = (bf16[2,64,1024]{2,1,0:T(8,128)(2,1)}, bf16[2,64,1024]{2,1,0:T(8,128)(2,1)}, u32[]{:S(2)}, u32[]{:S(2)}) collective-permute-start(bf16[2,64,1024]{2,1,0:T(8,128)(2,1)} %pad_maximum_fusion.28), channel_id=1, source_target_pairs={{0,24},{4,28},{8,16},{12,20},{16,8},{20,12},{24,0},{28,4},{1,25},{... | collective-permute-start | bytes 786440 | tf_op jit(solution)/shard_map/ppermute | solution.py:1234
  485.1 24.5 %collective-permute-start.36 = (bf16[2,8,64,1024]{3,2,1,0:T(8,128)(2,1)}, bf16[2,8,64,1024]{3,2,1,0:T(8,128)(2,1)}, u32[]{:S(2)}, u32[]{:S(2)}) collective-permute-start(bf16[2,8,64,1024]{3,2,1,0:T(8,128)(2,1)} %pad_maximum_fusion.3), channel_id=1, source_target_pairs={{0,1},{1,0},{2,3},{3,2},{4,5},{5,4},{6,7},{7,6},{8,9},{9,8},{10,11... | collective-permute-start | bytes 6291464 | tf_op jit(solution)/shard_map/ppermute | solution.py:453
  494.6 15.0 %collective-permute-start.35 = (bf16[1,4,64,1024]{3,2,1,0:T(8,128)(2,1)}, bf16[1,4,64,1024]{3,2,1,0:T(8,128)(2,1)S(1)}, u32[]{:S(2)}, u32[]{:S(2)}) collective-permute-start(bf16[1,4,64,1024]{3,2,1,0:T(8,128)(2,1)} %bitcast.203), channel_id=1, source_target_pairs={{0,2},{1,3},{2,0},{3,1},{4,6},{5,7},{6,4},{7,5},{8,10},{9,11},{10,... | collective-permute-start | bytes 1572872 | tf_op jit(solution)/shard_map/ppermute | solution.py:453
  511.9 5.6 %collective-permute-start.37 = (bf16[2,4,64,1024]{3,2,1,0:T(8,128)(2,1)}, bf16[2,4,64,1024]{3,2,1,0:T(8,128)(2,1)}, u32[]{:S(2)}, u32[]{:S(2)}) collective-permute-start(bf16[2,4,64,1024]{3,2,1,0:T(8,128)(2,1)} %pad_maximum_fusion.5), channel_id=1, source_target_pairs={{0,1},{1,0},{2,3},{3,2},{4,5},{5,4},{6,7},{7,6},{8,9},{9,8},{10,11... | collective-permute-start | bytes 3145736 | tf_op jit(solution)/shard_map/ppermute | solution.py:453
  (47 other events, 353.0 us)
Sparse Core Ops, SparseCore 0:
  9.6 48.7 all-gather.3
  102.8 36.5 all-gather.5
  142.6 37.6 all-gather.7
  182.7 57.9 reduce-scatter.2
  395.0 73.1 reduce-scatter.4

commit v2 on v1

--- a/solution.py
+++ b/solution.py
@@ -1111,13 +1111,13 @@
 
 
 def rows_kernel(heads, slices, me_ref, grad_ref, normed_ref, w_ref, cos_ref, sin_ref, *refs):
-    low_ref, weight_ref = refs[-2:]
+    kept_ref, sent_ref, weight_ref = refs[-3:]
     width = heads * HD
     column = me_ref[1]
 
     @pl.when(pl.program_id(0) == 0)
     def _():
-        if len(refs) > 2:
+        if len(refs) > 3:
             weight_ref[...] = refs[0][...]
         else:
             weight_ref[...] = jnp.zeros_like(weight_ref)
@@ -1129,7 +1129,7 @@
             part = turn(part.astype(F32), cos_ref[...], -sin_ref[...], heads).astype(BF16)
         parts.append(part)
     grads = jnp.concatenate(parts, axis=0)
-    if len(refs) > 2:
+    if len(refs) > 3:
         whole = weight_ref.shape[0] // 3
         start = lax.rem(me_ref[0], 2) * width
         for j in range(3):
@@ -1140,10 +1140,17 @@
     low = dot(grads.T, w_ref[...]).astype(BF16)
     part = low.shape[0] // slices
     for m in range(slices):
-        low_ref[lax.bitwise_xor(jnp.int32(m), column), 0] = low[m * part : (m + 1) * part]
-
-
-def norm_kernel(x_ref, gain_ref, bias_ref, normed_ref):
+        at = lax.bitwise_xor(jnp.int32(m), column)
+        for bit, ref in enumerate((kept_ref, sent_ref)):
+
+            @pl.when(at % 2 == bit)
+            def _():
+                ref[at // 2, 0] = low[m * part : (m + 1) * part]
+
+
+def norm_kernel(me_ref, x_ref, gain_ref, bias_ref, normed_ref, cols_ref):
+    cols = cols_ref.shape[2]
+    start = pl.multiple_of(me_ref[1] * cols, cols)
     step = math.gcd(x_ref.shape[1], 32)
     for r in range(0, x_ref.shape[1], step):
         x = x_ref[0, r : r + step].astype(F32)
@@ -1151,6 +1158,7 @@
         var = jnp.mean(cent * cent, axis=-1, keepdims=True)
         normed = cent * lax.rsqrt(var + EPS) * gain_ref[...] + bias_ref[...]
         normed_ref[0, r : r + step] = normed.astype(BF16)
+    cols_ref[0] = normed_ref[0, :, pl.ds(start, cols)]
 
 
 def finish_kernel(terms, which_ref, *refs):
@@ -1240,6 +1248,14 @@
     return jnp.concatenate([array[:1], got[:1], *gots], axis=0)
 
 
+def sum_on(terms, axis, n, masks):
+    for step in range(len(masks)):
+        terms = {k: v.astype(BF16) for k, v in terms.items()}
+        got = cube_send(terms, axis, n, masks[step:])
+        terms = cube_add(terms, got, masks[step:], F32)
+    return terms[0].astype(BF16)
+
+
 def take(array, index):
     return jnp.take(array, index, axis=0, mode="clip")
 
@@ -1441,14 +1457,18 @@
                 + [pl.BlockSpec(v.shape, whole2) for v in base],
                 out_specs=[
                     pl.BlockSpec(
-                        (slices, 1, sub, width),
+                        (slices // 2, 1, sub, width),
                         lambda s, me: (0, lax.bitwise_xor(s, me[0]), 0, 0),
-                    ),
+                    )
+                ]
+                * 2
+                + [
                     pl.BlockSpec((3 * joined, width), whole2),
                 ],
             ),
             out_shape=[
-                jax.ShapeDtypeStruct((slices, n, sub, width), BF16),
+                jax.ShapeDtypeStruct((slices // 2, n, sub, width), BF16),
+                jax.ShapeDtypeStruct((slices // 2, n, sub, width), BF16),
                 jax.ShapeDtypeStruct((3 * joined, width), F32),
             ],
             compiler_params=params(),
@@ -1456,18 +1476,27 @@
             name="rows_back",
         )(me, grads, normed, weight, cosine, sine, *base)
 
-    pack_spec = pl.BlockSpec((1, shard, width), lambda p: (p, 0, 0))
-    normed_low = pl.pallas_call(
+    pack_spec = pl.BlockSpec((1, shard, width), lambda p, *_: (p, 0, 0))
+    normed_low, normed_cols = pl.pallas_call(
         norm_kernel,
-        grid=(packs,),
-        in_specs=[pack_spec, pl.BlockSpec((1, width), whole2), pl.BlockSpec((1, width), whole2)],
-        out_specs=pack_spec,
-        out_shape=jax.ShapeDtypeStruct((packs, shard, width), BF16),
+        grid_spec=pltpu.PrefetchScalarGridSpec(
+            num_scalar_prefetch=1,
+            grid=(packs,),
+            in_specs=[
+                pack_spec,
+                pl.BlockSpec((1, width), whole2),
+                pl.BlockSpec((1, width), whole2),
+            ],
+            out_specs=[pack_spec, pl.BlockSpec((1, shard, cols), lambda p, *_: (p, 0, 0))],
+        ),
+        out_shape=[
+            jax.ShapeDtypeStruct((packs, shard, width), BF16),
+            jax.ShapeDtypeStruct((packs, shard, cols), BF16),
+        ],
         compiler_params=params(),
         cost_estimate=COST,
         name="norm",
-    )(tokens, gain, bias)
-    normed_cols = lax.dynamic_slice_in_dim(normed_low, column * cols, cols, 2)
+    )(me, tokens, gain, bias)
     send_own = take(normed_cols, own_dest)
     send_shared = take(normed_cols, shared_dest)
     own_x = exchange_x(send_own)
@@ -1556,33 +1585,44 @@
     terms_got = cube_send(terms, "seq", n, seq_masks)
     normed_shared, qkv_shared = project(rows_shared, w_shared, *turns[1])
     out_shared, kept_shared, log_shared = attend(1, qkv_shared)
-    out_shared, kept_shared, log_shared, grads = tie(out_shared, kept_shared, log_shared, grads)
+    out_shared, kept_shared, log_shared, grads, terms_got = tie(
+        out_shared, kept_shared, log_shared, grads, terms_got
+    )
+    terms = cube_add(terms, terms_got, seq_masks, BF16)
+    terms_got = cube_send(terms, "seq", n, seq_masks[1:])
 
     send_out = jnp.concatenate([out_own, out_shared], axis=1)
     out_x = exchange_x(send_out)
     back_own = attend_back(0, kept_own, log_own, qkv_own, grads)
     out_x, back_own, terms_got, send_out = tie(out_x, back_own, terms_got, send_out)
 
-    terms = cube_add(terms, terms_got, seq_masks, BF16)
-    terms_got = cube_send(terms, "seq", n, seq_masks[1:])
     out_z = exchange_z(send_out, out_x)
-    low_own, head_own = rows_back(back_own, normed_own, w_own, *turns[0])
+    low_kept, low_sent, head_own = rows_back(back_own, normed_own, w_own, *turns[0])
     back_shared = attend_back(1, kept_shared, log_shared, qkv_shared, grads)
-    out_z, terms_got, low_own, back_shared, send_out, out_x = tie(
-        out_z, terms_got, low_own, back_shared, send_out, out_x
-    )
-
-    low_own = cube_sum([low_own[k] for k in range(slices)], "mlp", mlp_masks, BF16).astype(BF16)
-    for step in range(1, len(seq_masks)):
-        last_step = step == len(seq_masks) - 1
-        terms = cube_add(terms, terms_got, seq_masks[step:], F32 if last_step else BF16)
-        if not last_step:
-            terms_got = cube_send(terms, "seq", n, seq_masks[step + 1 :])
-    terms = terms[0]
-    low_shared, head_all = rows_back(back_shared, normed_shared, w_shared, *turns[1], head_own)
+    out_z, low_kept, low_sent, back_shared, send_out, out_x = tie(
+        out_z, low_kept, low_sent, back_shared, send_out, out_x
+    )
+
+    others = [(i, i ^ 1) for i in range(slices)]
+    low_got, back_shared = tie(lax.ppermute(low_sent, "mlp", others), back_shared)
+    low_terms = {
+        2 * k: low_kept[k].astype(F32) + low_got[k].astype(F32) for k in range(slices // 2)
+    }
+    low_own = sum_on(low_terms, "mlp", slices, mlp_masks[1:])
+    low_kept, low_sent, head_all = rows_back(back_shared, normed_shared, w_shared, *turns[1], head_own)
     attended = take(
         exchanged(send_out, out_x, out_z).reshape(n * (heads + half), HD, shard), units_in
     ).reshape(packs, joined, shard)
+    for step in range(1, len(seq_masks) - 1):
+        terms = cube_add(terms, terms_got, seq_masks[step:], BF16)
+        terms_got = cube_send(terms, "seq", n, seq_masks[step + 1 :])
+    low_own, low_kept, low_sent, attended, terms_got = tie(
+        low_own, low_kept, low_sent, attended, terms_got
+    )
+    terms = cube_add(terms, terms_got, seq_masks[len(seq_masks) - 1 :], F32)[0]
+
+    low_own_x = exchange_x(low_own)
+    low_got = lax.ppermute(low_sent, "mlp", others)
     branch, merge_part = pl.pallas_call(
         functools.partial(join_kernel, slices),
         grid=(packs,),
@@ -1604,28 +1644,23 @@
         cost_estimate=COST,
         name="join",
     )(attended, cot, merge_weight, branch_ff)
-    low_terms = {k: low_shared[k] for k in range(slices)}
-    low_got = cube_send(low_terms, "mlp", slices, mlp_masks)
-    low_terms, low_got, low_own, branch, terms, low_ff, head_all = tie(
-        low_terms, low_got, low_own, branch, terms, low_ff, head_all
-    )
-
+    low_kept, low_got, low_own, low_own_x, branch, low_ff, head_all = tie(
+        low_kept, low_got, low_own, low_own_x, branch, low_ff, head_all
+    )
     summed = lax.psum_scatter(branch, "mlp", scatter_dimension=0, tiled=False)
 
-    low_own_x = exchange_x(low_own)
-    for step in range(len(mlp_masks)):
-        low_terms = cube_add(low_terms, low_got, mlp_masks[step:], BF16)
-        if step < len(mlp_masks) - 1:
-            low_got = cube_send(low_terms, "mlp", slices, mlp_masks[step + 1 :])
-    low_shared = low_terms[0]
+    low_terms = {
+        2 * k: low_kept[k].astype(F32) + low_got[k].astype(F32) for k in range(slices // 2)
+    }
+    low_shared = sum_on(low_terms, "mlp", slices, mlp_masks[1:])
     weights = {
         k: jnp.concatenate(pair, axis=0).astype(BF16)
         for k, pair in enumerate(zip(cut(head_all, 1, n, rank), cut(merge_part, 1, n, rank)))
     }
     low_own_z = exchange_z(low_own, low_own_x)
     weights_got = cube_send(weights, "seq", n, seq_masks)
-    low_own_z, low_shared, low_own, low_own_x, weights, weights_got = tie(
-        low_own_z, low_shared, low_own, low_own_x, weights, weights_got
+    low_own_z, low_shared, low_own, low_own_x, weights, weights_got, terms = tie(
+        low_own_z, low_shared, low_own, low_own_x, weights, weights_got, terms
     )
 
     low_shared_x = exchange_x(low_shared)

time: 541 us -> 537 us (level)
  starting transfers between devices: 51.5 us -> 35.1 us
  Pallas kernels: 197 us -> 211 us
    ppermute x10 -> x8, starting transfers between devices: 23.3 us -> 6.3 us  [cube_send(): return lax.ppermute(sent, axis, [(i, i ^ masks[0]) for i in range(n)])]
    ppermute x10 -> x8, waiting for transfers between devices: 19.9 us -> 36.2 us  [cube_send(): return lax.ppermute(sent, axis, [(i, i ^ masks[0]) for i in range(n)])]
    ppermute x6, waiting for transfers between devices: 8.83 us -> 0.09 us  [exchange_x(): return lax.ppermute(array[1::2], 'seq', [(i, i ^ 1) for i in range(n)])]
    convert_element_type x1 -> x4, other arithmetic: 2.5 us -> 9 us  [the longest x2 4.82 us: sum_on(): terms = {k: v.astype(BF16) for k, v in terms.items()}]
    slice x2 -> x0, local copies, waits for them, and re-layouts: 6.33 us -> none  [the longest x1 3.86 us: on_device_pairs(): low_terms = {k: low_shared[k] for k in range(slices)}]
    unnamed x129 -> x147, local copies, waits for them, and re-layouts: 25 us -> 29 us
  transfers between devices with their start and end apart: 43 -> 43, of which waited for: 12 -> 9; matrix products, arithmetic and copies ran while one was open for 36% -> 35% of each run, Pallas kernels for 36% -> 39%
where the time goes in v2:
time: 537 us; the launch traced here: 528 us
  Pallas kernels  211 us (39%)
  matrix products  81.4 us (15%)
  local copies, waits for them, and re-layouts  67.4 us (13%)
  waiting for transfers between devices  64.7 us (12%)
  other arithmetic  52.4 us (10%)
  starting transfers between devices  35.1 us (7%)
  between operations  15.8 us (3%)
    pallas_call x2, Pallas kernels, attend_back(): pl.pallas_call(functools.partial(unit_back_kernel, n, shard, c + 1), grid...  56.7 us
    pallas_call x2, Pallas kernels, attend(): pl.pallas_call(functools.partial(unit_kernel, n, shard), grid_spec=pltpu....  45.7 us
    ppermute x8, waiting for transfers between devices, cube_send(): return lax.ppermute(sent, axis, [(i, i ^ masks[0]) for i in range(n)])  36.2 us
    unnamed x147, local copies, waits for them, and re-layouts  29 us
    pallas_call x2, Pallas kernels, rows_back(): pl.pallas_call(functools.partial(rows_kernel, h, slices), grid_spec=pltpu...  28 us
    pallas_call x2, Pallas kernels, project(): pl.pallas_call(functools.partial(qkv_kernel, h), grid_spec=pltpu.Prefetch...  21 us
    dot_general x1, matrix products, on_device_pairs(): jnp.einsum('psd,fd->psf', cot, down_here, preferred_element_type=F32)  18.8 us
    ppermute x18, starting transfers between devices, exchange_z(): lax.ppermute(jnp.stack([array[k], got[k // 2]]), 'seq', [(i, i ^ k) for i...  17.3 us
  transfers between devices with their start and end apart: 43, of which 9 were waited for; matrix products, arithmetic and copies ran while one was open for 35% of the time, Pallas kernels for 39%

profile of v2, /device:TPU:17, one launch (start us, length us, event | category | flops | bytes accessed | tf_op | source)
XLA Modules:
  0.0 527.6 jit_solution(9970827425244416174)
XLA Ops:
  11.5 12.4 %norm.1 = (bf16[12,256,1024]{2,1,0:T(8,128)(2,1)}, bf16[12,256,256]{2,1,0:T(8,128)(2,1)}) custom-call(s32[2]{0:T(128)} %pad_add_fusion.1.me_ref, bf16[12,256,1024]{2,1,0:T(8,128)(2,1)} %refs_3_.1, f32[1,1024]{1,0:T(1,128)} %bitcast.196, f32[1,1024]{1,0:T(1,128)} %bitcast.201), custom_call_target="tpu_custom_call" | custom-call | flops 1048576 | bytes 1048576 | tf_op jit(solution)/shard_map/norm/pallas_call | solution.py:1480
  23.9 2.1 gather_fusion.2
  30.2 2.6 copy.45
  32.8 2.3 constant_dynamic-slice_fusion.20
  37.1 12.4 %broadcast_add_fusion = f32[12,256,1024]{2,1,0:T(8,128)} fusion(f32[1024]{0:T(1024)S(1)} %copy-done.53, bf16[12,256,1024]{2,1,0:T(8,128)(2,1)} %get-tuple-element.141, bf16[1024,1024]{1,0:T(8,128)(2,1)S(1)} %copy-done.50), kind=kOutput, calls=%fused_computation.24 | convolution fusion | flops 6445596672 | bytes 20975616 | tf_op jit(solution)/shard_map/psd,df->psf/dot_general | solution.py:1505
  51.8 2.8 multiply_sine_fusion
  57.2 12.7 %convolution_convert_fusion.1.branch_ref = bf16[12,256,1024]{2,1,0:T(8,128)(2,1)} fusion(bf16[1024,1024]{1,0:T(8,128)(2,1)S(1)} %copy-done, f32[12,256,1024]{2,1,0:T(8,128)} %broadcast_add_fusion), kind=kOutput, calls=%fused_computation.28 | convolution fusion | flops 6473908224 | bytes 20971520 | tf_op jit(solution)/shard_map/psf,fd->psd/dot_general | solution.py:1512
  75.5 18.8 %fusion.6 = bf16[12,256,1024]{2,1,0:T(8,128)(2,1)} fusion(f32[12,256,1024]{2,1,0:T(8,128)} %broadcast_add_fusion, bf16[12,256,1024]{2,1,0:T(8,128)(2,1)} %all-gather.4.cloned.1.call-done.c_ref.refs_3_.refs_4_, bf16[1024,1024]{1,0:T(8,128)(2,1)S(1)} %copy-done), kind=kOutput, calls=%fused_computation.15 | convolution fusion | flops 6505365504 | bytes 27262976 | tf_op jit(solution)/shard_map/psd,fd->psf/dot_general | solution.py:1529
  94.3 3.5 collective-permute-done.4
  107.1 12.9 %bitcast_convert_fusion.1 = bf16[1024,1024]{1,0:T(8,128)(2,1)} fusion(bf16[12,256,1024]{2,1,0:T(8,128)(2,1)} %get-tuple-element.141, bf16[12,256,1024]{2,1,0:T(8,128)(2,1)} %fusion.6), kind=kOutput, calls=%fused_computation.26 | convolution fusion | flops 6443499520 | bytes 14680064 | tf_op jit(solution)/shard_map/psd,psf->df/dot_general | solution.py:1540
  120.1 11.0 %fusion.16 = bf16[1024,1024]{1,0:T(8,128)(2,1)} fusion(bf16[12,256,1024]{2,1,0:T(8,128)(2,1)S(1)} %bitcast.172, f32[12,256,1024]{2,1,0:T(8,128)} %broadcast_add_fusion), kind=kOutput, calls=%fused_computation.45 | convolution fusion | flops 6471811072 | bytes 20971520 | tf_op jit(solution)/shard_map/psd,psf->df/dot_general | solution.py:1543
  131.1 3.0 convolution_convert_fusion.2
  134.1 2.1 gather_fusion.5
  143.3 3.9 convert_reduce_fusion
  148.5 10.5 %convolution_convert_fusion = bf16[12,256,1024]{2,1,0:T(8,128)(2,1)S(1)} fusion(bf16[12,256,1024]{2,1,0:T(8,128)(2,1)} %fusion.6, bf16[1024,1024]{1,0:T(8,128)(2,1)S(1)} %copy-done.51), kind=kOutput, calls=%fused_computation.27 | convolution fusion | flops 6445596672 | bytes 14680064 | tf_op jit(solution)/shard_map/psf,df->psd/dot_general | solution.py:1552
  159.0 3.3 copy.50
  176.0 2.1 collective-permute-start.10
  179.4 10.9 %project.2 = (bf16[2048,1024]{1,0:T(8,128)(2,1)}, bf16[4,3,64,2048]{3,2,1,0:T(8,128)(2,1)}) custom-call(s32[2]{0:T(128)} %pad_add_fusion.1.me_ref, bf16[8,256,1024]{2,1,0:T(8,128)(2,1)} %all-gather.6.cloned.1.call-done.x_ref, bf16[768,1024]{1,0:T(8,128)(2,1)} %bitcast.175, f32[32,2048]{1,0:T(8,128)} %get-tuple-element.164.cos_ref, ...), custom_call_target="tpu_custom_call" | custom-call | flops 1048576 | bytes 1048576 | tf_op jit(solution)/shard_map/project/pallas_call | solution.py:1351
  190.3 26.8 %attend.2 = (bf16[8,4,64,256]{3,2,1,0:T(8,128)(2,1)}, bf16[4,8,64,256]{3,2,1,0:T(8,128)(2,1)}, f32[4,8,256]{2,1,0:T(8,128)}) custom-call(s32[2]{0:T(128)} %pad_add_fusion.1.me_ref, s32[8]{0:T(128)} %get-tuple-element.459.low_ref, s32[8,256]{1,0:T(8,128)} %copy-done.40, bf16[4,3,64,2048]{3,2,1,0:T(8,128)(2,1)} %get-tuple-element.166.qkv_ref), custom_call_target="tpu_custom_call" | custom-call | flops 1048576 | bytes 1048576 | tf_op jit(solution)/shard_map/attend/pallas_call | solution.py:1395
  217.2 10.1 %project.3 = (bf16[2048,1024]{1,0:T(8,128)(2,1)}, bf16[2,3,64,2048]{3,2,1,0:T(8,128)(2,1)}) custom-call(s32[2]{0:T(128)} %pad_add_fusion.1.me_ref, bf16[8,256,1024]{2,1,0:T(8,128)(2,1)} %all-gather.8.cloned.1.call-done.x_ref, bf16[384,1024]{1,0:T(8,128)(2,1)} %bitcast.177, f32[32,2048]{1,0:T(8,128)} %get-tuple-element.178.cos_ref, ...), custom_call_target="tpu_custom_call" | custom-call | flops 1048576 | bytes 1048576 | tf_op jit(solution)/shard_map/project/pallas_call | solution.py:1351
  227.3 18.9 %attend.3 = (bf16[8,2,64,256]{3,2,1,0:T(8,128)(2,1)}, bf16[2,8,64,256]{3,2,1,0:T(8,128)(2,1)}, f32[2,8,256]{2,1,0:T(8,128)}) custom-call(s32[2]{0:T(128)} %pad_add_fusion.1.me_ref, s32[8]{0:T(128)} %get-tuple-element.458.low_ref, s32[8,256]{1,0:T(8,128)} %copy-done.39, bf16[2,3,64,2048]{3,2,1,0:T(8,128)(2,1)} %get-tuple-element.180.qkv_ref), custom_call_target="tpu_custom_call" | custom-call | flops 1048576 | bytes 1048576 | tf_op jit(solution)/shard_map/attend/pallas_call | solution.py:1395
  249.3 2.2 add_convert_fusion.9
  252.8 32.2 %attend_back.2.grad_ref = bf16[4,3,64,2048]{3,2,1,0:T(8,128)(2,1)} custom-call(s32[2]{0:T(128)} %pad_add_fusion.1.me_ref, s32[8]{0:T(128)} %get-tuple-element.459.low_ref, s32[8,256]{1,0:T(8,128)} %copy-done.40, bf16[4,8,64,256]{3,2,1,0:T(8,128)(2,1)} %get-tuple-element.192.keep_ref, f32[4,8,256]{2,1,0:T(8,128)} %get-tuple-element.193.logsum_ref, ...), custom_call_target="tpu_custom_call" | custom-call | flops 1048576 | bytes 1048576 | tf_op jit(solution)/shard_map/attend_back/pallas_call | solution.py:1422
  288.2 24.5 %attend_back.3.grad_ref = bf16[2,3,64,2048]{3,2,1,0:T(8,128)(2,1)} custom-call(s32[2]{0:T(128)} %pad_add_fusion.1.me_ref, s32[8]{0:T(128)} %get-tuple-element.458.low_ref, s32[8,256]{1,0:T(8,128)} %copy-done.39, bf16[2,8,64,256]{3,2,1,0:T(8,128)(2,1)} %get-tuple-element.202.keep_ref, f32[2,8,256]{2,1,0:T(8,128)} %get-tuple-element.203.logsum_ref, ...), custom_call_target="tpu_custom_call" | custom-call | flops 1048576 | bytes 1048576 | tf_op jit(solution)/shard_map/attend_back/pallas_call | solution.py:1422
  312.7 14.7 %rows_back.2 = (bf16[2,8,64,1024]{3,2,1,0:T(8,128)(2,1)}, bf16[2,8,64,1024]{3,2,1,0:T(8,128)(2,1)}, f32[768,1024]{1,0:T(8,128)}) custom-call(s32[2]{0:T(128)} %pad_add_fusion.1.me_ref, bf16[4,3,64,2048]{3,2,1,0:T(8,128)(2,1)} %attend_back.2.grad_ref, bf16[2048,1024]{1,0:T(8,128)(2,1)} %get-tuple-element.199.normed_ref, bf16[768,1024]{1,0:T(8,128)(2,1)} %bitcast.176, ...), custom_call_target="tpu_custom_call" | custom-call | flops 1048576 | bytes 1048576 | tf_op jit(solution)/shard_map/rows_back/pallas_call | solution.py:1445
  327.4 4.3 collective-permute-start.18
  333.1 2.8 collective-permute-done.18
  335.9 3.0 add_convert_fusion.4
  340.1 2.2 add_convert_fusion.6
  342.3 3.9 collective-permute-start.20
  352.8 3.2 gather_fusion.6
  356.1 13.3 %rows_back.3 = (bf16[2,8,64,1024]{3,2,1,0:T(8,128)(2,1)}, bf16[2,8,64,1024]{3,2,1,0:T(8,128)(2,1)}, f32[768,1024]{1,0:T(8,128)}) custom-call(s32[2]{0:T(128)} %pad_add_fusion.1.me_ref, bf16[2,3,64,2048]{3,2,1,0:T(8,128)(2,1)} %attend_back.3.grad_ref, bf16[2048,1024]{1,0:T(8,128)(2,1)} %get-tuple-element.209.normed_ref, bf16[384,1024]{1,0:T(8,128)(2,1)} %bitcast.178, ...), custom_call_target="tpu_custom_call" | custom-call | flops 1048576 | bytes 1048576 | tf_op jit(solution)/shard_map/rows_back/pallas_call | solution.py:1445
  369.4 2.3 fusion.19
  373.5 13.7 %join.1 = (bf16[4,12,256,256]{3,2,1,0:T(8,128)(2,1)}, f32[256,1024]{1,0:T(8,128)}) custom-call(bf16[12,256,256]{2,1,0:T(8,128)(2,1)} %bitcast.182, bf16[12,256,1024]{2,1,0:T(8,128)(2,1)} %all-gather.4.cloned.1.call-done.c_ref.refs_3_.refs_4_, bf16[256,1024]{1,0:T(8,128)(2,1)} %merge_ref.1, bf16[12,256,1024]{2,1,0:T(8,128)(2,1)} %convolution_convert_fusion.1.branch_ref), custom_call_target="tpu_custom_call" | custom-call | flops 1048576 | bytes 1048576 | tf_op jit(solution)/shard_map/join/pallas_call | solution.py:1626
  397.4 2.7 collective-permute-start.25
  400.2 29.1 %collective-permute-done.26 = bf16[1,8,64,1024]{3,2,1,0:T(8,128)(2,1)S(1)} collective-permute-done((bf16[1,8,64,1024]{3,2,1,0:T(8,128)(2,1)S(1)}, bf16[1,8,64,1024]{3,2,1,0:T(8,128)(2,1)S(1)}, u32[]{:S(2)}, u32[]{:S(2)}) %collective-permute-start.26) | collective-permute-done | bytes 1048608 | tf_op jit(solution)/shard_map/ppermute | solution.py:432
  433.0 7.9 %finish.2 = (bf16[8,64,1024]{2,1,0:T(8,128)(2,1)}, f32[2,1024]{1,0:T(2,128)}) custom-call(s32[24]{0:T(128)} %pad_add_fusion.2.which_ref, bf16[8,64,1024]{2,1,0:T(8,128)(2,1)} %copy-done.16, bf16[12,64,1024]{2,1,0:T(8,128)(2,1)} %bitcast.185, bf16[12,256,1024]{2,1,0:T(8,128)(2,1)} %refs_3_.1, ...), custom_call_target="tpu_custom_call" | custom-call | flops 1048576 | bytes 1048576 | tf_op jit(solution)/shard_map/finish/pallas_call | solution.py:1680
  445.8 2.3 collective-permute-start.31
  448.8 5.3 %collective-permute-done.34 = bf16[1,1024,128]{2,1,0:T(8,128)(2,1)S(1)} collective-permute-done((bf16[1,1024,128]{2,1,0:T(8,128)(2,1)S(1)}, bf16[1,1024,128]{2,1,0:T(8,128)(2,1)S(1)}, u32[]{:S(2)}, u32[]{:S(2)}) %collective-permute-start.34) | collective-permute-done | bytes 262176 | tf_op jit(solution)/shard_map/ppermute | solution.py:432
  454.2 7.6 %reduce-scatter.5.cloned.1.call-done = bf16[1,12,256,256]{3,2,1,0:T(8,128)(2,1)} async-done(((bf16[4,12,256,256]{3,2,1,0:T(8,128)(2,1)}), bf16[1,12,256,256]{3,2,1,0:T(8,128)(2,1)}) %reduce-scatter.5.cloned.1.call-update) | async-done | bytes 1572880 | tf_op jit(solution)/shard_map/reduce_scatter | solution.py:1650
  461.9 3.6 fusion.11
  465.4 5.0 collective-permute-done.31
  470.4 8.7 %collective-permute-done.32 = bf16[2,64,1024]{2,1,0:T(8,128)(2,1)} collective-permute-done((bf16[2,64,1024]{2,1,0:T(8,128)(2,1)}, bf16[2,64,1024]{2,1,0:T(8,128)(2,1)}, u32[]{:S(2)}, u32[]{:S(2)}) %collective-permute-start.32) | collective-permute-done | bytes 262176 | tf_op jit(solution)/shard_map/ppermute | solution.py:1242
  479.1 2.7 pad_maximum_fusion.1
  486.0 5.1 finish.3
  492.5 13.5 %small_sum.1 = f32[2,128]{1,0:T(2,128)} custom-call(f32[8,2,128]{2,1,0:T(2,128)} %add_bitcast_fusion.x_ref), custom_call_target="tpu_custom_call" | custom-call | flops 1048576 | bytes 1048576 | tf_op jit(solution)/shard_map/small_sum/pallas_call | solution.py:374
  506.1 2.3 pad_maximum_fusion.3
  513.9 6.7 %settle.1 = bf16[12,256,1024]{2,1,0:T(8,128)(2,1)} custom-call(s32[13]{0:T(128)} %pad_add_fusion.3.table_ref, bf16[1,8,64,1024]{3,2,1,0:T(8,128)(2,1)} %bitcast.188, bf16[1,8,64,1024]{3,2,1,0:T(8,128)(2,1)} %collective-permute-done.33.refs_1_, bf16[2,8,64,1024]{3,2,1,0:T(8,128)(2,1)} %collective-permute-done.36.refs_2_, bf16[1,4,64,1024]{3,2,1,0:T(8,128)(2,1)} %bitcast.192, ...), custom_call_target="tpu_custom_call" | custom-call | tf_op jit(solution)/shard_map/settle/pallas_call | solution.py:1745
  (374 shorter events, 101.7 us)
Async XLA Ops:
  7.2 50.0 %copy-start = (bf16[1024,1024]{1,0:T(8,128)(2,1)S(1)}, bf16[1024,1024]{1,0:T(8,128)(2,1)}, u32[]{:S(2)}) copy-start(bf16[1024,1024]{1,0:T(8,128)(2,1)} %param.21) | copy-start | bytes 6291460
  7.2 68.3 %all-gather.4.cloned.1.call-start = ((), (), s32[]{:S(2)}) async-start(), calls=%async_computation.2 | async-start | bytes 7864320 | tf_op jit(solution)/shard_map/all_gather | solution.py:1291
  7.9 158.7 %all-gather.6.cloned.1.call-start = ((), (), s32[]{:S(2)}) async-start(), calls=%async_computation.3 | async-start | bytes 5242880 | tf_op jit(solution)/shard_map/all_gather | solution.py:1533
  10.9 90.9 %copy-start.42 = (s32[8]{0:T(128)}, s32[8]{0:T(128)S(1)}, u32[]{:S(2)}) copy-start(s32[8]{0:T(128)S(1)} %gather_fusion.1) | copy-start | bytes 100
  26.9 27.6 %collective-permute-start = (bf16[4,256,256]{2,1,0:T(8,128)(2,1)}, bf16[4,256,256]{2,1,0:T(8,128)(2,1)}, u32[]{:S(2)}, u32[]{:S(2)}) collective-permute-start(bf16[4,256,256]{2,1,0:T(8,128)(2,1)} %slice.258), channel_id=1, source_target_pairs={{0,4},{4,0},{8,12},{12,8},{16,20},{20,16},{24,28},{28,24},{1,5},{5... | collective-permute-start | bytes 1572872 | tf_op jit(solution)/shard_map/ppermute | solution.py:1236
  55.5 14.4 %collective-permute-start.1 = (bf16[2,256,256]{2,1,0:T(8,128)(2,1)S(1)}, bf16[2,256,256]{2,1,0:T(8,128)(2,1)S(1)}, u32[]{:S(2)}, u32[]{:S(2)}) collective-permute-start(bf16[2,256,256]{2,1,0:T(8,128)(2,1)S(1)} %pad_maximum_fusion.11), channel_id=1, source_target_pairs={{0,8},{4,12},{8,0},{12,4},{16,24},{20,28},{24,16},{28,20},{1,9},{5... | collective-permute-start | bytes 786440 | tf_op jit(solution)/shard_map/ppermute | solution.py:1242
  57.0 13.0 %collective-permute-start.2 = (bf16[4,256,256]{2,1,0:T(8,128)(2,1)S(1)}, bf16[4,256,256]{2,1,0:T(8,128)(2,1)S(1)}, u32[]{:S(2)}, u32[]{:S(2)}) collective-permute-start(bf16[4,256,256]{2,1,0:T(8,128)(2,1)S(1)} %slice.262), channel_id=1, source_target_pairs={{0,4},{4,0},{8,12},{12,8},{16,20},{20,16},{24,28},{28,24},{1,5},{5... | collective-permute-start | bytes 1572872 | tf_op jit(solution)/shard_map/ppermute | solution.py:1236
  73.2 21.1 %collective-permute-start.3 = (bf16[2,256,256]{2,1,0:T(8,128)(2,1)}, bf16[2,256,256]{2,1,0:T(8,128)(2,1)}, u32[]{:S(2)}, u32[]{:S(2)}) collective-permute-start(bf16[2,256,256]{2,1,0:T(8,128)(2,1)} %pad_maximum_fusion.12), channel_id=1, source_target_pairs={{0,16},{4,20},{8,24},{12,28},{16,0},{20,4},{24,8},{28,12},{1,17},{... | collective-permute-start | bytes 786440 | tf_op jit(solution)/shard_map/ppermute | solution.py:1242
  74.0 23.8 %collective-permute-start.4 = (bf16[2,256,256]{2,1,0:T(8,128)(2,1)}, bf16[2,256,256]{2,1,0:T(8,128)(2,1)}, u32[]{:S(2)}, u32[]{:S(2)}) collective-permute-start(bf16[2,256,256]{2,1,0:T(8,128)(2,1)} %pad_maximum_fusion.13), channel_id=1, source_target_pairs={{0,24},{4,28},{8,16},{12,20},{16,8},{20,12},{24,0},{28,4},{1,25},{... | collective-permute-start | bytes 786440 | tf_op jit(solution)/shard_map/ppermute | solution.py:1242
  101.8 115.3 %all-gather.8.cloned.1.call-start = ((), (), s32[]{:S(2)}) async-start(), calls=%async_computation.4 | async-start | bytes 5242880 | tf_op jit(solution)/shard_map/all_gather | solution.py:1547
  103.0 33.1 %collective-permute-start.5 = (bf16[2,256,256]{2,1,0:T(8,128)(2,1)}, bf16[2,256,256]{2,1,0:T(8,128)(2,1)S(1)}, u32[]{:S(2)}, u32[]{:S(2)}) collective-permute-start(bf16[2,256,256]{2,1,0:T(8,128)(2,1)} %pad_maximum_fusion.14), channel_id=1, source_target_pairs={{0,8},{4,12},{8,0},{12,4},{16,24},{20,28},{24,16},{28,20},{1,9},{5... | collective-permute-start | bytes 786440 | tf_op jit(solution)/shard_map/ppermute | solution.py:1242
  103.7 32.4 %collective-permute-start.6 = (bf16[2,256,256]{2,1,0:T(8,128)(2,1)}, bf16[2,256,256]{2,1,0:T(8,128)(2,1)}, u32[]{:S(2)}, u32[]{:S(2)}) collective-permute-start(bf16[2,256,256]{2,1,0:T(8,128)(2,1)} %pad_maximum_fusion.15), channel_id=1, source_target_pairs={{0,16},{4,20},{8,24},{12,28},{16,0},{20,4},{24,8},{28,12},{1,17},{... | collective-permute-start | bytes 786440 | tf_op jit(solution)/shard_map/ppermute | solution.py:1242
  106.5 29.7 %collective-permute-start.7 = (bf16[2,256,256]{2,1,0:T(8,128)(2,1)}, bf16[2,256,256]{2,1,0:T(8,128)(2,1)}, u32[]{:S(2)}, u32[]{:S(2)}) collective-permute-start(bf16[2,256,256]{2,1,0:T(8,128)(2,1)} %pad_maximum_fusion.16), channel_id=1, source_target_pairs={{0,24},{4,28},{8,16},{12,20},{16,8},{20,12},{24,0},{28,4},{1,25},{... | collective-permute-start | bytes 786440 | tf_op jit(solution)/shard_map/ppermute | solution.py:1242
  141.8 245.5 %reduce-scatter.3.cloned.1.call-start = ((), (), s32[]{:S(2)}) async-start(), calls=%async_computation.5 | async-start | bytes 7864320 | tf_op jit(solution)/shard_map/reduce_scatter | solution.py:1560
  143.2 28.9 %copy-start.39 = (s32[8,256]{1,0:T(8,128)}, s32[8,256]{1,0:T(8,128)S(1)}, u32[]{:S(2)}) copy-start(s32[8,256]{1,0:T(8,128)S(1)} %reshape.725.first_ref) | copy-start | bytes 24580
  143.2 29.0 %copy-start.40 = (s32[8,256]{1,0:T(8,128)}, s32[8,256]{1,0:T(8,128)S(1)}, u32[]{:S(2)}) copy-start(s32[8,256]{1,0:T(8,128)S(1)} %reshape.724.first_ref) | copy-start | bytes 24580
  147.3 19.3 %collective-permute-start.8 = (bf16[4,6,64,256]{3,2,1,0:T(8,128)(2,1)S(1)}, bf16[4,6,64,256]{3,2,1,0:T(8,128)(2,1)}, u32[]{:S(2)}, u32[]{:S(2)}) collective-permute-start(bf16[4,6,64,256]{3,2,1,0:T(8,128)(2,1)S(1)} %slice.274), channel_id=1, source_target_pairs={{0,4},{4,0},{8,12},{12,8},{16,20},{20,16},{24,28},{28,24},{1,5},{5... | collective-permute-start | bytes 2359304 | tf_op jit(solution)/shard_map/ppermute | solution.py:1236
  167.9 293.9 %reduce-scatter.5.cloned.1.call-start = ((), (), s32[]{:S(2)}) async-start(), calls=%async_computation.6 | async-start | bytes 7864320 | tf_op jit(solution)/shard_map/reduce_scatter | solution.py:1650
  172.0 77.3 %collective-permute-start.12 = (bf16[4,144,2048]{2,1,0:T(8,128)(2,1)}, bf16[4,144,2048]{2,1,0:T(8,128)(2,1)}, u32[]{:S(2)}, u32[]{:S(2)}) collective-permute-start(bf16[4,144,2048]{2,1,0:T(8,128)(2,1)} %pad_maximum_fusion), channel_id=1, source_target_pairs={{0,4},{4,0},{8,12},{12,8},{16,20},{20,16},{24,28},{28,24},{1,5},{5... | collective-permute-start | bytes 7077896 | tf_op jit(solution)/shard_map/ppermute | solution.py:432
  175.2 42.0 %collective-permute-start.9 = (bf16[2,6,64,256]{3,2,1,0:T(8,128)(2,1)}, bf16[2,6,64,256]{3,2,1,0:T(8,128)(2,1)}, u32[]{:S(2)}, u32[]{:S(2)}) collective-permute-start(bf16[2,6,64,256]{3,2,1,0:T(8,128)(2,1)} %pad_maximum_fusion.5), channel_id=1, source_target_pairs={{0,8},{4,12},{8,0},{12,4},{16,24},{20,28},{24,16},{28,20},{1,9},{5... | collective-permute-start | bytes 1179656 | tf_op jit(solution)/shard_map/ppermute | solution.py:1242
  176.0 41.2 %collective-permute-start.10 = (bf16[2,6,64,256]{3,2,1,0:T(8,128)(2,1)}, bf16[2,6,64,256]{3,2,1,0:T(8,128)(2,1)}, u32[]{:S(2)}, u32[]{:S(2)}) collective-permute-start(bf16[2,6,64,256]{3,2,1,0:T(8,128)(2,1)} %pad_maximum_fusion.6), channel_id=1, source_target_pairs={{0,16},{4,20},{8,24},{12,28},{16,0},{20,4},{24,8},{28,12},{1,17},{... | collective-permute-start | bytes 1179656 | tf_op jit(solution)/shard_map/ppermute | solution.py:1242
  178.9 38.3 %collective-permute-start.11 = (bf16[2,6,64,256]{3,2,1,0:T(8,128)(2,1)}, bf16[2,6,64,256]{3,2,1,0:T(8,128)(2,1)}, u32[]{:S(2)}, u32[]{:S(2)}) collective-permute-start(bf16[2,6,64,256]{3,2,1,0:T(8,128)(2,1)} %pad_maximum_fusion.7), channel_id=1, source_target_pairs={{0,24},{4,28},{8,16},{12,20},{16,8},{20,12},{24,0},{28,4},{1,25},{... | collective-permute-start | bytes 1179656 | tf_op jit(solution)/shard_map/ppermute | solution.py:1242
  251.7 33.3 %collective-permute-start.14 = (bf16[2,144,2048]{2,1,0:T(8,128)(2,1)S(1)}, bf16[2,144,2048]{2,1,0:T(8,128)(2,1)S(1)}, u32[]{:S(2)}, u32[]{:S(2)}) collective-permute-start(bf16[2,144,2048]{2,1,0:T(8,128)(2,1)S(1)} %pad_maximum_fusion.2), channel_id=1, source_target_pairs={{0,8},{4,12},{8,0},{12,4},{16,24},{20,28},{24,16},{28,20},{1,9},{5... | collective-permute-start | bytes 3538952 | tf_op jit(solution)/shard_map/ppermute | solution.py:432
  252.8 32.3 %collective-permute-start.13 = (bf16[4,6,64,256]{3,2,1,0:T(8,128)(2,1)S(1)}, bf16[4,6,64,256]{3,2,1,0:T(8,128)(2,1)S(1)}, u32[]{:S(2)}, u32[]{:S(2)}) collective-permute-start(bf16[4,6,64,256]{3,2,1,0:T(8,128)(2,1)S(1)} %slice.289), channel_id=1, source_target_pairs={{0,4},{4,0},{8,12},{12,8},{16,20},{20,16},{24,28},{28,24},{1,5},{5... | collective-permute-start | bytes 2359304 | tf_op jit(solution)/shard_map/ppermute | solution.py:1236
  285.1 55.1 %copy-start.17 = (bf16[2,144,2048]{2,1,0:T(8,128)(2,1)}, bf16[2,144,2048]{2,1,0:T(8,128)(2,1)S(1)}, u32[]{:S(2)}) copy-start(bf16[2,144,2048]{2,1,0:T(8,128)(2,1)S(1)} %collective-permute-done.14) | copy-start | bytes 3538948
  285.2 42.1 %collective-permute-start.15 = (bf16[2,6,64,256]{3,2,1,0:T(8,128)(2,1)S(1)}, bf16[2,6,64,256]{3,2,1,0:T(8,128)(2,1)}, u32[]{:S(2)}, u32[]{:S(2)}) collective-permute-start(bf16[2,6,64,256]{3,2,1,0:T(8,128)(2,1)S(1)} %pad_maximum_fusion.8), channel_id=1, source_target_pairs={{0,8},{4,12},{8,0},{12,4},{16,24},{20,28},{24,16},{28,20},{1,9},{5... | collective-permute-start | bytes 1179656 | tf_op jit(solution)/shard_map/ppermute | solution.py:1242
  286.1 41.3 %collective-permute-start.16 = (bf16[2,6,64,256]{3,2,1,0:T(8,128)(2,1)S(1)}, bf16[2,6,64,256]{3,2,1,0:T(8,128)(2,1)}, u32[]{:S(2)}, u32[]{:S(2)}) collective-permute-start(bf16[2,6,64,256]{3,2,1,0:T(8,128)(2,1)S(1)} %pad_maximum_fusion.9), channel_id=1, source_target_pairs={{0,16},{4,20},{8,24},{12,28},{16,0},{20,4},{24,8},{28,12},{1,17},{... | collective-permute-start | bytes 1179656 | tf_op jit(solution)/shard_map/ppermute | solution.py:1242
  286.2 41.2 %collective-permute-start.17 = (bf16[2,6,64,256]{3,2,1,0:T(8,128)(2,1)S(1)}, bf16[2,6,64,256]{3,2,1,0:T(8,128)(2,1)S(1)}, u32[]{:S(2)}, u32[]{:S(2)}) collective-permute-start(bf16[2,6,64,256]{3,2,1,0:T(8,128)(2,1)S(1)} %pad_maximum_fusion.10), channel_id=1, source_target_pairs={{0,24},{4,28},{8,16},{12,20},{16,8},{20,12},{24,0},{28,4},{1,25},{... | collective-permute-start | bytes 1179656 | tf_op jit(solution)/shard_map/ppermute | solution.py:1242
  327.4 8.5 %collective-permute-start.18 = (bf16[2,8,64,1024]{3,2,1,0:T(8,128)(2,1)}, bf16[2,8,64,1024]{3,2,1,0:T(8,128)(2,1)}, u32[]{:S(2)}, u32[]{:S(2)}) collective-permute-start(bf16[2,8,64,1024]{3,2,1,0:T(8,128)(2,1)} %get-tuple-element.205), channel_id=1, source_target_pairs={{0,1},{1,0},{2,3},{3,2},{4,5},{5,4},{6,7},{7,6},{8,9},{9,8},{10,11... | collective-permute-start | bytes 6291464 | tf_op jit(solution)/shard_map/ppermute | solution.py:1607
  338.9 30.5 %collective-permute-start.19 = (bf16[1,8,64,1024]{3,2,1,0:T(8,128)(2,1)}, bf16[1,8,64,1024]{3,2,1,0:T(8,128)(2,1)}, u32[]{:S(2)}, u32[]{:S(2)}) collective-permute-start(bf16[1,8,64,1024]{3,2,1,0:T(8,128)(2,1)} %add_convert_fusion.4), channel_id=1, source_target_pairs={{0,2},{1,3},{2,0},{3,1},{4,6},{5,7},{6,4},{7,5},{8,10},{9,11},{10,... | collective-permute-start | bytes 3145736 | tf_op jit(solution)/shard_map/ppermute | solution.py:432
  342.3 29.4 %collective-permute-start.20 = (bf16[1,144,2048]{2,1,0:T(8,128)(2,1)}, bf16[1,144,2048]{2,1,0:T(8,128)(2,1)S(1)}, u32[]{:S(2)}, u32[]{:S(2)}) collective-permute-start(bf16[1,144,2048]{2,1,0:T(8,128)(2,1)} %add_convert_fusion.6), channel_id=1, source_target_pairs={{0,16},{4,20},{8,24},{12,28},{16,0},{20,4},{24,8},{28,12},{1,17},{... | collective-permute-start | bytes 1769480 | tf_op jit(solution)/shard_map/ppermute | solution.py:432
  371.8 15.4 %collective-permute-start.21 = (bf16[2,8,64,1024]{3,2,1,0:T(8,128)(2,1)S(1)}, bf16[2,8,64,1024]{3,2,1,0:T(8,128)(2,1)}, u32[]{:S(2)}, u32[]{:S(2)}) collective-permute-start(bf16[2,8,64,1024]{3,2,1,0:T(8,128)(2,1)S(1)} %copy-done.52), channel_id=1, source_target_pairs={{0,1},{1,0},{2,3},{3,2},{4,5},{5,4},{6,7},{7,6},{8,9},{9,8},{10,11... | collective-permute-start | bytes 6291464 | tf_op jit(solution)/shard_map/ppermute | solution.py:1625
  372.9 14.4 %collective-permute-start.22 = (bf16[4,64,1024]{2,1,0:T(8,128)(2,1)S(1)}, bf16[4,64,1024]{2,1,0:T(8,128)(2,1)S(1)}, u32[]{:S(2)}, u32[]{:S(2)}) collective-permute-start(bf16[4,64,1024]{2,1,0:T(8,128)(2,1)S(1)} %slice.306), channel_id=1, source_target_pairs={{0,4},{4,0},{8,12},{12,8},{16,20},{20,16},{24,28},{28,24},{1,5},{5... | collective-permute-start | bytes 1572872 | tf_op jit(solution)/shard_map/ppermute | solution.py:1236
  394.8 34.6 %collective-permute-start.26 = (bf16[1,8,64,1024]{3,2,1,0:T(8,128)(2,1)S(1)}, bf16[1,8,64,1024]{3,2,1,0:T(8,128)(2,1)S(1)}, u32[]{:S(2)}, u32[]{:S(2)}) collective-permute-start(bf16[1,8,64,1024]{3,2,1,0:T(8,128)(2,1)S(1)} %add_convert_fusion.2), channel_id=1, source_target_pairs={{0,2},{1,3},{2,0},{3,1},{4,6},{5,7},{6,4},{7,5},{8,10},{9,11},{10,... | collective-permute-start | bytes 3145736 | tf_op jit(solution)/shard_map/ppermute | solution.py:432
  396.0 35.3 %collective-permute-start.27 = (bf16[4,1024,128]{2,1,0:T(8,128)(2,1)S(1)}, bf16[4,1024,128]{2,1,0:T(8,128)(2,1)S(1)}, u32[]{:S(2)}, u32[]{:S(2)}) collective-permute-start(bf16[4,1024,128]{2,1,0:T(8,128)(2,1)S(1)} %maximum_maximum_fusion), channel_id=1, source_target_pairs={{0,4},{4,0},{8,12},{12,8},{16,20},{20,16},{24,28},{28,24},{1,5},{5... | collective-permute-start | bytes 3145736 | tf_op jit(solution)/shard_map/ppermute | solution.py:432
  397.2 34.0 %collective-permute-start.23 = (bf16[2,64,1024]{2,1,0:T(8,128)(2,1)S(1)}, bf16[2,64,1024]{2,1,0:T(8,128)(2,1)S(1)}, u32[]{:S(2)}, u32[]{:S(2)}) collective-permute-start(bf16[2,64,1024]{2,1,0:T(8,128)(2,1)S(1)} %pad_maximum_fusion.17), channel_id=1, source_target_pairs={{0,8},{4,12},{8,0},{12,4},{16,24},{20,28},{24,16},{28,20},{1,9},{5... | collective-permute-start | bytes 786440 | tf_op jit(solution)/shard_map/ppermute | solution.py:1242
  397.3 33.9 %collective-permute-start.24 = (bf16[2,64,1024]{2,1,0:T(8,128)(2,1)S(1)}, bf16[2,64,1024]{2,1,0:T(8,128)(2,1)S(1)}, u32[]{:S(2)}, u32[]{:S(2)}) collective-permute-start(bf16[2,64,1024]{2,1,0:T(8,128)(2,1)S(1)} %pad_maximum_fusion.18), channel_id=1, source_target_pairs={{0,16},{4,20},{8,24},{12,28},{16,0},{20,4},{24,8},{28,12},{1,17},{... | collective-permute-start | bytes 786440 | tf_op jit(solution)/shard_map/ppermute | solution.py:1242
  397.4 33.8 %collective-permute-start.25 = (bf16[2,64,1024]{2,1,0:T(8,128)(2,1)S(1)}, bf16[2,64,1024]{2,1,0:T(8,128)(2,1)S(1)}, u32[]{:S(2)}, u32[]{:S(2)}) collective-permute-start(bf16[2,64,1024]{2,1,0:T(8,128)(2,1)S(1)} %pad_maximum_fusion.19), channel_id=1, source_target_pairs={{0,24},{4,28},{8,16},{12,20},{16,8},{20,12},{24,0},{28,4},{1,25},{... | collective-permute-start | bytes 786440 | tf_op jit(solution)/shard_map/ppermute | solution.py:1242
  431.5 11.2 %collective-permute-start.29 = (bf16[2,1024,128]{2,1,0:T(8,128)(2,1)S(1)}, bf16[2,1024,128]{2,1,0:T(8,128)(2,1)S(1)}, u32[]{:S(2)}, u32[]{:S(2)}) collective-permute-start(bf16[2,1024,128]{2,1,0:T(8,128)(2,1)S(1)} %pad_maximum_fusion.4), channel_id=1, source_target_pairs={{0,8},{4,12},{8,0},{12,4},{16,24},{20,28},{24,16},{28,20},{1,9},{5... | collective-permute-start | bytes 1572872 | tf_op jit(solution)/shard_map/ppermute | solution.py:432
  431.6 11.2 %collective-permute-start.28 = (bf16[4,64,1024]{2,1,0:T(8,128)(2,1)S(1)}, bf16[4,64,1024]{2,1,0:T(8,128)(2,1)S(1)}, u32[]{:S(2)}, u32[]{:S(2)}) collective-permute-start(bf16[4,64,1024]{2,1,0:T(8,128)(2,1)S(1)} %slice.319), channel_id=1, source_target_pairs={{0,4},{4,0},{8,12},{12,8},{16,20},{20,16},{24,28},{28,24},{1,5},{5... | collective-permute-start | bytes 1572872 | tf_op jit(solution)/shard_map/ppermute | solution.py:1236
  442.9 11.2 %collective-permute-start.34 = (bf16[1,1024,128]{2,1,0:T(8,128)(2,1)S(1)}, bf16[1,1024,128]{2,1,0:T(8,128)(2,1)S(1)}, u32[]{:S(2)}, u32[]{:S(2)}) collective-permute-start(bf16[1,1024,128]{2,1,0:T(8,128)(2,1)S(1)} %fusion.31), channel_id=1, source_target_pairs={{0,16},{4,20},{8,24},{12,28},{16,0},{20,4},{24,8},{28,12},{1,17},{... | collective-permute-start | bytes 786440 | tf_op jit(solution)/shard_map/ppermute | solution.py:432
  443.0 36.1 %collective-permute-start.33 = (bf16[1,8,64,1024]{3,2,1,0:T(8,128)(2,1)}, bf16[1,8,64,1024]{3,2,1,0:T(8,128)(2,1)}, u32[]{:S(2)}, u32[]{:S(2)}) collective-permute-start(bf16[1,8,64,1024]{3,2,1,0:T(8,128)(2,1)} %bitcast.187), channel_id=1, source_target_pairs={{0,2},{1,3},{2,0},{3,1},{4,6},{5,7},{6,4},{7,5},{8,10},{9,11},{10,... | collective-permute-start | bytes 3145736 | tf_op jit(solution)/shard_map/ppermute | solution.py:453
  444.0 21.5 %collective-permute-start.30 = (bf16[2,64,1024]{2,1,0:T(8,128)(2,1)}, bf16[2,64,1024]{2,1,0:T(8,128)(2,1)S(1)}, u32[]{:S(2)}, u32[]{:S(2)}) collective-permute-start(bf16[2,64,1024]{2,1,0:T(8,128)(2,1)} %pad_maximum_fusion.24), channel_id=1, source_target_pairs={{0,8},{4,12},{8,0},{12,4},{16,24},{20,28},{24,16},{28,20},{1,9},{5... | collective-permute-start | bytes 786440 | tf_op jit(solution)/shard_map/ppermute | solution.py:1242
  445.8 24.6 %collective-permute-start.31 = (bf16[2,64,1024]{2,1,0:T(8,128)(2,1)}, bf16[2,64,1024]{2,1,0:T(8,128)(2,1)S(1)}, u32[]{:S(2)}, u32[]{:S(2)}) collective-permute-start(bf16[2,64,1024]{2,1,0:T(8,128)(2,1)} %pad_maximum_fusion.25), channel_id=1, source_target_pairs={{0,16},{4,20},{8,24},{12,28},{16,0},{20,4},{24,8},{28,12},{1,17},{... | collective-permute-start | bytes 786440 | tf_op jit(solution)/shard_map/ppermute | solution.py:1242
  448.8 30.3 %collective-permute-start.32 = (bf16[2,64,1024]{2,1,0:T(8,128)(2,1)}, bf16[2,64,1024]{2,1,0:T(8,128)(2,1)}, u32[]{:S(2)}, u32[]{:S(2)}) collective-permute-start(bf16[2,64,1024]{2,1,0:T(8,128)(2,1)} %pad_maximum_fusion.26), channel_id=1, source_target_pairs={{0,24},{4,28},{8,16},{12,20},{16,8},{20,12},{24,0},{28,4},{1,25},{... | collective-permute-start | bytes 786440 | tf_op jit(solution)/shard_map/ppermute | solution.py:1242
  481.8 24.2 %collective-permute-start.36 = (bf16[2,8,64,1024]{3,2,1,0:T(8,128)(2,1)}, bf16[2,8,64,1024]{3,2,1,0:T(8,128)(2,1)}, u32[]{:S(2)}, u32[]{:S(2)}) collective-permute-start(bf16[2,8,64,1024]{3,2,1,0:T(8,128)(2,1)} %pad_maximum_fusion.1), channel_id=1, source_target_pairs={{0,1},{1,0},{2,3},{3,2},{4,5},{5,4},{6,7},{7,6},{8,9},{9,8},{10,11... | collective-permute-start | bytes 6291464 | tf_op jit(solution)/shard_map/ppermute | solution.py:453
  491.1 14.9 %collective-permute-start.35 = (bf16[1,4,64,1024]{3,2,1,0:T(8,128)(2,1)}, bf16[1,4,64,1024]{3,2,1,0:T(8,128)(2,1)S(1)}, u32[]{:S(2)}, u32[]{:S(2)}) collective-permute-start(bf16[1,4,64,1024]{3,2,1,0:T(8,128)(2,1)} %bitcast.190), channel_id=1, source_target_pairs={{0,2},{1,3},{2,0},{3,1},{4,6},{5,7},{6,4},{7,5},{8,10},{9,11},{10,... | collective-permute-start | bytes 1572872 | tf_op jit(solution)/shard_map/ppermute | solution.py:453
  508.4 5.5 %collective-permute-start.37 = (bf16[2,4,64,1024]{3,2,1,0:T(8,128)(2,1)}, bf16[2,4,64,1024]{3,2,1,0:T(8,128)(2,1)}, u32[]{:S(2)}, u32[]{:S(2)}) collective-permute-start(bf16[2,4,64,1024]{3,2,1,0:T(8,128)(2,1)} %pad_maximum_fusion.3), channel_id=1, source_target_pairs={{0,1},{1,0},{2,3},{3,2},{4,5},{5,4},{6,7},{7,6},{8,9},{9,8},{10,11... | collective-permute-start | bytes 3145736 | tf_op jit(solution)/shard_map/ppermute | solution.py:453
  (56 other events, 379.6 us)
Sparse Core Ops, SparseCore 0:
  9.6 48.7 all-gather.3
  101.9 36.3 all-gather.5
  141.9 37.4 all-gather.7
  181.8 57.9 reduce-scatter.2
  387.5 74.3 reduce-scatter.4

commit v3 on v2

--- a/solution.py
+++ b/solution.py
@@ -970,7 +970,7 @@
     normed = x_ref[0]
     normed_ref[...] = normed
     for j in range(3):
-        part = dot(w_ref[j * width : (j + 1) * width, :], normed, ((1,), (1,)))
+        part = dot(w_ref[j].reshape(width, w_ref.shape[3]), normed, ((1,), (1,)))
         if j < 2:
             part = turn(part, cos_ref[...], sin_ref[...], heads)
         if j == 0:
@@ -1137,7 +1137,7 @@
             weight_ref[rows, :] += dot(parts[j], normed_ref[...])
     else:
         weight_ref[...] += dot(grads, normed_ref[...])
-    low = dot(grads.T, w_ref[...]).astype(BF16)
+    low = dot(grads.T, w_ref[...].reshape(3 * width, w_ref.shape[3])).astype(BF16)
     part = low.shape[0] // slices
     for m in range(slices):
         at = lax.bitwise_xor(jnp.int32(m), column)
@@ -1331,9 +1331,6 @@
         return jnp.cos(angle), jnp.sin(angle)
 
     w_heads = jnp.transpose(head_weight, (0, 2, 1)).reshape(3, heads, HD, width)
-    w_own = w_heads.reshape(3 * joined, width)
-    part_at = (rank % 2) * half
-    w_shared = lax.dynamic_slice_in_dim(w_heads, part_at, half, 1).reshape(3 * half * HD, width)
     packs_here = (own_of[rank], shared_of[rank // 2])
     turns = [tables(p) for p in packs_here]
     firsts = [take(first, p).reshape(n, shard) for p in packs_here]
@@ -1346,8 +1343,13 @@
     def lane_at(s, *_):
         return (0, s)
 
-    def project(rows, weight, cosine, sine):
-        h = weight.shape[0] // (3 * HD)
+    def heads_at(h):
+        pieces = heads // h
+        return pl.BlockSpec(
+            (3, h, HD, width), lambda s, me: (0, lax.rem(me[0], jnp.int32(pieces)), 0, 0)
+        )
+
+    def project(rows, h, cosine, sine):
         return pl.pallas_call(
             functools.partial(qkv_kernel, h),
             grid_spec=pltpu.PrefetchScalarGridSpec(
@@ -1357,7 +1359,7 @@
                     pl.BlockSpec(
                         (1, shard, width), lambda s, me: (lax.bitwise_xor(s, me[0]), 0, 0)
                     ),
-                    pl.BlockSpec(weight.shape, whole2),
+                    heads_at(h),
                     pl.BlockSpec((ROT, shard), lane_at),
                     pl.BlockSpec((ROT, shard), lane_at),
                 ],
@@ -1373,7 +1375,7 @@
             compiler_params=params(),
             cost_estimate=COST,
             name="project",
-        )(me, rows, weight, cosine, sine)
+        )(me, rows, w_heads, cosine, sine)
 
     def wide(h):
         return [pltpu.VMEM((h, n, HD, shard), BF16)]
@@ -1440,7 +1442,7 @@
             name="attend_back",
         )(me, lows[c], firsts[c], kept, logsum, qkv, grads)
 
-    def rows_back(grads, normed, weight, cosine, sine, *base):
+    def rows_back(grads, normed, cosine, sine, *base):
         h = grads.shape[0]
         return pl.pallas_call(
             functools.partial(rows_kernel, h, slices),
@@ -1450,7 +1452,7 @@
                 in_specs=[
                     pl.BlockSpec((h, 3, HD, shard), lambda s, *_: (0, 0, 0, s)),
                     pl.BlockSpec((shard, width), lambda s, *_: (s, 0)),
-                    pl.BlockSpec(weight.shape, whole2),
+                    heads_at(h),
                     pl.BlockSpec((ROT, shard), lane_at),
                     pl.BlockSpec((ROT, shard), lane_at),
                 ]
@@ -1474,7 +1476,7 @@
             compiler_params=params(),
             cost_estimate=COST,
             name="rows_back",
-        )(me, grads, normed, weight, cosine, sine, *base)
+        )(me, grads, normed, w_heads, cosine, sine, *base)
 
     pack_spec = pl.BlockSpec((1, shard, width), lambda p, *_: (p, 0, 0))
     normed_low, normed_cols = pl.pallas_call(
@@ -1512,7 +1514,7 @@
     branch_ff = jnp.einsum(
         "psf,fd->psd", active_low, down_weight, preferred_element_type=F32
     ).astype(BF16)
-    own_z, shared_x, branch_ff, send_own, own_x, merge_here, down_here, turns, w_own, w_shared = tie(
+    own_z, shared_x, branch_ff, send_own, own_x, merge_here, down_here, turns, w_heads = tie(
         own_z,
         shared_x,
         branch_ff,
@@ -1521,15 +1523,17 @@
         merge_weight,
         down_weight,
         turns,
-        w_own,
-        w_shared,
+        w_heads,
     )
 
     own_z += exchange_z(send_own, own_x, range(4, n, 2))
     active_grad = jnp.einsum("psd,fd->psf", cot, down_here, preferred_element_type=F32)
     _, gelu_back = jax.vjp(lambda values: jax.nn.gelu(values, approximate=True), hidden)
     hidden_grad = gelu_back(active_grad)[0].astype(BF16)
-    own_z, hidden_grad, send_shared, shared_x = tie(own_z, hidden_grad, send_shared, shared_x)
+    biases = jnp.sum(hidden_grad.astype(F32), axis=(0, 1)), jnp.sum(cot.astype(F32), axis=(0, 1))
+    own_z, hidden_grad, send_shared, shared_x, biases = tie(
+        own_z, hidden_grad, send_shared, shared_x, biases
+    )
     rows_own = lax.all_gather(exchanged(send_own, own_x, own_z), "mlp", axis=2, tiled=True)
 
     shared_z = exchange_z(send_shared, shared_x)
@@ -1555,14 +1559,13 @@
     low_ff = jnp.transpose(low_ff.reshape(packs, slices, sub, width), (1, 0, 2, 3)).reshape(
         slices * packs * sub, width
     )
-    biases = jnp.sum(hidden_grad.astype(F32), axis=(0, 1)), jnp.sum(cot.astype(F32), axis=(0, 1))
     grad_x, send_grad, low_ff, rows_own, biases = tie(grad_x, send_grad, low_ff, rows_own, biases)
     low_ff = lax.psum_scatter(low_ff, "mlp", scatter_dimension=0, tiled=True).reshape(
         packs, sub, width
     )
 
     grad_z = exchange_z(send_grad, grad_x)
-    normed_own, qkv_own = project(rows_own, w_own, *turns[0])
+    normed_own, qkv_own = project(rows_own, heads, *turns[0])
     out_own, kept_own, log_own = attend(0, qkv_own)
     grad_z, out_own, kept_own, log_own, rows_shared = tie(
         grad_z, out_own, kept_own, log_own, rows_shared
@@ -1583,7 +1586,7 @@
         )
     )
     terms_got = cube_send(terms, "seq", n, seq_masks)
-    normed_shared, qkv_shared = project(rows_shared, w_shared, *turns[1])
+    normed_shared, qkv_shared = project(rows_shared, half, *turns[1])
     out_shared, kept_shared, log_shared = attend(1, qkv_shared)
     out_shared, kept_shared, log_shared, grads, terms_got = tie(
         out_shared, kept_shared, log_shared, grads, terms_got
@@ -1597,7 +1600,7 @@
     out_x, back_own, terms_got, send_out = tie(out_x, back_own, terms_got, send_out)
 
     out_z = exchange_z(send_out, out_x)
-    low_kept, low_sent, head_own = rows_back(back_own, normed_own, w_own, *turns[0])
+    low_kept, low_sent, head_own = rows_back(back_own, normed_own, *turns[0])
     back_shared = attend_back(1, kept_shared, log_shared, qkv_shared, grads)
     out_z, low_kept, low_sent, back_shared, send_out, out_x = tie(
         out_z, low_kept, low_sent, back_shared, send_out, out_x
@@ -1609,7 +1612,7 @@
         2 * k: low_kept[k].astype(F32) + low_got[k].astype(F32) for k in range(slices // 2)
     }
     low_own = sum_on(low_terms, "mlp", slices, mlp_masks[1:])
-    low_kept, low_sent, head_all = rows_back(back_shared, normed_shared, w_shared, *turns[1], head_own)
+    low_kept, low_sent, head_all = rows_back(back_shared, normed_shared, *turns[1], head_own)
     attended = take(
         exchanged(send_out, out_x, out_z).reshape(n * (heads + half), HD, shard), units_in
     ).reshape(packs, joined, shard)

time: 537 us -> 529 us (0.985)
  starting transfers between devices: 35.1 us -> 59 us
  Pallas kernels: 211 us -> 189 us
  waiting for transfers between devices: 64.7 us -> 56.1 us
    ppermute x8, starting transfers between devices: 6.3 us -> 17.1 us  [cube_send(): return lax.ppermute(sent, axis, [(i, i ^ masks[0]) for i in range(n)])]
    pallas_call x2, Pallas kernels: 56.7 us -> 46.2 us  [attend_back(): pl.pallas_call(functools.partial(unit_back_kernel, n, shard, c + 1), grid...]
    pallas_call x2, Pallas kernels: 45.7 us -> 35.7 us  [attend(): pl.pallas_call(functools.partial(unit_kernel, n, shard), grid_spec=pltpu....]
    ppermute x18, starting transfers between devices: 17.3 us -> 25.4 us  [exchange_z(): lax.ppermute(jnp.stack([array[k], got[k // 2]]), 'seq', [(i, i ^ k) for i...]
    ppermute x8, waiting for transfers between devices: 36.2 us -> 29.4 us  [cube_send(): return lax.ppermute(sent, axis, [(i, i ^ masks[0]) for i in range(n)])]
    unnamed x147 -> x142, local copies, waits for them, and re-layouts: 29 us -> 29.3 us
  transfers between devices with their start and end apart: 43 -> 43, of which waited for: 9 -> 6; matrix products, arithmetic and copies ran while one was open for 35% -> 35% of each run, Pallas kernels for 39% -> 35%
where the time goes in v3:
time: 529 us; the launch traced here: 520 us
  Pallas kernels  189 us (36%)
  matrix products  81.9 us (15%)
  local copies, waits for them, and re-layouts  69.2 us (13%)
  starting transfers between devices  59 us (11%)
  waiting for transfers between devices  56.1 us (11%)
  other arithmetic  48.4 us (9%)
  between operations  15.8 us (3%)
    pallas_call x2, Pallas kernels, attend_back(): pl.pallas_call(functools.partial(unit_back_kernel, n, shard, c + 1), grid...  46.2 us
    pallas_call x2, Pallas kernels, attend(): pl.pallas_call(functools.partial(unit_kernel, n, shard), grid_spec=pltpu....  35.7 us
    ppermute x8, waiting for transfers between devices, cube_send(): return lax.ppermute(sent, axis, [(i, i ^ masks[0]) for i in range(n)])  29.4 us
    unnamed x142, local copies, waits for them, and re-layouts  29.3 us
    pallas_call x2, Pallas kernels, rows_back(): pl.pallas_call(functools.partial(rows_kernel, h, slices), grid_spec=pltpu...  27.9 us
    ppermute x18, starting transfers between devices, exchange_z(): lax.ppermute(jnp.stack([array[k], got[k // 2]]), 'seq', [(i, i ^ k) for i...  25.4 us
    pallas_call x2, Pallas kernels, project(): pl.pallas_call(functools.partial(qkv_kernel, h), grid_spec=pltpu.Prefetch...  20.9 us
    dot_general x1, matrix products, on_device_pairs(): jnp.einsum('psd,fd->psf', cot, down_here, preferred_element_type=F32)  20.7 us
  transfers between devices with their start and end apart: 43, of which 6 were waited for; matrix products, arithmetic and copies ran while one was open for 35% of the time, Pallas kernels for 35%

profile of v3, /device:TPU:17, one launch (start us, length us, event | category | flops | bytes accessed | tf_op | source)
XLA Modules:
  0.0 519.8 jit_solution(16613351308071316266)
XLA Ops:
  11.4 12.4 %norm.1 = (bf16[12,256,1024]{2,1,0:T(8,128)(2,1)}, bf16[12,256,256]{2,1,0:T(8,128)(2,1)}) custom-call(s32[2]{0:T(128)} %pad_add_fusion.1.me_ref, bf16[12,256,1024]{2,1,0:T(8,128)(2,1)} %refs_3_.1, f32[1,1024]{1,0:T(1,128)} %bitcast.192, f32[1,1024]{1,0:T(1,128)} %bitcast.197), custom_call_target="tpu_custom_call" | custom-call | flops 1048576 | bytes 1048576 | tf_op jit(solution)/shard_map/norm/pallas_call | solution.py:1482
  32.0 12.1 %broadcast_add_fusion = f32[12,256,1024]{2,1,0:T(8,128)} fusion(f32[1024]{0:T(1024)S(1)} %copy-done.53, bf16[12,256,1024]{2,1,0:T(8,128)(2,1)} %get-tuple-element.142, bf16[1024,1024]{1,0:T(8,128)(2,1)} %param.19), kind=kOutput, calls=%fused_computation.24 | convolution fusion | flops 6445596672 | bytes 20975616 | tf_op jit(solution)/shard_map/psd,df->psf/dot_general | solution.py:1507
  44.3 2.6 copy.42
  49.0 2.8 multiply_sine_fusion
  54.5 12.8 %convolution_convert_fusion.1.branch_ref = bf16[12,256,1024]{2,1,0:T(8,128)(2,1)} fusion(bf16[1024,1024]{1,0:T(8,128)(2,1)S(1)} %copy-done, f32[12,256,1024]{2,1,0:T(8,128)} %broadcast_add_fusion), kind=kOutput, calls=%fused_computation.28 | convolution fusion | flops 6473908224 | bytes 20971520 | tf_op jit(solution)/shard_map/psf,fd->psd/dot_general | solution.py:1514
  72.4 20.7 %convert_reduce_fusion.1 = (bf16[1024]{0:T(1024)(128)(2,1)}, bf16[12,256,1024]{2,1,0:T(8,128)(2,1)}) fusion(f32[12,256,1024]{2,1,0:T(8,128)} %broadcast_add_fusion, bf16[12,256,1024]{2,1,0:T(8,128)(2,1)} %all-gather.4.cloned.1.call-done.c_ref.refs_3_.refs_4_, bf16[1024,1024]{1,0:T(8,128)(2,1)S(1)} %copy-done), kind=kOutput, calls=%fused_computation.22 | convolution fusion | flops 6511655936 | bytes 27265024 | tf_op jit(solution)/shard_map/psd,fd->psf/dot_general | solution.py:1530
  100.0 2.4 collective-permute-start.5
  105.0 11.7 %bitcast_convert_fusion.1 = bf16[1024,1024]{1,0:T(8,128)(2,1)} fusion(bf16[12,256,1024]{2,1,0:T(8,128)(2,1)} %get-tuple-element.142, bf16[12,256,1024]{2,1,0:T(8,128)(2,1)} %get-tuple-element.157), kind=kOutput, calls=%fused_computation.26 | convolution fusion | flops 6443499520 | bytes 14680064 | tf_op jit(solution)/shard_map/psd,psf->df/dot_general | solution.py:1544
  116.8 11.0 %fusion.16 = bf16[1024,1024]{1,0:T(8,128)(2,1)} fusion(bf16[12,256,1024]{2,1,0:T(8,128)(2,1)S(1)} %bitcast.170, f32[12,256,1024]{2,1,0:T(8,128)} %broadcast_add_fusion), kind=kOutput, calls=%fused_computation.45 | convolution fusion | flops 6471811072 | bytes 20971520 | tf_op jit(solution)/shard_map/psd,psf->df/dot_general | solution.py:1547
  127.8 3.0 convolution_convert_fusion.2
  130.8 2.1 gather_fusion.5
  141.3 10.5 %convolution_convert_fusion = bf16[12,256,1024]{2,1,0:T(8,128)(2,1)S(1)} fusion(bf16[12,256,1024]{2,1,0:T(8,128)(2,1)} %get-tuple-element.157, bf16[1024,1024]{1,0:T(8,128)(2,1)} %param.19), kind=kOutput, calls=%fused_computation.27 | convolution fusion | flops 6445596672 | bytes 14680064 | tf_op jit(solution)/shard_map/psf,df->psd/dot_general | solution.py:1556
  151.8 3.3 copy.46
  167.3 2.5 collective-permute-start.9
  172.6 10.8 %project.2 = (bf16[2048,1024]{1,0:T(8,128)(2,1)}, bf16[4,3,64,2048]{3,2,1,0:T(8,128)(2,1)}) custom-call(s32[2]{0:T(128)} %pad_add_fusion.1.me_ref, bf16[8,256,1024]{2,1,0:T(8,128)(2,1)} %all-gather.6.cloned.1.call-done.x_ref, bf16[3,4,64,1024]{3,2,1,0:T(8,128)(2,1)} %bitcast.171, f32[32,2048]{1,0:T(8,128)} %get-tuple-element.167.cos_ref, ...), custom_call_target="tpu_custom_call" | custom-call | flops 1048576 | bytes 1048576 | tf_op jit(solution)/shard_map/project/pallas_call | solution.py:1353
  183.4 21.3 %attend.2 = (bf16[8,4,64,256]{3,2,1,0:T(8,128)(2,1)}, bf16[4,8,64,256]{3,2,1,0:T(8,128)(2,1)}, f32[4,8,256]{2,1,0:T(8,128)}) custom-call(s32[2]{0:T(128)} %pad_add_fusion.1.me_ref, s32[8]{0:T(128)} %get-tuple-element.463.low_ref, s32[8,256]{1,0:T(8,128)} %copy-done.40, bf16[4,3,64,2048]{3,2,1,0:T(8,128)(2,1)} %get-tuple-element.169.qkv_ref), custom_call_target="tpu_custom_call" | custom-call | flops 1048576 | bytes 1048576 | tf_op jit(solution)/shard_map/attend/pallas_call | solution.py:1397
  204.8 10.1 %project.3 = (bf16[2048,1024]{1,0:T(8,128)(2,1)}, bf16[2,3,64,2048]{3,2,1,0:T(8,128)(2,1)}) custom-call(s32[2]{0:T(128)} %pad_add_fusion.1.me_ref, bf16[8,256,1024]{2,1,0:T(8,128)(2,1)} %all-gather.8.cloned.1.call-done.x_ref, bf16[3,4,64,1024]{3,2,1,0:T(8,128)(2,1)} %bitcast.172, f32[32,2048]{1,0:T(8,128)} %get-tuple-element.180.cos_ref, ...), custom_call_target="tpu_custom_call" | custom-call | flops 1048576 | bytes 1048576 | tf_op jit(solution)/shard_map/project/pallas_call | solution.py:1353
  214.9 14.4 %attend.3 = (bf16[8,2,64,256]{3,2,1,0:T(8,128)(2,1)}, bf16[2,8,64,256]{3,2,1,0:T(8,128)(2,1)}, f32[2,8,256]{2,1,0:T(8,128)}) custom-call(s32[2]{0:T(128)} %pad_add_fusion.1.me_ref, s32[8]{0:T(128)} %get-tuple-element.462.low_ref, s32[8,256]{1,0:T(8,128)} %copy-done.39, bf16[2,3,64,2048]{3,2,1,0:T(8,128)(2,1)} %get-tuple-element.182.qkv_ref), custom_call_target="tpu_custom_call" | custom-call | flops 1048576 | bytes 1048576 | tf_op jit(solution)/shard_map/attend/pallas_call | solution.py:1397
  232.5 2.2 add_convert_fusion.9
  236.8 27.1 %attend_back.2.grad_ref = bf16[4,3,64,2048]{3,2,1,0:T(8,128)(2,1)} custom-call(s32[2]{0:T(128)} %pad_add_fusion.1.me_ref, s32[8]{0:T(128)} %get-tuple-element.463.low_ref, s32[8,256]{1,0:T(8,128)} %copy-done.40, bf16[4,8,64,256]{3,2,1,0:T(8,128)(2,1)} %get-tuple-element.194.keep_ref, f32[4,8,256]{2,1,0:T(8,128)} %get-tuple-element.195.logsum_ref, ...), custom_call_target="tpu_custom_call" | custom-call | flops 1048576 | bytes 1048576 | tf_op jit(solution)/shard_map/attend_back/pallas_call | solution.py:1424
  264.8 8.5 %collective-permute-start.16 = (bf16[2,6,64,256]{3,2,1,0:T(8,128)(2,1)S(1)}, bf16[2,6,64,256]{3,2,1,0:T(8,128)(2,1)}, u32[]{:S(2)}, u32[]{:S(2)}) collective-permute-start(bf16[2,6,64,256]{3,2,1,0:T(8,128)(2,1)S(1)} %pad_maximum_fusion.9), channel_id=1, source_target_pairs={{0,16},{4,20},{8,24},{12,28},{16,0},{20,4},{24,8},{28,12},{1,17},{... | collective-permute-start | bytes 1179656 | tf_op jit(solution)/shard_map/ppermute | solution.py:1242
  273.7 19.1 %attend_back.3.grad_ref = bf16[2,3,64,2048]{3,2,1,0:T(8,128)(2,1)} custom-call(s32[2]{0:T(128)} %pad_add_fusion.1.me_ref, s32[8]{0:T(128)} %get-tuple-element.462.low_ref, s32[8,256]{1,0:T(8,128)} %copy-done.39, bf16[2,8,64,256]{3,2,1,0:T(8,128)(2,1)} %get-tuple-element.204.keep_ref, f32[2,8,256]{2,1,0:T(8,128)} %get-tuple-element.205.logsum_ref, ...), custom_call_target="tpu_custom_call" | custom-call | flops 1048576 | bytes 1048576 | tf_op jit(solution)/shard_map/attend_back/pallas_call | solution.py:1424
  292.9 14.7 %rows_back.2 = (bf16[2,8,64,1024]{3,2,1,0:T(8,128)(2,1)}, bf16[2,8,64,1024]{3,2,1,0:T(8,128)(2,1)}, f32[768,1024]{1,0:T(8,128)}) custom-call(s32[2]{0:T(128)} %pad_add_fusion.1.me_ref, bf16[4,3,64,2048]{3,2,1,0:T(8,128)(2,1)} %attend_back.2.grad_ref, bf16[2048,1024]{1,0:T(8,128)(2,1)} %get-tuple-element.201.normed_ref, bf16[3,4,64,1024]{3,2,1,0:T(8,128)(2,1)} %bitcast.173, ...), custom_call_target="tpu_custom_call" | custom-call | flops 1048576 | bytes 1048576 | tf_op jit(solution)/shard_map/rows_back/pallas_call | solution.py:1447
  307.6 6.9 %collective-permute-start.18 = (bf16[2,8,64,1024]{3,2,1,0:T(8,128)(2,1)}, bf16[2,8,64,1024]{3,2,1,0:T(8,128)(2,1)}, u32[]{:S(2)}, u32[]{:S(2)}) collective-permute-start(bf16[2,8,64,1024]{3,2,1,0:T(8,128)(2,1)} %get-tuple-element.207), channel_id=1, source_target_pairs={{0,1},{1,0},{2,3},{3,2},{4,5},{5,4},{6,7},{7,6},{8,9},{9,8},{10,11... | collective-permute-start | bytes 6291464 | tf_op jit(solution)/shard_map/ppermute | solution.py:1610
  315.8 2.8 collective-permute-done.18
  318.6 3.0 add_convert_fusion.4
  323.2 2.2 add_convert_fusion.6
  325.4 12.2 %collective-permute-start.20 = (bf16[1,144,2048]{2,1,0:T(8,128)(2,1)}, bf16[1,144,2048]{2,1,0:T(8,128)(2,1)}, u32[]{:S(2)}, u32[]{:S(2)}) collective-permute-start(bf16[1,144,2048]{2,1,0:T(8,128)(2,1)} %add_convert_fusion.6), channel_id=1, source_target_pairs={{0,16},{4,20},{8,24},{12,28},{16,0},{20,4},{24,8},{28,12},{1,17},{... | collective-permute-start | bytes 1769480 | tf_op jit(solution)/shard_map/ppermute | solution.py:432
  344.2 3.3 gather_fusion.6
  347.5 13.2 %rows_back.3 = (bf16[2,8,64,1024]{3,2,1,0:T(8,128)(2,1)}, bf16[2,8,64,1024]{3,2,1,0:T(8,128)(2,1)}, f32[768,1024]{1,0:T(8,128)}) custom-call(s32[2]{0:T(128)} %pad_add_fusion.1.me_ref, bf16[2,3,64,2048]{3,2,1,0:T(8,128)(2,1)} %attend_back.3.grad_ref, bf16[2048,1024]{1,0:T(8,128)(2,1)} %get-tuple-element.211.normed_ref, bf16[3,4,64,1024]{3,2,1,0:T(8,128)(2,1)} %bitcast.174, ...), custom_call_target="tpu_custom_call" | custom-call | flops 1048576 | bytes 1048576 | tf_op jit(solution)/shard_map/rows_back/pallas_call | solution.py:1447
  360.7 2.3 fusion.19
  364.5 13.7 %join.1 = (bf16[4,12,256,256]{3,2,1,0:T(8,128)(2,1)}, f32[256,1024]{1,0:T(8,128)}) custom-call(bf16[12,256,256]{2,1,0:T(8,128)(2,1)} %bitcast.177, bf16[12,256,1024]{2,1,0:T(8,128)(2,1)} %all-gather.4.cloned.1.call-done.c_ref.refs_3_.refs_4_, bf16[256,1024]{1,0:T(8,128)(2,1)} %merge_ref.1, bf16[12,256,1024]{2,1,0:T(8,128)(2,1)} %convolution_convert_fusion.1.branch_ref), custom_call_target="tpu_custom_call" | custom-call | flops 1048576 | bytes 1048576 | tf_op jit(solution)/shard_map/join/pallas_call | solution.py:1629
  382.6 3.0 convert_add_fusion.1
  386.2 2.2 copy-done.31
  391.5 2.7 collective-permute-start.25
  394.3 26.4 %collective-permute-done.26 = bf16[1,8,64,1024]{3,2,1,0:T(8,128)(2,1)S(1)} collective-permute-done((bf16[1,8,64,1024]{3,2,1,0:T(8,128)(2,1)S(1)}, bf16[1,8,64,1024]{3,2,1,0:T(8,128)(2,1)S(1)}, u32[]{:S(2)}, u32[]{:S(2)}) %collective-permute-start.26) | collective-permute-done | bytes 1048608 | tf_op jit(solution)/shard_map/ppermute | solution.py:432
  425.7 8.1 %finish.2 = (bf16[8,64,1024]{2,1,0:T(8,128)(2,1)}, f32[2,1024]{1,0:T(2,128)}) custom-call(s32[24]{0:T(128)} %pad_add_fusion.2.which_ref, bf16[8,64,1024]{2,1,0:T(8,128)(2,1)} %copy-done.19, bf16[12,64,1024]{2,1,0:T(8,128)(2,1)} %bitcast.180, bf16[12,256,1024]{2,1,0:T(8,128)(2,1)} %refs_3_.1, ...), custom_call_target="tpu_custom_call" | custom-call | flops 1048576 | bytes 1048576 | tf_op jit(solution)/shard_map/finish/pallas_call | solution.py:1683
  437.6 2.3 collective-permute-start.31
  440.7 3.0 collective-permute-done.34
  443.8 9.7 %reduce-scatter.5.cloned.1.call-done = bf16[1,12,256,256]{3,2,1,0:T(8,128)(2,1)} async-done(((bf16[4,12,256,256]{3,2,1,0:T(8,128)(2,1)}), bf16[1,12,256,256]{3,2,1,0:T(8,128)(2,1)}) %reduce-scatter.5.cloned.1.call-update) | async-done | bytes 1572880 | tf_op jit(solution)/shard_map/reduce_scatter | solution.py:1653
  453.5 3.6 fusion.11
  457.1 4.2 collective-permute-done.31
  461.3 9.0 %collective-permute-done.32 = bf16[2,64,1024]{2,1,0:T(8,128)(2,1)} collective-permute-done((bf16[2,64,1024]{2,1,0:T(8,128)(2,1)}, bf16[2,64,1024]{2,1,0:T(8,128)(2,1)}, u32[]{:S(2)}, u32[]{:S(2)}) %collective-permute-start.32) | collective-permute-done | bytes 262176 | tf_op jit(solution)/shard_map/ppermute | solution.py:1242
  470.4 2.7 pad_maximum_fusion.1
  478.1 5.1 finish.3
  485.3 12.8 %small_sum.1 = f32[2,128]{1,0:T(2,128)} custom-call(f32[8,2,128]{2,1,0:T(2,128)} %add_bitcast_fusion.x_ref), custom_call_target="tpu_custom_call" | custom-call | flops 1048576 | bytes 1048576 | tf_op jit(solution)/shard_map/small_sum/pallas_call | solution.py:374
  498.1 2.3 pad_maximum_fusion.3
  506.1 6.7 %settle.1 = bf16[12,256,1024]{2,1,0:T(8,128)(2,1)} custom-call(s32[13]{0:T(128)} %pad_add_fusion.3.table_ref, bf16[1,8,64,1024]{3,2,1,0:T(8,128)(2,1)} %bitcast.183, bf16[1,8,64,1024]{3,2,1,0:T(8,128)(2,1)} %collective-permute-done.33.refs_1_, bf16[2,8,64,1024]{3,2,1,0:T(8,128)(2,1)} %collective-permute-done.36.refs_2_, bf16[1,4,64,1024]{3,2,1,0:T(8,128)(2,1)} %bitcast.187, ...), custom_call_target="tpu_custom_call" | custom-call | tf_op jit(solution)/shard_map/settle/pallas_call | solution.py:1748
  (367 shorter events, 102.5 us)
Async XLA Ops:
  7.2 47.3 %copy-start = (bf16[1024,1024]{1,0:T(8,128)(2,1)S(1)}, bf16[1024,1024]{1,0:T(8,128)(2,1)}, u32[]{:S(2)}) copy-start(bf16[1024,1024]{1,0:T(8,128)(2,1)} %param.21) | copy-start | bytes 6291460
  7.2 65.2 %all-gather.4.cloned.1.call-start = ((), (), s32[]{:S(2)}) async-start(), calls=%async_computation.2 | async-start | bytes 7864320 | tf_op jit(solution)/shard_map/all_gather | solution.py:1291
  7.9 150.5 %all-gather.6.cloned.1.call-start = ((), (), s32[]{:S(2)}) async-start(), calls=%async_computation.3 | async-start | bytes 5242880 | tf_op jit(solution)/shard_map/all_gather | solution.py:1537
  10.8 88.0 %copy-start.44 = (s32[8]{0:T(128)}, s32[8]{0:T(128)S(1)}, u32[]{:S(2)}) copy-start(s32[8]{0:T(128)S(1)} %gather_fusion.1) | copy-start | bytes 100
  26.8 24.9 %collective-permute-start = (bf16[4,256,256]{2,1,0:T(8,128)(2,1)}, bf16[4,256,256]{2,1,0:T(8,128)(2,1)}, u32[]{:S(2)}, u32[]{:S(2)}) collective-permute-start(bf16[4,256,256]{2,1,0:T(8,128)(2,1)} %slice.258), channel_id=1, source_target_pairs={{0,4},{4,0},{8,12},{12,8},{16,20},{20,16},{24,28},{28,24},{1,5},{5... | collective-permute-start | bytes 1572872 | tf_op jit(solution)/shard_map/ppermute | solution.py:1236
  52.7 14.6 %collective-permute-start.1 = (bf16[2,256,256]{2,1,0:T(8,128)(2,1)S(1)}, bf16[2,256,256]{2,1,0:T(8,128)(2,1)S(1)}, u32[]{:S(2)}, u32[]{:S(2)}) collective-permute-start(bf16[2,256,256]{2,1,0:T(8,128)(2,1)S(1)} %pad_maximum_fusion.11), channel_id=1, source_target_pairs={{0,8},{4,12},{8,0},{12,4},{16,24},{20,28},{24,16},{28,20},{1,9},{5... | collective-permute-start | bytes 786440 | tf_op jit(solution)/shard_map/ppermute | solution.py:1242
  54.1 13.1 %collective-permute-start.2 = (bf16[4,256,256]{2,1,0:T(8,128)(2,1)S(1)}, bf16[4,256,256]{2,1,0:T(8,128)(2,1)S(1)}, u32[]{:S(2)}, u32[]{:S(2)}) collective-permute-start(bf16[4,256,256]{2,1,0:T(8,128)(2,1)S(1)} %slice.262), channel_id=1, source_target_pairs={{0,4},{4,0},{8,12},{12,8},{16,20},{20,16},{24,28},{28,24},{1,5},{5... | collective-permute-start | bytes 1572872 | tf_op jit(solution)/shard_map/ppermute | solution.py:1236
  70.5 24.2 %collective-permute-start.3 = (bf16[2,256,256]{2,1,0:T(8,128)(2,1)}, bf16[2,256,256]{2,1,0:T(8,128)(2,1)}, u32[]{:S(2)}, u32[]{:S(2)}) collective-permute-start(bf16[2,256,256]{2,1,0:T(8,128)(2,1)} %pad_maximum_fusion.12), channel_id=1, source_target_pairs={{0,16},{4,20},{8,24},{12,28},{16,0},{20,4},{24,8},{28,12},{1,17},{... | collective-permute-start | bytes 786440 | tf_op jit(solution)/shard_map/ppermute | solution.py:1242
  71.3 23.5 %collective-permute-start.4 = (bf16[2,256,256]{2,1,0:T(8,128)(2,1)}, bf16[2,256,256]{2,1,0:T(8,128)(2,1)}, u32[]{:S(2)}, u32[]{:S(2)}) collective-permute-start(bf16[2,256,256]{2,1,0:T(8,128)(2,1)} %pad_maximum_fusion.13), channel_id=1, source_target_pairs={{0,24},{4,28},{8,16},{12,20},{16,8},{20,12},{24,0},{28,4},{1,25},{... | collective-permute-start | bytes 786440 | tf_op jit(solution)/shard_map/ppermute | solution.py:1242
  98.8 105.9 %all-gather.8.cloned.1.call-start = ((), (), s32[]{:S(2)}) async-start(), calls=%async_computation.4 | async-start | bytes 5242880 | tf_op jit(solution)/shard_map/all_gather | solution.py:1551
  100.0 32.9 %collective-permute-start.5 = (bf16[2,256,256]{2,1,0:T(8,128)(2,1)}, bf16[2,256,256]{2,1,0:T(8,128)(2,1)S(1)}, u32[]{:S(2)}, u32[]{:S(2)}) collective-permute-start(bf16[2,256,256]{2,1,0:T(8,128)(2,1)} %pad_maximum_fusion.14), channel_id=1, source_target_pairs={{0,8},{4,12},{8,0},{12,4},{16,24},{20,28},{24,16},{28,20},{1,9},{5... | collective-permute-start | bytes 786440 | tf_op jit(solution)/shard_map/ppermute | solution.py:1242
  103.1 29.8 %collective-permute-start.6 = (bf16[2,256,256]{2,1,0:T(8,128)(2,1)}, bf16[2,256,256]{2,1,0:T(8,128)(2,1)}, u32[]{:S(2)}, u32[]{:S(2)}) collective-permute-start(bf16[2,256,256]{2,1,0:T(8,128)(2,1)} %pad_maximum_fusion.15), channel_id=1, source_target_pairs={{0,16},{4,20},{8,24},{12,28},{16,0},{20,4},{24,8},{28,12},{1,17},{... | collective-permute-start | bytes 786440 | tf_op jit(solution)/shard_map/ppermute | solution.py:1242
  103.9 29.0 %collective-permute-start.7 = (bf16[2,256,256]{2,1,0:T(8,128)(2,1)}, bf16[2,256,256]{2,1,0:T(8,128)(2,1)}, u32[]{:S(2)}, u32[]{:S(2)}) collective-permute-start(bf16[2,256,256]{2,1,0:T(8,128)(2,1)} %pad_maximum_fusion.16), channel_id=1, source_target_pairs={{0,24},{4,28},{8,16},{12,20},{16,8},{20,12},{24,0},{28,4},{1,25},{... | collective-permute-start | bytes 786440 | tf_op jit(solution)/shard_map/ppermute | solution.py:1242
  138.5 239.9 %reduce-scatter.3.cloned.1.call-start = ((), (), s32[]{:S(2)}) async-start(), calls=%async_computation.5 | async-start | bytes 7864320 | tf_op jit(solution)/shard_map/reduce_scatter | solution.py:1563
  139.9 24.4 %copy-start.39 = (s32[8,256]{1,0:T(8,128)}, s32[8,256]{1,0:T(8,128)S(1)}, u32[]{:S(2)}) copy-start(s32[8,256]{1,0:T(8,128)S(1)} %reshape.721.first_ref) | copy-start | bytes 24580
  139.9 24.5 %copy-start.40 = (s32[8,256]{1,0:T(8,128)}, s32[8,256]{1,0:T(8,128)S(1)}, u32[]{:S(2)}) copy-start(s32[8,256]{1,0:T(8,128)S(1)} %reshape.720.first_ref) | copy-start | bytes 24580
  140.0 18.4 %collective-permute-start.8 = (bf16[4,6,64,256]{3,2,1,0:T(8,128)(2,1)S(1)}, bf16[4,6,64,256]{3,2,1,0:T(8,128)(2,1)}, u32[]{:S(2)}, u32[]{:S(2)}) collective-permute-start(bf16[4,6,64,256]{3,2,1,0:T(8,128)(2,1)S(1)} %slice.274), channel_id=1, source_target_pairs={{0,4},{4,0},{8,12},{12,8},{16,20},{20,16},{24,28},{28,24},{1,5},{5... | collective-permute-start | bytes 2359304 | tf_op jit(solution)/shard_map/ppermute | solution.py:1236
  159.8 293.7 %reduce-scatter.5.cloned.1.call-start = ((), (), s32[]{:S(2)}) async-start(), calls=%async_computation.6 | async-start | bytes 7864320 | tf_op jit(solution)/shard_map/reduce_scatter | solution.py:1653
  163.9 68.6 %collective-permute-start.12 = (bf16[4,144,2048]{2,1,0:T(8,128)(2,1)}, bf16[4,144,2048]{2,1,0:T(8,128)(2,1)}, u32[]{:S(2)}, u32[]{:S(2)}) collective-permute-start(bf16[4,144,2048]{2,1,0:T(8,128)(2,1)} %pad_maximum_fusion), channel_id=1, source_target_pairs={{0,4},{4,0},{8,12},{12,8},{16,20},{20,16},{24,28},{28,24},{1,5},{5... | collective-permute-start | bytes 7077896 | tf_op jit(solution)/shard_map/ppermute | solution.py:432
  167.3 37.4 %collective-permute-start.9 = (bf16[2,6,64,256]{3,2,1,0:T(8,128)(2,1)}, bf16[2,6,64,256]{3,2,1,0:T(8,128)(2,1)}, u32[]{:S(2)}, u32[]{:S(2)}) collective-permute-start(bf16[2,6,64,256]{3,2,1,0:T(8,128)(2,1)} %pad_maximum_fusion.5), channel_id=1, source_target_pairs={{0,8},{4,12},{8,0},{12,4},{16,24},{20,28},{24,16},{28,20},{1,9},{5... | collective-permute-start | bytes 1179656 | tf_op jit(solution)/shard_map/ppermute | solution.py:1242
  170.6 34.2 %collective-permute-start.10 = (bf16[2,6,64,256]{3,2,1,0:T(8,128)(2,1)}, bf16[2,6,64,256]{3,2,1,0:T(8,128)(2,1)}, u32[]{:S(2)}, u32[]{:S(2)}) collective-permute-start(bf16[2,6,64,256]{3,2,1,0:T(8,128)(2,1)} %pad_maximum_fusion.6), channel_id=1, source_target_pairs={{0,16},{4,20},{8,24},{12,28},{16,0},{20,4},{24,8},{28,12},{1,17},{... | collective-permute-start | bytes 1179656 | tf_op jit(solution)/shard_map/ppermute | solution.py:1242
  171.4 33.4 %collective-permute-start.11 = (bf16[2,6,64,256]{3,2,1,0:T(8,128)(2,1)}, bf16[2,6,64,256]{3,2,1,0:T(8,128)(2,1)}, u32[]{:S(2)}, u32[]{:S(2)}) collective-permute-start(bf16[2,6,64,256]{3,2,1,0:T(8,128)(2,1)} %pad_maximum_fusion.7), channel_id=1, source_target_pairs={{0,24},{4,28},{8,16},{12,20},{16,8},{20,12},{24,0},{28,4},{1,25},{... | collective-permute-start | bytes 1179656 | tf_op jit(solution)/shard_map/ppermute | solution.py:1242
  234.9 28.9 %collective-permute-start.14 = (bf16[2,144,2048]{2,1,0:T(8,128)(2,1)S(1)}, bf16[2,144,2048]{2,1,0:T(8,128)(2,1)S(1)}, u32[]{:S(2)}, u32[]{:S(2)}) collective-permute-start(bf16[2,144,2048]{2,1,0:T(8,128)(2,1)S(1)} %pad_maximum_fusion.2), channel_id=1, source_target_pairs={{0,8},{4,12},{8,0},{12,4},{16,24},{20,28},{24,16},{28,20},{1,9},{5... | collective-permute-start | bytes 3538952 | tf_op jit(solution)/shard_map/ppermute | solution.py:432
  236.7 27.1 %collective-permute-start.13 = (bf16[4,6,64,256]{3,2,1,0:T(8,128)(2,1)S(1)}, bf16[4,6,64,256]{3,2,1,0:T(8,128)(2,1)S(1)}, u32[]{:S(2)}, u32[]{:S(2)}) collective-permute-start(bf16[4,6,64,256]{3,2,1,0:T(8,128)(2,1)S(1)} %slice.289), channel_id=1, source_target_pairs={{0,4},{4,0},{8,12},{12,8},{16,20},{20,16},{24,28},{28,24},{1,5},{5... | collective-permute-start | bytes 2359304 | tf_op jit(solution)/shard_map/ppermute | solution.py:1236
  263.8 59.4 %copy-start.20 = (bf16[2,144,2048]{2,1,0:T(8,128)(2,1)}, bf16[2,144,2048]{2,1,0:T(8,128)(2,1)S(1)}, u32[]{:S(2)}) copy-start(bf16[2,144,2048]{2,1,0:T(8,128)(2,1)S(1)} %collective-permute-done.14) | copy-start | bytes 3538948
  264.0 43.6 %collective-permute-start.15 = (bf16[2,6,64,256]{3,2,1,0:T(8,128)(2,1)S(1)}, bf16[2,6,64,256]{3,2,1,0:T(8,128)(2,1)}, u32[]{:S(2)}, u32[]{:S(2)}) collective-permute-start(bf16[2,6,64,256]{3,2,1,0:T(8,128)(2,1)S(1)} %pad_maximum_fusion.8), channel_id=1, source_target_pairs={{0,8},{4,12},{8,0},{12,4},{16,24},{20,28},{24,16},{28,20},{1,9},{5... | collective-permute-start | bytes 1179656 | tf_op jit(solution)/shard_map/ppermute | solution.py:1242
  264.8 42.8 %collective-permute-start.16 = (bf16[2,6,64,256]{3,2,1,0:T(8,128)(2,1)S(1)}, bf16[2,6,64,256]{3,2,1,0:T(8,128)(2,1)}, u32[]{:S(2)}, u32[]{:S(2)}) collective-permute-start(bf16[2,6,64,256]{3,2,1,0:T(8,128)(2,1)S(1)} %pad_maximum_fusion.9), channel_id=1, source_target_pairs={{0,16},{4,20},{8,24},{12,28},{16,0},{20,4},{24,8},{28,12},{1,17},{... | collective-permute-start | bytes 1179656 | tf_op jit(solution)/shard_map/ppermute | solution.py:1242
  273.4 34.2 %collective-permute-start.17 = (bf16[2,6,64,256]{3,2,1,0:T(8,128)(2,1)S(1)}, bf16[2,6,64,256]{3,2,1,0:T(8,128)(2,1)S(1)}, u32[]{:S(2)}, u32[]{:S(2)}) collective-permute-start(bf16[2,6,64,256]{3,2,1,0:T(8,128)(2,1)S(1)} %pad_maximum_fusion.10), channel_id=1, source_target_pairs={{0,24},{4,28},{8,16},{12,20},{16,8},{20,12},{24,0},{28,4},{1,25},{... | collective-permute-start | bytes 1179656 | tf_op jit(solution)/shard_map/ppermute | solution.py:1242
  307.6 11.0 %collective-permute-start.18 = (bf16[2,8,64,1024]{3,2,1,0:T(8,128)(2,1)}, bf16[2,8,64,1024]{3,2,1,0:T(8,128)(2,1)}, u32[]{:S(2)}, u32[]{:S(2)}) collective-permute-start(bf16[2,8,64,1024]{3,2,1,0:T(8,128)(2,1)} %get-tuple-element.207), channel_id=1, source_target_pairs={{0,1},{1,0},{2,3},{3,2},{4,5},{5,4},{6,7},{7,6},{8,9},{9,8},{10,11... | collective-permute-start | bytes 6291464 | tf_op jit(solution)/shard_map/ppermute | solution.py:1610
  321.6 39.1 %collective-permute-start.19 = (bf16[1,8,64,1024]{3,2,1,0:T(8,128)(2,1)}, bf16[1,8,64,1024]{3,2,1,0:T(8,128)(2,1)}, u32[]{:S(2)}, u32[]{:S(2)}) collective-permute-start(bf16[1,8,64,1024]{3,2,1,0:T(8,128)(2,1)} %add_convert_fusion.4), channel_id=1, source_target_pairs={{0,2},{1,3},{2,0},{3,1},{4,6},{5,7},{6,4},{7,5},{8,10},{9,11},{10,... | collective-permute-start | bytes 3145736 | tf_op jit(solution)/shard_map/ppermute | solution.py:432
  325.4 37.7 %collective-permute-start.20 = (bf16[1,144,2048]{2,1,0:T(8,128)(2,1)}, bf16[1,144,2048]{2,1,0:T(8,128)(2,1)}, u32[]{:S(2)}, u32[]{:S(2)}) collective-permute-start(bf16[1,144,2048]{2,1,0:T(8,128)(2,1)} %add_convert_fusion.6), channel_id=1, source_target_pairs={{0,16},{4,20},{8,24},{12,28},{16,0},{20,4},{24,8},{28,12},{1,17},{... | collective-permute-start | bytes 1769480 | tf_op jit(solution)/shard_map/ppermute | solution.py:432
  363.1 15.2 %collective-permute-start.21 = (bf16[2,8,64,1024]{3,2,1,0:T(8,128)(2,1)S(1)}, bf16[2,8,64,1024]{3,2,1,0:T(8,128)(2,1)S(1)}, u32[]{:S(2)}, u32[]{:S(2)}) collective-permute-start(bf16[2,8,64,1024]{3,2,1,0:T(8,128)(2,1)S(1)} %copy-done.52), channel_id=1, source_target_pairs={{0,1},{1,0},{2,3},{3,2},{4,5},{5,4},{6,7},{7,6},{8,9},{9,8},{10,11... | collective-permute-start | bytes 6291464 | tf_op jit(solution)/shard_map/ppermute | solution.py:1628
  364.1 14.2 %collective-permute-start.22 = (bf16[4,64,1024]{2,1,0:T(8,128)(2,1)S(1)}, bf16[4,64,1024]{2,1,0:T(8,128)(2,1)}, u32[]{:S(2)}, u32[]{:S(2)}) collective-permute-start(bf16[4,64,1024]{2,1,0:T(8,128)(2,1)S(1)} %slice.306), channel_id=1, source_target_pairs={{0,4},{4,0},{8,12},{12,8},{16,20},{20,16},{24,28},{28,24},{1,5},{5... | collective-permute-start | bytes 1572872 | tf_op jit(solution)/shard_map/ppermute | solution.py:1236
  386.1 34.6 %collective-permute-start.26 = (bf16[1,8,64,1024]{3,2,1,0:T(8,128)(2,1)S(1)}, bf16[1,8,64,1024]{3,2,1,0:T(8,128)(2,1)S(1)}, u32[]{:S(2)}, u32[]{:S(2)}) collective-permute-start(bf16[1,8,64,1024]{3,2,1,0:T(8,128)(2,1)S(1)} %add_convert_fusion.2), channel_id=1, source_target_pairs={{0,2},{1,3},{2,0},{3,1},{4,6},{5,7},{6,4},{7,5},{8,10},{9,11},{10,... | collective-permute-start | bytes 3145736 | tf_op jit(solution)/shard_map/ppermute | solution.py:432
  388.9 32.5 %collective-permute-start.27 = (bf16[4,1024,128]{2,1,0:T(8,128)(2,1)S(1)}, bf16[4,1024,128]{2,1,0:T(8,128)(2,1)S(1)}, u32[]{:S(2)}, u32[]{:S(2)}) collective-permute-start(bf16[4,1024,128]{2,1,0:T(8,128)(2,1)S(1)} %maximum_maximum_fusion), channel_id=1, source_target_pairs={{0,4},{4,0},{8,12},{12,8},{16,20},{20,16},{24,28},{28,24},{1,5},{5... | collective-permute-start | bytes 3145736 | tf_op jit(solution)/shard_map/ppermute | solution.py:432
  391.3 30.1 %collective-permute-start.23 = (bf16[2,64,1024]{2,1,0:T(8,128)(2,1)S(1)}, bf16[2,64,1024]{2,1,0:T(8,128)(2,1)S(1)}, u32[]{:S(2)}, u32[]{:S(2)}) collective-permute-start(bf16[2,64,1024]{2,1,0:T(8,128)(2,1)S(1)} %pad_maximum_fusion.17), channel_id=1, source_target_pairs={{0,8},{4,12},{8,0},{12,4},{16,24},{20,28},{24,16},{28,20},{1,9},{5... | collective-permute-start | bytes 786440 | tf_op jit(solution)/shard_map/ppermute | solution.py:1242
  391.4 30.0 %collective-permute-start.24 = (bf16[2,64,1024]{2,1,0:T(8,128)(2,1)S(1)}, bf16[2,64,1024]{2,1,0:T(8,128)(2,1)S(1)}, u32[]{:S(2)}, u32[]{:S(2)}) collective-permute-start(bf16[2,64,1024]{2,1,0:T(8,128)(2,1)S(1)} %pad_maximum_fusion.18), channel_id=1, source_target_pairs={{0,16},{4,20},{8,24},{12,28},{16,0},{20,4},{24,8},{28,12},{1,17},{... | collective-permute-start | bytes 786440 | tf_op jit(solution)/shard_map/ppermute | solution.py:1242
  391.5 29.9 %collective-permute-start.25 = (bf16[2,64,1024]{2,1,0:T(8,128)(2,1)S(1)}, bf16[2,64,1024]{2,1,0:T(8,128)(2,1)S(1)}, u32[]{:S(2)}, u32[]{:S(2)}) collective-permute-start(bf16[2,64,1024]{2,1,0:T(8,128)(2,1)S(1)} %pad_maximum_fusion.19), channel_id=1, source_target_pairs={{0,24},{4,28},{8,16},{12,20},{16,8},{20,12},{24,0},{28,4},{1,25},{... | collective-permute-start | bytes 786440 | tf_op jit(solution)/shard_map/ppermute | solution.py:1242
  422.5 11.3 %collective-permute-start.29 = (bf16[2,1024,128]{2,1,0:T(8,128)(2,1)}, bf16[2,1024,128]{2,1,0:T(8,128)(2,1)S(1)}, u32[]{:S(2)}, u32[]{:S(2)}) collective-permute-start(bf16[2,1024,128]{2,1,0:T(8,128)(2,1)} %pad_maximum_fusion.4), channel_id=1, source_target_pairs={{0,8},{4,12},{8,0},{12,4},{16,24},{20,28},{24,16},{28,20},{1,9},{5... | collective-permute-start | bytes 1572872 | tf_op jit(solution)/shard_map/ppermute | solution.py:432
  422.5 11.3 %collective-permute-start.28 = (bf16[4,64,1024]{2,1,0:T(8,128)(2,1)S(1)}, bf16[4,64,1024]{2,1,0:T(8,128)(2,1)S(1)}, u32[]{:S(2)}, u32[]{:S(2)}) collective-permute-start(bf16[4,64,1024]{2,1,0:T(8,128)(2,1)S(1)} %slice.319), channel_id=1, source_target_pairs={{0,4},{4,0},{8,12},{12,8},{16,20},{20,16},{24,28},{28,24},{1,5},{5... | collective-permute-start | bytes 1572872 | tf_op jit(solution)/shard_map/ppermute | solution.py:1236
  433.9 9.8 %collective-permute-start.34 = (bf16[1,1024,128]{2,1,0:T(8,128)(2,1)S(1)}, bf16[1,1024,128]{2,1,0:T(8,128)(2,1)S(1)}, u32[]{:S(2)}, u32[]{:S(2)}) collective-permute-start(bf16[1,1024,128]{2,1,0:T(8,128)(2,1)S(1)} %fusion.31), channel_id=1, source_target_pairs={{0,16},{4,20},{8,24},{12,28},{16,0},{20,4},{24,8},{28,12},{1,17},{... | collective-permute-start | bytes 786440 | tf_op jit(solution)/shard_map/ppermute | solution.py:432
  434.0 36.4 %collective-permute-start.33 = (bf16[1,8,64,1024]{3,2,1,0:T(8,128)(2,1)}, bf16[1,8,64,1024]{3,2,1,0:T(8,128)(2,1)}, u32[]{:S(2)}, u32[]{:S(2)}) collective-permute-start(bf16[1,8,64,1024]{3,2,1,0:T(8,128)(2,1)} %bitcast.182), channel_id=1, source_target_pairs={{0,2},{1,3},{2,0},{3,1},{4,6},{5,7},{6,4},{7,5},{8,10},{9,11},{10,... | collective-permute-start | bytes 3145736 | tf_op jit(solution)/shard_map/ppermute | solution.py:453
  436.0 21.1 %collective-permute-start.30 = (bf16[2,64,1024]{2,1,0:T(8,128)(2,1)}, bf16[2,64,1024]{2,1,0:T(8,128)(2,1)S(1)}, u32[]{:S(2)}, u32[]{:S(2)}) collective-permute-start(bf16[2,64,1024]{2,1,0:T(8,128)(2,1)} %pad_maximum_fusion.24), channel_id=1, source_target_pairs={{0,8},{4,12},{8,0},{12,4},{16,24},{20,28},{24,16},{28,20},{1,9},{5... | collective-permute-start | bytes 786440 | tf_op jit(solution)/shard_map/ppermute | solution.py:1242
  437.6 23.7 %collective-permute-start.31 = (bf16[2,64,1024]{2,1,0:T(8,128)(2,1)}, bf16[2,64,1024]{2,1,0:T(8,128)(2,1)}, u32[]{:S(2)}, u32[]{:S(2)}) collective-permute-start(bf16[2,64,1024]{2,1,0:T(8,128)(2,1)} %pad_maximum_fusion.25), channel_id=1, source_target_pairs={{0,16},{4,20},{8,24},{12,28},{16,0},{20,4},{24,8},{28,12},{1,17},{... | collective-permute-start | bytes 786440 | tf_op jit(solution)/shard_map/ppermute | solution.py:1242
  440.7 29.7 %collective-permute-start.32 = (bf16[2,64,1024]{2,1,0:T(8,128)(2,1)}, bf16[2,64,1024]{2,1,0:T(8,128)(2,1)}, u32[]{:S(2)}, u32[]{:S(2)}) collective-permute-start(bf16[2,64,1024]{2,1,0:T(8,128)(2,1)} %pad_maximum_fusion.26), channel_id=1, source_target_pairs={{0,24},{4,28},{8,16},{12,20},{16,8},{20,12},{24,0},{28,4},{1,25},{... | collective-permute-start | bytes 786440 | tf_op jit(solution)/shard_map/ppermute | solution.py:1242
  473.1 25.0 %collective-permute-start.36 = (bf16[2,8,64,1024]{3,2,1,0:T(8,128)(2,1)}, bf16[2,8,64,1024]{3,2,1,0:T(8,128)(2,1)}, u32[]{:S(2)}, u32[]{:S(2)}) collective-permute-start(bf16[2,8,64,1024]{3,2,1,0:T(8,128)(2,1)} %pad_maximum_fusion.1), channel_id=1, source_target_pairs={{0,1},{1,0},{2,3},{3,2},{4,5},{5,4},{6,7},{7,6},{8,9},{9,8},{10,11... | collective-permute-start | bytes 6291464 | tf_op jit(solution)/shard_map/ppermute | solution.py:453
  483.1 14.9 %collective-permute-start.35 = (bf16[1,4,64,1024]{3,2,1,0:T(8,128)(2,1)}, bf16[1,4,64,1024]{3,2,1,0:T(8,128)(2,1)S(1)}, u32[]{:S(2)}, u32[]{:S(2)}) collective-permute-start(bf16[1,4,64,1024]{3,2,1,0:T(8,128)(2,1)} %bitcast.185), channel_id=1, source_target_pairs={{0,2},{1,3},{2,0},{3,1},{4,6},{5,7},{6,4},{7,5},{8,10},{9,11},{10,... | collective-permute-start | bytes 1572872 | tf_op jit(solution)/shard_map/ppermute | solution.py:453
  500.4 5.6 %collective-permute-start.37 = (bf16[2,4,64,1024]{3,2,1,0:T(8,128)(2,1)}, bf16[2,4,64,1024]{3,2,1,0:T(8,128)(2,1)}, u32[]{:S(2)}, u32[]{:S(2)}) collective-permute-start(bf16[2,4,64,1024]{3,2,1,0:T(8,128)(2,1)} %pad_maximum_fusion.3), channel_id=1, source_target_pairs={{0,1},{1,0},{2,3},{3,2},{4,5},{5,4},{6,7},{7,6},{8,9},{9,8},{10,11... | collective-permute-start | bytes 3145736 | tf_op jit(solution)/shard_map/ppermute | solution.py:453
  (54 other events, 382.1 us)
Sparse Core Ops, SparseCore 0:
  9.6 48.6 all-gather.3
  99.0 39.0 all-gather.5
  139.6 39.8 all-gather.7
  181.9 57.9 reduce-scatter.2
  378.5 74.9 reduce-scatter.4

commit v4 on v3

--- a/solution.py
+++ b/solution.py
@@ -1044,9 +1044,12 @@
 
 
 def unit_back_kernel(
-    n, block, by, me_ref, low_ref, first_ref, keep_ref, logsum_ref, qkv_ref, grad_ref, out_ref,
-    qt, kt, gt, qn, kn, vn, gn, dk, dv, dqs
+    n, block, by, me_ref, low_ref, first_ref, keep_ref, logsum_ref, qkv_ref, *refs
 ):
+    out_ref, qt, kt, gt, qn, kn, vn, gn, dk, dv, dqs = refs[-11:]
+    grads = [(refs[0], 0), (refs[1], 0)]
+    for ref in refs[2:-11]:
+        grads += [(ref, 0), (ref, 1)]
     me = me_ref[0]
     pair = range(qkv_ref.shape[0])
     for u in pair:
@@ -1059,7 +1062,7 @@
                 n_ref[u, i] = part.T
         for k in range(n):
             d = lax.bitwise_xor(jnp.int32(k), me)
-            part = grad_ref[k, u]
+            part = grads[k][0][grads[k][1], u]
             gt[u, d] = part
             gn[u, d] = part.T
     dk[...] = jnp.zeros_like(dk)
@@ -1431,7 +1434,12 @@
                     keep_spec(step),
                     log_spec(step),
                     unit_spec(step),
-                    pl.BlockSpec((n, step, HD, shard), lambda u, *_: (0, u + skip, 0, 0)),
+                ]
+                + [
+                    pl.BlockSpec(
+                        (1 if at < 2 else 2, step, HD, shard), lambda u, *_: (0, u + skip, 0, 0)
+                    )
+                    for at in range(len(grads))
                 ],
                 out_specs=unit_spec(step),
                 scratch_shapes=wide(step) * 3 + tall(step) * 4 + tall(step, F32) * 2 + wide(step),
@@ -1440,7 +1448,7 @@
             compiler_params=params(),
             cost_estimate=COST,
             name="attend_back",
-        )(me, lows[c], firsts[c], kept, logsum, qkv, grads)
+        )(me, lows[c], firsts[c], kept, logsum, qkv, *grads)
 
     def rows_back(grads, normed, cosine, sine, *base):
         h = grads.shape[0]
@@ -1570,7 +1578,7 @@
     grad_z, out_own, kept_own, log_own, rows_shared = tie(
         grad_z, out_own, kept_own, log_own, rows_shared
     )
-    grads = exchanged(send_grad, grad_x, grad_z)
+    grads = [send_grad, grad_x, *grad_z]
 
     def with_row(*parts):
         weight = jnp.concatenate(parts[:2], axis=1)

time: 529 us -> 522 us (0.987)
    unnamed x142 -> x140, local copies, waits for them, and re-layouts: 29.3 us -> 25.1 us
  transfers between devices with their start and end apart: 43 -> 43, of which waited for: 6 -> 8; matrix products, arithmetic and copies ran while one was open for 35% -> 35% of each run, Pallas kernels for 35% -> 35%
where the time goes in v4:
time: 522 us; the launch traced here: 513 us
  Pallas kernels  187 us (36%)
  matrix products  81.9 us (16%)
  local copies, waits for them, and re-layouts  64.6 us (12%)
  waiting for transfers between devices  58.2 us (11%)
  starting transfers between devices  57.5 us (11%)
  other arithmetic  48 us (9%)
  between operations  15.7 us (3%)
    pallas_call x2, Pallas kernels, attend_back(): pl.pallas_call(functools.partial(unit_back_kernel, n, shard, c + 1), grid...  45.1 us
    pallas_call x2, Pallas kernels, attend(): pl.pallas_call(functools.partial(unit_kernel, n, shard), grid_spec=pltpu....  34.9 us
    ppermute x8, waiting for transfers between devices, cube_send(): return lax.ppermute(sent, axis, [(i, i ^ masks[0]) for i in range(n)])  31.4 us
    pallas_call x2, Pallas kernels, rows_back(): pl.pallas_call(functools.partial(rows_kernel, h, slices), grid_spec=pltpu...  28 us
    unnamed x140, local copies, waits for them, and re-layouts  25.1 us
    ppermute x18, starting transfers between devices, exchange_z(): lax.ppermute(jnp.stack([array[k], got[k // 2]]), 'seq', [(i, i ^ k) for i...  22.2 us
    pallas_call x2, Pallas kernels, project(): pl.pallas_call(functools.partial(qkv_kernel, h), grid_spec=pltpu.Prefetch...  21 us
    dot_general x1, matrix products, on_device_pairs(): jnp.einsum('psd,fd->psf', cot, down_here, preferred_element_type=F32)  20.1 us
  transfers between devices with their start and end apart: 43, of which 8 were waited for; matrix products, arithmetic and copies ran while one was open for 35% of the time, Pallas kernels for 35%

profile of v4, /device:TPU:17, one launch (start us, length us, event | category | flops | bytes accessed | tf_op | source)
XLA Modules:
  0.0 513.5 jit_solution(3399365412170303389)
XLA Ops:
  11.5 12.4 %norm.1 = (bf16[12,256,1024]{2,1,0:T(8,128)(2,1)}, bf16[12,256,256]{2,1,0:T(8,128)(2,1)}) custom-call(s32[2]{0:T(128)} %pad_add_fusion.1.me_ref, bf16[12,256,1024]{2,1,0:T(8,128)(2,1)} %refs_3_.1, f32[1,1024]{1,0:T(1,128)} %bitcast.194, f32[1,1024]{1,0:T(1,128)} %bitcast.199), custom_call_target="tpu_custom_call" | custom-call | flops 1048576 | bytes 1048576 | tf_op jit(solution)/shard_map/norm/pallas_call | solution.py:1490
  23.9 2.1 gather_fusion.2
  32.2 12.1 %broadcast_add_fusion = f32[12,256,1024]{2,1,0:T(8,128)} fusion(f32[1024]{0:T(1024)S(1)} %copy-done.54, bf16[12,256,1024]{2,1,0:T(8,128)(2,1)} %get-tuple-element.146, bf16[1024,1024]{1,0:T(8,128)(2,1)} %param.19), kind=kOutput, calls=%fused_computation.24 | convolution fusion | flops 6445596672 | bytes 20975616 | tf_op jit(solution)/shard_map/psd,df->psf/dot_general | solution.py:1515
  44.4 2.6 copy.42
  47.0 2.1 gather_fusion.4
  49.1 2.8 multiply_sine_fusion
  54.6 12.9 %convolution_convert_fusion.1.branch_ref = bf16[12,256,1024]{2,1,0:T(8,128)(2,1)} fusion(bf16[1024,1024]{1,0:T(8,128)(2,1)S(1)} %copy-done, f32[12,256,1024]{2,1,0:T(8,128)} %broadcast_add_fusion), kind=kOutput, calls=%fused_computation.28 | convolution fusion | flops 6473908224 | bytes 20971520 | tf_op jit(solution)/shard_map/psf,fd->psd/dot_general | solution.py:1522
  72.7 20.1 %convert_reduce_fusion.1 = (bf16[1024]{0:T(1024)(128)(2,1)S(1)}, bf16[12,256,1024]{2,1,0:T(8,128)(2,1)}) fusion(f32[12,256,1024]{2,1,0:T(8,128)} %broadcast_add_fusion, bf16[12,256,1024]{2,1,0:T(8,128)(2,1)} %all-gather.4.cloned.1.call-done.c_ref.refs_3_.refs_4_, bf16[1024,1024]{1,0:T(8,128)(2,1)S(1)} %copy-done), kind=kOutput, calls=%fused_computation.22 | convolution fusion | flops 6511655936 | bytes 27265024 | tf_op jit(solution)/shard_map/psd,fd->psf/dot_general | solution.py:1538
  104.1 12.4 %bitcast_convert_fusion.1 = bf16[1024,1024]{1,0:T(8,128)(2,1)} fusion(bf16[12,256,1024]{2,1,0:T(8,128)(2,1)} %get-tuple-element.146, bf16[12,256,1024]{2,1,0:T(8,128)(2,1)} %get-tuple-element.161), kind=kOutput, calls=%fused_computation.26 | convolution fusion | flops 6443499520 | bytes 14680064 | tf_op jit(solution)/shard_map/psd,psf->df/dot_general | solution.py:1552
  116.5 11.0 %fusion.16 = bf16[1024,1024]{1,0:T(8,128)(2,1)} fusion(bf16[12,256,1024]{2,1,0:T(8,128)(2,1)S(1)} %bitcast.170, f32[12,256,1024]{2,1,0:T(8,128)} %broadcast_add_fusion), kind=kOutput, calls=%fused_computation.45 | convolution fusion | flops 6471811072 | bytes 20971520 | tf_op jit(solution)/shard_map/psd,psf->df/dot_general | solution.py:1555
  127.5 3.0 convolution_convert_fusion.2
  130.5 2.1 gather_fusion.5
  139.6 10.5 %convolution_convert_fusion = bf16[12,256,1024]{2,1,0:T(8,128)(2,1)S(1)} fusion(bf16[12,256,1024]{2,1,0:T(8,128)(2,1)} %get-tuple-element.161, bf16[1024,1024]{1,0:T(8,128)(2,1)} %param.19), kind=kOutput, calls=%fused_computation.27 | convolution fusion | flops 6445596672 | bytes 14680064 | tf_op jit(solution)/shard_map/psf,df->psd/dot_general | solution.py:1564
  150.1 3.5 copy.46
  170.2 10.7 %project.2 = (bf16[2048,1024]{1,0:T(8,128)(2,1)}, bf16[4,3,64,2048]{3,2,1,0:T(8,128)(2,1)}) custom-call(s32[2]{0:T(128)} %pad_add_fusion.1.me_ref, bf16[8,256,1024]{2,1,0:T(8,128)(2,1)} %all-gather.6.cloned.1.call-done.x_ref, bf16[3,4,64,1024]{3,2,1,0:T(8,128)(2,1)} %bitcast.171, f32[32,2048]{1,0:T(8,128)} %get-tuple-element.171.cos_ref, ...), custom_call_target="tpu_custom_call" | custom-call | flops 1048576 | bytes 1048576 | tf_op jit(solution)/shard_map/project/pallas_call | solution.py:1356
  180.9 21.4 %attend.2 = (bf16[8,4,64,256]{3,2,1,0:T(8,128)(2,1)}, bf16[4,8,64,256]{3,2,1,0:T(8,128)(2,1)}, f32[4,8,256]{2,1,0:T(8,128)}) custom-call(s32[2]{0:T(128)} %pad_add_fusion.1.me_ref, s32[8]{0:T(128)} %get-tuple-element.469.low_ref, s32[8,256]{1,0:T(8,128)} %copy-done.41, bf16[4,3,64,2048]{3,2,1,0:T(8,128)(2,1)} %get-tuple-element.173.qkv_ref), custom_call_target="tpu_custom_call" | custom-call | flops 1048576 | bytes 1048576 | tf_op jit(solution)/shard_map/attend/pallas_call | solution.py:1400
  202.5 10.2 %project.3 = (bf16[2048,1024]{1,0:T(8,128)(2,1)}, bf16[2,3,64,2048]{3,2,1,0:T(8,128)(2,1)}) custom-call(s32[2]{0:T(128)} %pad_add_fusion.1.me_ref, bf16[8,256,1024]{2,1,0:T(8,128)(2,1)} %all-gather.8.cloned.1.call-done.x_ref, bf16[3,4,64,1024]{3,2,1,0:T(8,128)(2,1)} %bitcast.172, f32[32,2048]{1,0:T(8,128)} %get-tuple-element.184.cos_ref, ...), custom_call_target="tpu_custom_call" | custom-call | flops 1048576 | bytes 1048576 | tf_op jit(solution)/shard_map/project/pallas_call | solution.py:1356
  212.7 13.6 %attend.3 = (bf16[8,2,64,256]{3,2,1,0:T(8,128)(2,1)}, bf16[2,8,64,256]{3,2,1,0:T(8,128)(2,1)}, f32[2,8,256]{2,1,0:T(8,128)}) custom-call(s32[2]{0:T(128)} %pad_add_fusion.1.me_ref, s32[8]{0:T(128)} %get-tuple-element.468.low_ref, s32[8,256]{1,0:T(8,128)} %copy-done.40, bf16[2,3,64,2048]{3,2,1,0:T(8,128)(2,1)} %get-tuple-element.186.qkv_ref), custom_call_target="tpu_custom_call" | custom-call | flops 1048576 | bytes 1048576 | tf_op jit(solution)/shard_map/attend/pallas_call | solution.py:1400
  228.2 3.0 collective-permute-start.14
  232.6 27.1 %attend_back.2.grad_ref = bf16[4,3,64,2048]{3,2,1,0:T(8,128)(2,1)} custom-call(s32[2]{0:T(128)} %pad_add_fusion.1.me_ref, s32[8]{0:T(128)} %get-tuple-element.469.low_ref, s32[8,256]{1,0:T(8,128)} %copy-done.41, bf16[4,8,64,256]{3,2,1,0:T(8,128)(2,1)} %get-tuple-element.198.keep_ref, f32[4,8,256]{2,1,0:T(8,128)} %get-tuple-element.199.logsum_ref, ...), custom_call_target="tpu_custom_call" | custom-call | flops 1048576 | bytes 1048576 | tf_op jit(solution)/shard_map/attend_back/pallas_call | solution.py:1427
  261.8 5.4 %collective-permute-start.16 = (bf16[2,6,64,256]{3,2,1,0:T(8,128)(2,1)S(1)}, bf16[2,6,64,256]{3,2,1,0:T(8,128)(2,1)}, u32[]{:S(2)}, u32[]{:S(2)}) collective-permute-start(bf16[2,6,64,256]{3,2,1,0:T(8,128)(2,1)S(1)} %pad_maximum_fusion.9), channel_id=1, source_target_pairs={{0,16},{4,20},{8,24},{12,28},{16,0},{20,4},{24,8},{28,12},{1,17},{... | collective-permute-start | bytes 1179656 | tf_op jit(solution)/shard_map/ppermute | solution.py:1245
  267.6 18.0 %attend_back.3.grad_ref = bf16[2,3,64,2048]{3,2,1,0:T(8,128)(2,1)} custom-call(s32[2]{0:T(128)} %pad_add_fusion.1.me_ref, s32[8]{0:T(128)} %get-tuple-element.468.low_ref, s32[8,256]{1,0:T(8,128)} %copy-done.40, bf16[2,8,64,256]{3,2,1,0:T(8,128)(2,1)} %get-tuple-element.212.keep_ref, f32[2,8,256]{2,1,0:T(8,128)} %get-tuple-element.213.logsum_ref, ...), custom_call_target="tpu_custom_call" | custom-call | flops 1048576 | bytes 1048576 | tf_op jit(solution)/shard_map/attend_back/pallas_call | solution.py:1427
  285.6 14.7 %rows_back.2 = (bf16[2,8,64,1024]{3,2,1,0:T(8,128)(2,1)}, bf16[2,8,64,1024]{3,2,1,0:T(8,128)(2,1)}, f32[768,1024]{1,0:T(8,128)}) custom-call(s32[2]{0:T(128)} %pad_add_fusion.1.me_ref, bf16[4,3,64,2048]{3,2,1,0:T(8,128)(2,1)} %attend_back.2.grad_ref, bf16[2048,1024]{1,0:T(8,128)(2,1)} %get-tuple-element.209.normed_ref, bf16[3,4,64,1024]{3,2,1,0:T(8,128)(2,1)} %bitcast.173, ...), custom_call_target="tpu_custom_call" | custom-call | flops 1048576 | bytes 1048576 | tf_op jit(solution)/shard_map/rows_back/pallas_call | solution.py:1455
  300.4 5.0 collective-permute-start.18
  307.3 2.3 collective-permute-done.18
  309.6 3.0 add_convert_fusion.4
  314.5 2.2 add_convert_fusion.6
  316.7 13.2 %collective-permute-start.20 = (bf16[1,144,2048]{2,1,0:T(8,128)(2,1)}, bf16[1,144,2048]{2,1,0:T(8,128)(2,1)}, u32[]{:S(2)}, u32[]{:S(2)}) collective-permute-start(bf16[1,144,2048]{2,1,0:T(8,128)(2,1)} %add_convert_fusion.6), channel_id=1, source_target_pairs={{0,16},{4,20},{8,24},{12,28},{16,0},{20,4},{24,8},{28,12},{1,17},{... | collective-permute-start | bytes 1769480 | tf_op jit(solution)/shard_map/ppermute | solution.py:432
  336.5 3.3 gather_fusion.6
  339.8 13.3 %rows_back.3 = (bf16[2,8,64,1024]{3,2,1,0:T(8,128)(2,1)}, bf16[2,8,64,1024]{3,2,1,0:T(8,128)(2,1)}, f32[768,1024]{1,0:T(8,128)}) custom-call(s32[2]{0:T(128)} %pad_add_fusion.1.me_ref, bf16[2,3,64,2048]{3,2,1,0:T(8,128)(2,1)} %attend_back.3.grad_ref, bf16[2048,1024]{1,0:T(8,128)(2,1)} %get-tuple-element.219.normed_ref, bf16[3,4,64,1024]{3,2,1,0:T(8,128)(2,1)} %bitcast.174, ...), custom_call_target="tpu_custom_call" | custom-call | flops 1048576 | bytes 1048576 | tf_op jit(solution)/shard_map/rows_back/pallas_call | solution.py:1455
  353.1 2.3 fusion.19
  357.7 13.7 %join.1 = (bf16[4,12,256,256]{3,2,1,0:T(8,128)(2,1)}, f32[256,1024]{1,0:T(8,128)}) custom-call(bf16[12,256,256]{2,1,0:T(8,128)(2,1)} %bitcast.181, bf16[12,256,1024]{2,1,0:T(8,128)(2,1)} %all-gather.4.cloned.1.call-done.c_ref.refs_3_.refs_4_, bf16[256,1024]{1,0:T(8,128)(2,1)} %merge_ref.1, bf16[12,256,1024]{2,1,0:T(8,128)(2,1)} %convolution_convert_fusion.1.branch_ref), custom_call_target="tpu_custom_call" | custom-call | flops 1048576 | bytes 1048576 | tf_op jit(solution)/shard_map/join/pallas_call | solution.py:1637
  375.9 3.0 convert_add_fusion.1
  379.4 2.2 copy-done.32
  383.9 2.7 collective-permute-start.25
  386.7 28.1 %collective-permute-done.26 = bf16[1,8,64,1024]{3,2,1,0:T(8,128)(2,1)S(1)} collective-permute-done((bf16[1,8,64,1024]{3,2,1,0:T(8,128)(2,1)S(1)}, bf16[1,8,64,1024]{3,2,1,0:T(8,128)(2,1)S(1)}, u32[]{:S(2)}, u32[]{:S(2)}) %collective-permute-start.26) | collective-permute-done | bytes 1048608 | tf_op jit(solution)/shard_map/ppermute | solution.py:432
  418.6 8.1 %finish.2 = (bf16[8,64,1024]{2,1,0:T(8,128)(2,1)}, f32[2,1024]{1,0:T(2,128)}) custom-call(s32[24]{0:T(128)} %pad_add_fusion.2.which_ref, bf16[8,64,1024]{2,1,0:T(8,128)(2,1)} %copy-done.21, bf16[12,64,1024]{2,1,0:T(8,128)(2,1)} %bitcast.182, bf16[12,256,1024]{2,1,0:T(8,128)(2,1)} %refs_3_.1, ...), custom_call_target="tpu_custom_call" | custom-call | flops 1048576 | bytes 1048576 | tf_op jit(solution)/shard_map/finish/pallas_call | solution.py:1691
  431.8 2.3 collective-permute-start.31
  434.8 2.3 collective-permute-done.34
  437.2 8.6 %reduce-scatter.5.cloned.1.call-done = bf16[1,12,256,256]{3,2,1,0:T(8,128)(2,1)} async-done(((bf16[4,12,256,256]{3,2,1,0:T(8,128)(2,1)}), bf16[1,12,256,256]{3,2,1,0:T(8,128)(2,1)}) %reduce-scatter.5.cloned.1.call-update) | async-done | bytes 1572880 | tf_op jit(solution)/shard_map/reduce_scatter | solution.py:1661
  445.9 3.6 fusion.11
  449.5 5.6 %collective-permute-done.31 = bf16[2,64,1024]{2,1,0:T(8,128)(2,1)} collective-permute-done((bf16[2,64,1024]{2,1,0:T(8,128)(2,1)}, bf16[2,64,1024]{2,1,0:T(8,128)(2,1)}, u32[]{:S(2)}, u32[]{:S(2)}) %collective-permute-start.31) | collective-permute-done | bytes 262176 | tf_op jit(solution)/shard_map/ppermute | solution.py:1245
  455.1 8.7 %collective-permute-done.32 = bf16[2,64,1024]{2,1,0:T(8,128)(2,1)} collective-permute-done((bf16[2,64,1024]{2,1,0:T(8,128)(2,1)}, bf16[2,64,1024]{2,1,0:T(8,128)(2,1)}, u32[]{:S(2)}, u32[]{:S(2)}) %collective-permute-start.32) | collective-permute-done | bytes 262176 | tf_op jit(solution)/shard_map/ppermute | solution.py:1245
  463.8 2.7 pad_maximum_fusion.1
  471.9 5.1 finish.3
  479.6 12.3 %small_sum.1 = f32[2,128]{1,0:T(2,128)} custom-call(f32[8,2,128]{2,1,0:T(2,128)} %add_bitcast_fusion.x_ref), custom_call_target="tpu_custom_call" | custom-call | flops 1048576 | bytes 1048576 | tf_op jit(solution)/shard_map/small_sum/pallas_call | solution.py:374
  491.9 2.3 pad_maximum_fusion.3
  499.8 6.7 %settle.1 = bf16[12,256,1024]{2,1,0:T(8,128)(2,1)} custom-call(s32[13]{0:T(128)} %pad_add_fusion.3.table_ref, bf16[1,8,64,1024]{3,2,1,0:T(8,128)(2,1)} %bitcast.185, bf16[1,8,64,1024]{3,2,1,0:T(8,128)(2,1)} %collective-permute-done.33.refs_1_, bf16[2,8,64,1024]{3,2,1,0:T(8,128)(2,1)} %collective-permute-done.36.refs_2_, bf16[1,4,64,1024]{3,2,1,0:T(8,128)(2,1)} %bitcast.189, ...), custom_call_target="tpu_custom_call" | custom-call | tf_op jit(solution)/shard_map/settle/pallas_call | solution.py:1756
  (366 shorter events, 101.5 us)
Async XLA Ops:
  7.2 47.4 %copy-start = (bf16[1024,1024]{1,0:T(8,128)(2,1)S(1)}, bf16[1024,1024]{1,0:T(8,128)(2,1)}, u32[]{:S(2)}) copy-start(bf16[1024,1024]{1,0:T(8,128)(2,1)} %param.21) | copy-start | bytes 6291460
  7.2 65.5 %all-gather.4.cloned.1.call-start = ((), (), s32[]{:S(2)}) async-start(), calls=%async_computation.2 | async-start | bytes 7864320 | tf_op jit(solution)/shard_map/all_gather | solution.py:1294
  7.9 149.0 %all-gather.6.cloned.1.call-start = ((), (), s32[]{:S(2)}) async-start(), calls=%async_computation.3 | async-start | bytes 5242880 | tf_op jit(solution)/shard_map/all_gather | solution.py:1545
  26.9 24.9 %collective-permute-start = (bf16[4,256,256]{2,1,0:T(8,128)(2,1)}, bf16[4,256,256]{2,1,0:T(8,128)(2,1)}, u32[]{:S(2)}, u32[]{:S(2)}) collective-permute-start(bf16[4,256,256]{2,1,0:T(8,128)(2,1)} %slice.252), channel_id=1, source_target_pairs={{0,4},{4,0},{8,12},{12,8},{16,20},{20,16},{24,28},{28,24},{1,5},{5... | collective-permute-start | bytes 1572872 | tf_op jit(solution)/shard_map/ppermute | solution.py:1239
  52.8 14.7 %collective-permute-start.1 = (bf16[2,256,256]{2,1,0:T(8,128)(2,1)S(1)}, bf16[2,256,256]{2,1,0:T(8,128)(2,1)S(1)}, u32[]{:S(2)}, u32[]{:S(2)}) collective-permute-start(bf16[2,256,256]{2,1,0:T(8,128)(2,1)S(1)} %pad_maximum_fusion.11), channel_id=1, source_target_pairs={{0,8},{4,12},{8,0},{12,4},{16,24},{20,28},{24,16},{28,20},{1,9},{5... | collective-permute-start | bytes 786440 | tf_op jit(solution)/shard_map/ppermute | solution.py:1245
  54.3 13.2 %collective-permute-start.2 = (bf16[4,256,256]{2,1,0:T(8,128)(2,1)S(1)}, bf16[4,256,256]{2,1,0:T(8,128)(2,1)S(1)}, u32[]{:S(2)}, u32[]{:S(2)}) collective-permute-start(bf16[4,256,256]{2,1,0:T(8,128)(2,1)S(1)} %slice.256), channel_id=1, source_target_pairs={{0,4},{4,0},{8,12},{12,8},{16,20},{20,16},{24,28},{28,24},{1,5},{5... | collective-permute-start | bytes 1572872 | tf_op jit(solution)/shard_map/ppermute | solution.py:1239
  70.8 23.0 %collective-permute-start.3 = (bf16[2,256,256]{2,1,0:T(8,128)(2,1)}, bf16[2,256,256]{2,1,0:T(8,128)(2,1)}, u32[]{:S(2)}, u32[]{:S(2)}) collective-permute-start(bf16[2,256,256]{2,1,0:T(8,128)(2,1)} %pad_maximum_fusion.12), channel_id=1, source_target_pairs={{0,16},{4,20},{8,24},{12,28},{16,0},{20,4},{24,8},{28,12},{1,17},{... | collective-permute-start | bytes 786440 | tf_op jit(solution)/shard_map/ppermute | solution.py:1245
  71.5 23.1 %collective-permute-start.4 = (bf16[2,256,256]{2,1,0:T(8,128)(2,1)}, bf16[2,256,256]{2,1,0:T(8,128)(2,1)}, u32[]{:S(2)}, u32[]{:S(2)}) collective-permute-start(bf16[2,256,256]{2,1,0:T(8,128)(2,1)} %pad_maximum_fusion.13), channel_id=1, source_target_pairs={{0,24},{4,28},{8,16},{12,20},{16,8},{20,12},{24,0},{28,4},{1,25},{... | collective-permute-start | bytes 786440 | tf_op jit(solution)/shard_map/ppermute | solution.py:1245
  98.7 103.7 %all-gather.8.cloned.1.call-start = ((), (), s32[]{:S(2)}) async-start(), calls=%async_computation.4 | async-start | bytes 5242880 | tf_op jit(solution)/shard_map/all_gather | solution.py:1559
  99.9 32.7 %collective-permute-start.5 = (bf16[2,256,256]{2,1,0:T(8,128)(2,1)}, bf16[2,256,256]{2,1,0:T(8,128)(2,1)S(1)}, u32[]{:S(2)}, u32[]{:S(2)}) collective-permute-start(bf16[2,256,256]{2,1,0:T(8,128)(2,1)} %pad_maximum_fusion.14), channel_id=1, source_target_pairs={{0,8},{4,12},{8,0},{12,4},{16,24},{20,28},{24,16},{28,20},{1,9},{5... | collective-permute-start | bytes 786440 | tf_op jit(solution)/shard_map/ppermute | solution.py:1245
  102.2 30.4 %collective-permute-start.6 = (bf16[2,256,256]{2,1,0:T(8,128)(2,1)}, bf16[2,256,256]{2,1,0:T(8,128)(2,1)}, u32[]{:S(2)}, u32[]{:S(2)}) collective-permute-start(bf16[2,256,256]{2,1,0:T(8,128)(2,1)} %pad_maximum_fusion.15), channel_id=1, source_target_pairs={{0,16},{4,20},{8,24},{12,28},{16,0},{20,4},{24,8},{28,12},{1,17},{... | collective-permute-start | bytes 786440 | tf_op jit(solution)/shard_map/ppermute | solution.py:1245
  103.8 28.8 %collective-permute-start.7 = (bf16[2,256,256]{2,1,0:T(8,128)(2,1)}, bf16[2,256,256]{2,1,0:T(8,128)(2,1)}, u32[]{:S(2)}, u32[]{:S(2)}) collective-permute-start(bf16[2,256,256]{2,1,0:T(8,128)(2,1)} %pad_maximum_fusion.16), channel_id=1, source_target_pairs={{0,24},{4,28},{8,16},{12,20},{16,8},{20,12},{24,0},{28,4},{1,25},{... | collective-permute-start | bytes 786440 | tf_op jit(solution)/shard_map/ppermute | solution.py:1245
  132.6 34.1 %copy-start.5 = (bf16[48,64,256]{2,1,0:T(8,128)(2,1)}, bf16[48,64,256]{2,1,0:T(8,128)(2,1)S(1)}, u32[]{:S(2)}) copy-start(bf16[48,64,256]{2,1,0:T(8,128)(2,1)S(1)} %gather_fusion.5) | copy-start | bytes 4718596
  138.1 233.4 %reduce-scatter.3.cloned.1.call-start = ((), (), s32[]{:S(2)}) async-start(), calls=%async_computation.5 | async-start | bytes 7864320 | tf_op jit(solution)/shard_map/reduce_scatter | solution.py:1571
  138.3 18.7 %collective-permute-start.8 = (bf16[4,6,64,256]{3,2,1,0:T(8,128)(2,1)S(1)}, bf16[4,6,64,256]{3,2,1,0:T(8,128)(2,1)S(1)}, u32[]{:S(2)}, u32[]{:S(2)}) collective-permute-start(bf16[4,6,64,256]{3,2,1,0:T(8,128)(2,1)S(1)} %slice.268), channel_id=1, source_target_pairs={{0,4},{4,0},{8,12},{12,8},{16,20},{20,16},{24,28},{28,24},{1,5},{5... | collective-permute-start | bytes 2359304 | tf_op jit(solution)/shard_map/ppermute | solution.py:1239
  158.4 287.4 %reduce-scatter.5.cloned.1.call-start = ((), (), s32[]{:S(2)}) async-start(), calls=%async_computation.6 | async-start | bytes 7864320 | tf_op jit(solution)/shard_map/reduce_scatter | solution.py:1661
  164.0 62.3 %collective-permute-start.12 = (bf16[4,144,2048]{2,1,0:T(8,128)(2,1)}, bf16[4,144,2048]{2,1,0:T(8,128)(2,1)}, u32[]{:S(2)}, u32[]{:S(2)}) collective-permute-start(bf16[4,144,2048]{2,1,0:T(8,128)(2,1)} %pad_maximum_fusion), channel_id=1, source_target_pairs={{0,4},{4,0},{8,12},{12,8},{16,20},{20,16},{24,28},{28,24},{1,5},{5... | collective-permute-start | bytes 7077896 | tf_op jit(solution)/shard_map/ppermute | solution.py:432
  166.9 35.5 %collective-permute-start.9 = (bf16[2,6,64,256]{3,2,1,0:T(8,128)(2,1)S(1)}, bf16[2,6,64,256]{3,2,1,0:T(8,128)(2,1)S(1)}, u32[]{:S(2)}, u32[]{:S(2)}) collective-permute-start(bf16[2,6,64,256]{3,2,1,0:T(8,128)(2,1)S(1)} %pad_maximum_fusion.5), channel_id=1, source_target_pairs={{0,8},{4,12},{8,0},{12,4},{16,24},{20,28},{24,16},{28,20},{1,9},{5... | collective-permute-start | bytes 1179656 | tf_op jit(solution)/shard_map/ppermute | solution.py:1245
  168.7 33.7 %collective-permute-start.10 = (bf16[2,6,64,256]{3,2,1,0:T(8,128)(2,1)S(1)}, bf16[2,6,64,256]{3,2,1,0:T(8,128)(2,1)S(1)}, u32[]{:S(2)}, u32[]{:S(2)}) collective-permute-start(bf16[2,6,64,256]{3,2,1,0:T(8,128)(2,1)S(1)} %pad_maximum_fusion.6), channel_id=1, source_target_pairs={{0,16},{4,20},{8,24},{12,28},{16,0},{20,4},{24,8},{28,12},{1,17},{... | collective-permute-start | bytes 1179656 | tf_op jit(solution)/shard_map/ppermute | solution.py:1245
  169.1 33.3 %collective-permute-start.11 = (bf16[2,6,64,256]{3,2,1,0:T(8,128)(2,1)S(1)}, bf16[2,6,64,256]{3,2,1,0:T(8,128)(2,1)S(1)}, u32[]{:S(2)}, u32[]{:S(2)}) collective-permute-start(bf16[2,6,64,256]{3,2,1,0:T(8,128)(2,1)S(1)} %pad_maximum_fusion.7), channel_id=1, source_target_pairs={{0,24},{4,28},{8,16},{12,20},{16,8},{20,12},{24,0},{28,4},{1,25},{... | collective-permute-start | bytes 1179656 | tf_op jit(solution)/shard_map/ppermute | solution.py:1245
  180.9 21.4 %copy-start.44 = (bf16[128]{0:T(256)(128)(2,1)S(1)}, bf16[128]{0:T(256)(128)(2,1)}, u32[]{:S(2)}) copy-start(bf16[128]{0:T(256)(128)(2,1)} %get-tuple-element.447) | copy-start | bytes 772
  180.9 21.4 %copy-start.46 = (bf16[128]{0:T(256)(128)(2,1)S(1)}, bf16[128]{0:T(256)(128)(2,1)}, u32[]{:S(2)}) copy-start(bf16[128]{0:T(256)(128)(2,1)} %get-tuple-element.455) | copy-start | bytes 772
  228.2 31.5 %collective-permute-start.14 = (bf16[2,144,2048]{2,1,0:T(8,128)(2,1)S(1)}, bf16[2,144,2048]{2,1,0:T(8,128)(2,1)S(1)}, u32[]{:S(2)}, u32[]{:S(2)}) collective-permute-start(bf16[2,144,2048]{2,1,0:T(8,128)(2,1)S(1)} %pad_maximum_fusion.2), channel_id=1, source_target_pairs={{0,8},{4,12},{8,0},{12,4},{16,24},{20,28},{24,16},{28,20},{1,9},{5... | collective-permute-start | bytes 3538952 | tf_op jit(solution)/shard_map/ppermute | solution.py:432
  231.5 28.2 %collective-permute-start.13 = (bf16[4,6,64,256]{3,2,1,0:T(8,128)(2,1)S(1)}, bf16[4,6,64,256]{3,2,1,0:T(8,128)(2,1)S(1)}, u32[]{:S(2)}, u32[]{:S(2)}) collective-permute-start(bf16[4,6,64,256]{3,2,1,0:T(8,128)(2,1)S(1)} %slice.281), channel_id=1, source_target_pairs={{0,4},{4,0},{8,12},{12,8},{16,20},{20,16},{24,28},{28,24},{1,5},{5... | collective-permute-start | bytes 2359304 | tf_op jit(solution)/shard_map/ppermute | solution.py:1239
  259.7 54.8 %copy-start.22 = (bf16[2,144,2048]{2,1,0:T(8,128)(2,1)}, bf16[2,144,2048]{2,1,0:T(8,128)(2,1)S(1)}, u32[]{:S(2)}) copy-start(bf16[2,144,2048]{2,1,0:T(8,128)(2,1)S(1)} %collective-permute-done.14) | copy-start | bytes 3538948
  259.9 40.5 %collective-permute-start.15 = (bf16[2,6,64,256]{3,2,1,0:T(8,128)(2,1)S(1)}, bf16[2,6,64,256]{3,2,1,0:T(8,128)(2,1)}, u32[]{:S(2)}, u32[]{:S(2)}) collective-permute-start(bf16[2,6,64,256]{3,2,1,0:T(8,128)(2,1)S(1)} %pad_maximum_fusion.8), channel_id=1, source_target_pairs={{0,8},{4,12},{8,0},{12,4},{16,24},{20,28},{24,16},{28,20},{1,9},{5... | collective-permute-start | bytes 1179656 | tf_op jit(solution)/shard_map/ppermute | solution.py:1245
  261.8 38.6 %collective-permute-start.16 = (bf16[2,6,64,256]{3,2,1,0:T(8,128)(2,1)S(1)}, bf16[2,6,64,256]{3,2,1,0:T(8,128)(2,1)}, u32[]{:S(2)}, u32[]{:S(2)}) collective-permute-start(bf16[2,6,64,256]{3,2,1,0:T(8,128)(2,1)S(1)} %pad_maximum_fusion.9), channel_id=1, source_target_pairs={{0,16},{4,20},{8,24},{12,28},{16,0},{20,4},{24,8},{28,12},{1,17},{... | collective-permute-start | bytes 1179656 | tf_op jit(solution)/shard_map/ppermute | solution.py:1245
  267.3 33.2 %collective-permute-start.17 = (bf16[2,6,64,256]{3,2,1,0:T(8,128)(2,1)S(1)}, bf16[2,6,64,256]{3,2,1,0:T(8,128)(2,1)S(1)}, u32[]{:S(2)}, u32[]{:S(2)}) collective-permute-start(bf16[2,6,64,256]{3,2,1,0:T(8,128)(2,1)S(1)} %pad_maximum_fusion.10), channel_id=1, source_target_pairs={{0,24},{4,28},{8,16},{12,20},{16,8},{20,12},{24,0},{28,4},{1,25},{... | collective-permute-start | bytes 1179656 | tf_op jit(solution)/shard_map/ppermute | solution.py:1245
  300.4 9.2 %collective-permute-start.18 = (bf16[2,8,64,1024]{3,2,1,0:T(8,128)(2,1)}, bf16[2,8,64,1024]{3,2,1,0:T(8,128)(2,1)}, u32[]{:S(2)}, u32[]{:S(2)}) collective-permute-start(bf16[2,8,64,1024]{3,2,1,0:T(8,128)(2,1)} %get-tuple-element.215), channel_id=1, source_target_pairs={{0,1},{1,0},{2,3},{3,2},{4,5},{5,4},{6,7},{7,6},{8,9},{9,8},{10,11... | collective-permute-start | bytes 6291464 | tf_op jit(solution)/shard_map/ppermute | solution.py:1618
  312.6 40.6 %collective-permute-start.19 = (bf16[1,8,64,1024]{3,2,1,0:T(8,128)(2,1)}, bf16[1,8,64,1024]{3,2,1,0:T(8,128)(2,1)}, u32[]{:S(2)}, u32[]{:S(2)}) collective-permute-start(bf16[1,8,64,1024]{3,2,1,0:T(8,128)(2,1)} %add_convert_fusion.4), channel_id=1, source_target_pairs={{0,2},{1,3},{2,0},{3,1},{4,6},{5,7},{6,4},{7,5},{8,10},{9,11},{10,... | collective-permute-start | bytes 3145736 | tf_op jit(solution)/shard_map/ppermute | solution.py:432
  316.7 38.8 %collective-permute-start.20 = (bf16[1,144,2048]{2,1,0:T(8,128)(2,1)}, bf16[1,144,2048]{2,1,0:T(8,128)(2,1)}, u32[]{:S(2)}, u32[]{:S(2)}) collective-permute-start(bf16[1,144,2048]{2,1,0:T(8,128)(2,1)} %add_convert_fusion.6), channel_id=1, source_target_pairs={{0,16},{4,20},{8,24},{12,28},{16,0},{20,4},{24,8},{28,12},{1,17},{... | collective-permute-start | bytes 1769480 | tf_op jit(solution)/shard_map/ppermute | solution.py:432
  355.5 15.9 %collective-permute-start.21 = (bf16[2,8,64,1024]{3,2,1,0:T(8,128)(2,1)S(1)}, bf16[2,8,64,1024]{3,2,1,0:T(8,128)(2,1)S(1)}, u32[]{:S(2)}, u32[]{:S(2)}) collective-permute-start(bf16[2,8,64,1024]{3,2,1,0:T(8,128)(2,1)S(1)} %copy-done.53), channel_id=1, source_target_pairs={{0,1},{1,0},{2,3},{3,2},{4,5},{5,4},{6,7},{7,6},{8,9},{9,8},{10,11... | collective-permute-start | bytes 6291464 | tf_op jit(solution)/shard_map/ppermute | solution.py:1636
  356.6 14.9 %collective-permute-start.22 = (bf16[4,64,1024]{2,1,0:T(8,128)(2,1)S(1)}, bf16[4,64,1024]{2,1,0:T(8,128)(2,1)}, u32[]{:S(2)}, u32[]{:S(2)}) collective-permute-start(bf16[4,64,1024]{2,1,0:T(8,128)(2,1)S(1)} %slice.298), channel_id=1, source_target_pairs={{0,4},{4,0},{8,12},{12,8},{16,20},{20,16},{24,28},{28,24},{1,5},{5... | collective-permute-start | bytes 1572872 | tf_op jit(solution)/shard_map/ppermute | solution.py:1239
  379.3 35.4 %collective-permute-start.26 = (bf16[1,8,64,1024]{3,2,1,0:T(8,128)(2,1)S(1)}, bf16[1,8,64,1024]{3,2,1,0:T(8,128)(2,1)S(1)}, u32[]{:S(2)}, u32[]{:S(2)}) collective-permute-start(bf16[1,8,64,1024]{3,2,1,0:T(8,128)(2,1)S(1)} %add_convert_fusion.2), channel_id=1, source_target_pairs={{0,2},{1,3},{2,0},{3,1},{4,6},{5,7},{6,4},{7,5},{8,10},{9,11},{10,... | collective-permute-start | bytes 3145736 | tf_op jit(solution)/shard_map/ppermute | solution.py:432
  382.1 33.3 %collective-permute-start.27 = (bf16[4,1024,128]{2,1,0:T(8,128)(2,1)S(1)}, bf16[4,1024,128]{2,1,0:T(8,128)(2,1)S(1)}, u32[]{:S(2)}, u32[]{:S(2)}) collective-permute-start(bf16[4,1024,128]{2,1,0:T(8,128)(2,1)S(1)} %maximum_maximum_fusion), channel_id=1, source_target_pairs={{0,4},{4,0},{8,12},{12,8},{16,20},{20,16},{24,28},{28,24},{1,5},{5... | collective-permute-start | bytes 3145736 | tf_op jit(solution)/shard_map/ppermute | solution.py:432
  383.7 31.7 %collective-permute-start.23 = (bf16[2,64,1024]{2,1,0:T(8,128)(2,1)S(1)}, bf16[2,64,1024]{2,1,0:T(8,128)(2,1)S(1)}, u32[]{:S(2)}, u32[]{:S(2)}) collective-permute-start(bf16[2,64,1024]{2,1,0:T(8,128)(2,1)S(1)} %pad_maximum_fusion.17), channel_id=1, source_target_pairs={{0,8},{4,12},{8,0},{12,4},{16,24},{20,28},{24,16},{28,20},{1,9},{5... | collective-permute-start | bytes 786440 | tf_op jit(solution)/shard_map/ppermute | solution.py:1245
  383.8 31.6 %collective-permute-start.24 = (bf16[2,64,1024]{2,1,0:T(8,128)(2,1)S(1)}, bf16[2,64,1024]{2,1,0:T(8,128)(2,1)S(1)}, u32[]{:S(2)}, u32[]{:S(2)}) collective-permute-start(bf16[2,64,1024]{2,1,0:T(8,128)(2,1)S(1)} %pad_maximum_fusion.18), channel_id=1, source_target_pairs={{0,16},{4,20},{8,24},{12,28},{16,0},{20,4},{24,8},{28,12},{1,17},{... | collective-permute-start | bytes 786440 | tf_op jit(solution)/shard_map/ppermute | solution.py:1245
  383.9 31.5 %collective-permute-start.25 = (bf16[2,64,1024]{2,1,0:T(8,128)(2,1)S(1)}, bf16[2,64,1024]{2,1,0:T(8,128)(2,1)S(1)}, u32[]{:S(2)}, u32[]{:S(2)}) collective-permute-start(bf16[2,64,1024]{2,1,0:T(8,128)(2,1)S(1)} %pad_maximum_fusion.19), channel_id=1, source_target_pairs={{0,24},{4,28},{8,16},{12,20},{16,8},{20,12},{24,0},{28,4},{1,25},{... | collective-permute-start | bytes 786440 | tf_op jit(solution)/shard_map/ppermute | solution.py:1245
  416.6 11.1 %collective-permute-start.29 = (bf16[2,1024,128]{2,1,0:T(8,128)(2,1)}, bf16[2,1024,128]{2,1,0:T(8,128)(2,1)S(1)}, u32[]{:S(2)}, u32[]{:S(2)}) collective-permute-start(bf16[2,1024,128]{2,1,0:T(8,128)(2,1)} %pad_maximum_fusion.4), channel_id=1, source_target_pairs={{0,8},{4,12},{8,0},{12,4},{16,24},{20,28},{24,16},{28,20},{1,9},{5... | collective-permute-start | bytes 1572872 | tf_op jit(solution)/shard_map/ppermute | solution.py:432
  416.6 11.1 %collective-permute-start.28 = (bf16[4,64,1024]{2,1,0:T(8,128)(2,1)S(1)}, bf16[4,64,1024]{2,1,0:T(8,128)(2,1)S(1)}, u32[]{:S(2)}, u32[]{:S(2)}) collective-permute-start(bf16[4,64,1024]{2,1,0:T(8,128)(2,1)S(1)} %slice.311), channel_id=1, source_target_pairs={{0,4},{4,0},{8,12},{12,8},{16,20},{20,16},{24,28},{28,24},{1,5},{5... | collective-permute-start | bytes 1572872 | tf_op jit(solution)/shard_map/ppermute | solution.py:1239
  427.8 9.3 %collective-permute-start.34 = (bf16[1,1024,128]{2,1,0:T(8,128)(2,1)S(1)}, bf16[1,1024,128]{2,1,0:T(8,128)(2,1)S(1)}, u32[]{:S(2)}, u32[]{:S(2)}) collective-permute-start(bf16[1,1024,128]{2,1,0:T(8,128)(2,1)S(1)} %fusion.31), channel_id=1, source_target_pairs={{0,16},{4,20},{8,24},{12,28},{16,0},{20,4},{24,8},{28,12},{1,17},{... | collective-permute-start | bytes 786440 | tf_op jit(solution)/shard_map/ppermute | solution.py:432
  427.9 35.9 %collective-permute-start.33 = (bf16[1,8,64,1024]{3,2,1,0:T(8,128)(2,1)}, bf16[1,8,64,1024]{3,2,1,0:T(8,128)(2,1)}, u32[]{:S(2)}, u32[]{:S(2)}) collective-permute-start(bf16[1,8,64,1024]{3,2,1,0:T(8,128)(2,1)} %bitcast.184), channel_id=1, source_target_pairs={{0,2},{1,3},{2,0},{3,1},{4,6},{5,7},{6,4},{7,5},{8,10},{9,11},{10,... | collective-permute-start | bytes 3145736 | tf_op jit(solution)/shard_map/ppermute | solution.py:453
  430.1 19.4 %collective-permute-start.30 = (bf16[2,64,1024]{2,1,0:T(8,128)(2,1)}, bf16[2,64,1024]{2,1,0:T(8,128)(2,1)S(1)}, u32[]{:S(2)}, u32[]{:S(2)}) collective-permute-start(bf16[2,64,1024]{2,1,0:T(8,128)(2,1)} %pad_maximum_fusion.24), channel_id=1, source_target_pairs={{0,8},{4,12},{8,0},{12,4},{16,24},{20,28},{24,16},{28,20},{1,9},{5... | collective-permute-start | bytes 786440 | tf_op jit(solution)/shard_map/ppermute | solution.py:1245
  431.8 23.3 %collective-permute-start.31 = (bf16[2,64,1024]{2,1,0:T(8,128)(2,1)}, bf16[2,64,1024]{2,1,0:T(8,128)(2,1)}, u32[]{:S(2)}, u32[]{:S(2)}) collective-permute-start(bf16[2,64,1024]{2,1,0:T(8,128)(2,1)} %pad_maximum_fusion.25), channel_id=1, source_target_pairs={{0,16},{4,20},{8,24},{12,28},{16,0},{20,4},{24,8},{28,12},{1,17},{... | collective-permute-start | bytes 786440 | tf_op jit(solution)/shard_map/ppermute | solution.py:1245
  434.8 28.9 %collective-permute-start.32 = (bf16[2,64,1024]{2,1,0:T(8,128)(2,1)}, bf16[2,64,1024]{2,1,0:T(8,128)(2,1)}, u32[]{:S(2)}, u32[]{:S(2)}) collective-permute-start(bf16[2,64,1024]{2,1,0:T(8,128)(2,1)} %pad_maximum_fusion.26), channel_id=1, source_target_pairs={{0,24},{4,28},{8,16},{12,20},{16,8},{20,12},{24,0},{28,4},{1,25},{... | collective-permute-start | bytes 786440 | tf_op jit(solution)/shard_map/ppermute | solution.py:1245
  466.5 25.4 %collective-permute-start.36 = (bf16[2,8,64,1024]{3,2,1,0:T(8,128)(2,1)}, bf16[2,8,64,1024]{3,2,1,0:T(8,128)(2,1)}, u32[]{:S(2)}, u32[]{:S(2)}) collective-permute-start(bf16[2,8,64,1024]{3,2,1,0:T(8,128)(2,1)} %pad_maximum_fusion.1), channel_id=1, source_target_pairs={{0,1},{1,0},{2,3},{3,2},{4,5},{5,4},{6,7},{7,6},{8,9},{9,8},{10,11... | collective-permute-start | bytes 6291464 | tf_op jit(solution)/shard_map/ppermute | solution.py:453
  477.0 14.9 %collective-permute-start.35 = (bf16[1,4,64,1024]{3,2,1,0:T(8,128)(2,1)}, bf16[1,4,64,1024]{3,2,1,0:T(8,128)(2,1)S(1)}, u32[]{:S(2)}, u32[]{:S(2)}) collective-permute-start(bf16[1,4,64,1024]{3,2,1,0:T(8,128)(2,1)} %bitcast.187), channel_id=1, source_target_pairs={{0,2},{1,3},{2,0},{3,1},{4,6},{5,7},{6,4},{7,5},{8,10},{9,11},{10,... | collective-permute-start | bytes 1572872 | tf_op jit(solution)/shard_map/ppermute | solution.py:453
  494.2 5.5 %collective-permute-start.37 = (bf16[2,4,64,1024]{3,2,1,0:T(8,128)(2,1)}, bf16[2,4,64,1024]{3,2,1,0:T(8,128)(2,1)}, u32[]{:S(2)}, u32[]{:S(2)}) collective-permute-start(bf16[2,4,64,1024]{3,2,1,0:T(8,128)(2,1)} %pad_maximum_fusion.3), channel_id=1, source_target_pairs={{0,1},{1,0},{2,3},{3,2},{4,5},{5,4},{6,7},{7,6},{8,9},{9,8},{10,11... | collective-permute-start | bytes 3145736 | tf_op jit(solution)/shard_map/ppermute | solution.py:453
  (55 other events, 440.4 us)
Sparse Core Ops, SparseCore 0:
  9.6 48.6 all-gather.3
  98.8 38.1 all-gather.5
  139.1 39.2 all-gather.7
  180.7 57.9 reduce-scatter.2
  371.7 74.1 reduce-scatter.4
